TPU v7x, 256 devices: a whole 4x4x8 slice. The times are simulated.
256 devices in a mesh: dp: 16 (over x_lo, y, core), tensor: 16 (over x_hi, z).
Axes of the slice: x: 4 (x_hi: 2, x_lo: 2; x = x_hi * 2 + x_lo), y: 4, z: 8, core: 2. Of those that a mesh axis runs over, the one named last changes fastest.
Arguments:
- tokens: bfloat16 [8192, 2048], P('dp', 'tensor'), may hold values from -6 to 6
- series_ids: int32 [8192], replicated, may hold values from 0 to 7, never falling along the last dimension, each value on 1 to 5120 neighbouring positions
- offsets: int32 [8192], P('dp'), may hold values from 0 to 65535
- norm_gain: float32 [2048], replicated, may hold values from 0.5 to 1.5
- mlp_gain: float32 [2048], replicated, may hold values from 0.5 to 1.5
- w_query: bfloat16 [2048, 2048], P(None, 'tensor')
- w_key: bfloat16 [2048, 2048], P(None, 'tensor')
- w_value: bfloat16 [2048, 2048], P(None, 'tensor'), may hold values from -0.125 to 0.125
- w_out: bfloat16 [2048, 2048], P('tensor'), may hold values from -0.125 to 0.125
- w_gate: bfloat16 [2048, 8192], P(None, 'tensor'), may hold values from -0.125 to 0.125
- w_up: bfloat16 [2048, 8192], P(None, 'tensor'), may hold values from -0.125 to 0.125
- w_down: bfloat16 [8192, 2048], P('tensor'), may hold values from -0.0625 to 0.0625
- projector: bfloat16 [2048, 512], replicated, may hold values from -0.125 to 0.125
- student_in: bfloat16 [8192, 512], P('dp'), may hold values from -6 to 6
- s_gate: bfloat16 [512, 2048], P(None, 'tensor'), may hold values from -0.25 to 0.25
- s_up: bfloat16 [512, 2048], P(None, 'tensor'), may hold values from -0.25 to 0.25
- s_down: bfloat16 [2048, 512], P('tensor'), may hold values from -0.125 to 0.125
Outputs:
- teacher_out: bfloat16 [8192, 2048], P('dp', 'tensor')
- grad_gate: float32 [512, 2048], P(None, 'tensor')
- grad_up: float32 [512, 2048], P(None, 'tensor')
- grad_down: float32 [2048, 512], P('tensor')
- error: float32 [], replicated
Inputs may be any that keep to these rules, and one draw needn't show every extreme that they name: `series_ids`: ids never fall along the window; each series covers 1 to 5120 consecutive rows, one series exactly that many.
All inputs are finite; a program needn't handle non-finite values.
Results may differ from a plain program's by a relative error of at most 0.025.
Values may be sent and summed in bfloat16 or wider, within the bound.
A program may use at most 128 MiB of HBM per device.

v0:
```python
import jax
import jax.numpy as jnp
from jax import lax
from jax.sharding import PartitionSpec as P

HD = 128


def rms_scale(values):
    return values * lax.rsqrt(jnp.mean(values * values, axis=-1, keepdims=True) + 1e-05)


def frequencies(head_dim):
    indices = jnp.arange(head_dim // 2).astype(jnp.float32)
    return jnp.exp(-jnp.log(500000.0) * 2.0 * indices / head_dim)


def rotary(inputs, angles):
    half_dim = inputs.shape[-1] // 2
    cosine = jnp.cos(angles)
    sine = jnp.sin(angles)
    first_half = inputs[..., :half_dim]
    second_half = inputs[..., half_dim:]
    return jnp.concatenate(
        [first_half * cosine - second_half * sine, first_half * sine + second_half * cosine],
        axis=-1,
    )


def local(
    tokens,
    series_ids,
    offsets,
    norm_gain,
    mlp_gain,
    w_query,
    w_key,
    w_value,
    w_out,
    w_gate,
    w_up,
    w_down,
    projector,
    student_in,
    s_gate,
    s_up,
    s_down,
):
    row_count = tokens.shape[0]
    heads_dev = w_query.shape[1] // HD
    first_row = lax.axis_index("dp") * row_count
    tokens_full = lax.all_gather(tokens, "tensor", axis=1, tiled=True).astype(jnp.float32)
    normed = (rms_scale(tokens_full) * norm_gain).astype(jnp.bfloat16)
    angles = offsets.astype(jnp.float32)[:, None, None] * frequencies(HD)[None, None, :]
    queries = rotary(
        jnp.dot(normed, w_query, preferred_element_type=jnp.float32).reshape(
            row_count, heads_dev, HD
        ),
        angles,
    ).astype(jnp.bfloat16)
    keys_rot = rotary(
        jnp.dot(normed, w_key, preferred_element_type=jnp.float32).reshape(
            row_count, heads_dev, HD
        ),
        angles,
    ).astype(jnp.bfloat16)
    values_mine = jnp.dot(normed, w_value, preferred_element_type=jnp.float32).astype(jnp.bfloat16)
    keys_flat = keys_rot.reshape(row_count, heads_dev * HD)
    query_pos = first_row + jnp.arange(row_count, dtype=jnp.int32)
    query_series = lax.dynamic_slice_in_dim(series_ids, first_row, row_count, 0)
    factor = HD ** (-0.5)
    peak = jnp.full((row_count, heads_dev), -1e30, jnp.float32)
    key_block = lax.all_gather(keys_flat, "dp", axis=0, tiled=True)
    value_block = lax.all_gather(values_mine, "dp", axis=0, tiled=True)
    count = key_block.shape[0]
    key_pos = jnp.arange(count, dtype=jnp.int32)
    allowed = (
        (key_pos[None, :] >= 0)
        & (key_pos[None, :] <= query_pos[:, None])
        & (series_ids[None, :] == query_series[:, None])
    )
    scores = (
        jnp.einsum(
            "qhd,khd->qhk",
            queries,
            key_block.reshape(count, heads_dev, HD),
            preferred_element_type=jnp.float32,
        )
        * factor
    )
    scores = jnp.where(allowed[:, None, :], scores, -1e30)
    new_peak = jnp.maximum(peak, jnp.max(scores, axis=2))
    weights = jnp.where(allowed[:, None, :], jnp.exp(scores - new_peak[:, :, None]), 0.0)
    denom = jnp.sum(weights, axis=2)
    accum = jnp.einsum(
        "qhk,khd->qhd",
        weights.astype(jnp.bfloat16),
        value_block.reshape(count, heads_dev, HD),
        preferred_element_type=jnp.float32,
    )
    peak, denom, accum = (new_peak, denom, accum)
    attended = (accum / denom[:, :, None]).astype(jnp.bfloat16).reshape(row_count, heads_dev * HD)
    partial_out = jnp.dot(attended, w_out, preferred_element_type=jnp.float32)
    own_sum = lax.psum_scatter(
        partial_out.astype(jnp.bfloat16), "tensor", scatter_dimension=1, tiled=True
    ).astype(jnp.float32)
    mixed_own = (tokens.astype(jnp.float32) + own_sum).astype(jnp.bfloat16)
    mixed = lax.all_gather(mixed_own, "tensor", axis=1, tiled=True)
    normed_two = (rms_scale(mixed.astype(jnp.float32)) * mlp_gain).astype(jnp.bfloat16)
    gate_out = jnp.dot(normed_two, w_gate, preferred_element_type=jnp.float32)
    up_out = jnp.dot(normed_two, w_up, preferred_element_type=jnp.float32)
    hidden = (jax.nn.silu(gate_out) * up_out).astype(jnp.bfloat16)
    mlp_part = jnp.dot(hidden, w_down, preferred_element_type=jnp.float32)
    mlp_own = lax.psum_scatter(
        mlp_part.astype(jnp.bfloat16), "tensor", scatter_dimension=1, tiled=True
    ).astype(jnp.float32)
    teacher_out = (mixed_own.astype(jnp.float32) + mlp_own).astype(jnp.bfloat16)
    student_full = student_in.astype(jnp.float32)
    student_normed = rms_scale(student_full).astype(jnp.bfloat16)
    s_gate_out = jnp.dot(student_normed, s_gate, preferred_element_type=jnp.float32)
    s_up_out = jnp.dot(student_normed, s_up, preferred_element_type=jnp.float32)
    sigmoid_gate = jax.nn.sigmoid(s_gate_out)
    s_hidden = (s_gate_out * sigmoid_gate * s_up_out).astype(jnp.bfloat16)
    student_part = jnp.dot(s_hidden, s_down, preferred_element_type=jnp.float32)
    teacher_full = lax.all_gather(teacher_out, "tensor", axis=1, tiled=True)
    target = jnp.dot(teacher_full, projector, preferred_element_type=jnp.float32)
    student_summed = lax.psum(student_part.astype(jnp.bfloat16), "tensor").astype(jnp.float32)
    difference = student_full + student_summed - target
    total_rows = row_count * lax.axis_size("dp")
    scaled = (difference * total_rows ** (-0.5)).astype(jnp.bfloat16)
    grad_down_part = jnp.einsum("rk,rc->kc", s_hidden, scaled, preferred_element_type=jnp.float32)
    grad_hidden = jnp.einsum("rc,kc->rk", scaled, s_down, preferred_element_type=jnp.float32)
    grad_up_in = (grad_hidden * s_gate_out * sigmoid_gate).astype(jnp.bfloat16)
    grad_gate_in = (
        grad_hidden * s_up_out * sigmoid_gate * (1.0 + s_gate_out * (1.0 - sigmoid_gate))
    ).astype(jnp.bfloat16)
    grad_gate_part = jnp.einsum(
        "rc,rk->ck", student_normed, grad_gate_in, preferred_element_type=jnp.float32
    )
    grad_up_part = jnp.einsum(
        "rc,rk->ck", student_normed, grad_up_in, preferred_element_type=jnp.float32
    )
    square_sum = jnp.sum(difference * difference)
    grad_gate, grad_up, grad_down, square_total = (
        lax.psum(grad_gate_part.astype(jnp.bfloat16), "dp").astype(jnp.float32),
        lax.psum(grad_up_part.astype(jnp.bfloat16), "dp").astype(jnp.float32),
        lax.psum(grad_down_part.astype(jnp.bfloat16), "dp").astype(jnp.float32),
        lax.psum(square_sum.astype(jnp.bfloat16), "dp").astype(jnp.float32),
    )
    error = square_total / (total_rows * difference.shape[1])
    return (teacher_out, grad_gate, grad_up, grad_down, error)


def solution(mesh):
    in_specs = (
        P("dp", "tensor"),
        P(),
        P("dp"),
        P(),
        P(),
        P(None, "tensor"),
        P(None, "tensor"),
        P(None, "tensor"),
        P("tensor", None),
        P(None, "tensor"),
        P(None, "tensor"),
        P("tensor", None),
        P(),
        P("dp", None),
        P(None, "tensor"),
        P(None, "tensor"),
        P("tensor", None),
    )
    out_specs = (P("dp", "tensor"), P(None, "tensor"), P(None, "tensor"), P("tensor", None), P())
    return jax.shard_map(local, mesh=mesh, in_specs=in_specs, out_specs=out_specs, check_vma=False)
```

profile of v0, /device:TPU:1, one launch (start us, length us, event | category | flops | bytes accessed | tf_op | source)
XLA Modules:
  0.0 1086.4 jit_solution(6128594377128564638)
XLA Ops:
  8.7 87.6 %all-gather.6.cloned.1.call-done = bf16[512,2048]{1,0:T(8,128)(2,1)} async-done(((bf16[512,128]{1,0:T(8,128)(2,1)}), bf16[512,2048]{1,0:T(8,128)(2,1)}) %all-gather.6.cloned.1.call-update) | async-done | bytes 2097168 | tf_op jit(solution)/shard_map/all_gather | solution.py:52
  96.2 2.1 fusion.7
  98.3 2.1 fusion.9
  104.0 3.0 convolution_convert_fusion.6
  107.2 33.4 %all-gather.10.cloned.1.call-done = bf16[8192,128]{0,1:T(8,128)(2,1)} async-done(((bf16[512,128]{0,1:T(8,128)(2,1)}), bf16[8192,128]{0,1:T(8,128)(2,1)}) %all-gather.10.cloned.1.call-update) | async-done | bytes 2097168 | tf_op jit(solution)/shard_map/all_gather | solution.py:73
  140.6 5.7 fusion.1
  146.3 5.7 copy-done.2
  152.0 5.8 fusion.2
  157.8 21.8 %all-gather.8.cloned.1.call-done = bf16[8192,128]{1,0:T(8,128)(2,1)} async-done(((bf16[512,128]{1,0:T(8,128)(2,1)}), bf16[8192,128]{1,0:T(8,128)(2,1)}) %all-gather.8.cloned.1.call-update) | async-done | bytes 2097168 | tf_op jit(solution)/shard_map/all_gather | solution.py:74
  179.6 14.0 %convolution_convert_fusion = bf16[512,2048]{1,0:T(8,128)(2,1)} fusion(bf16[128,2048]{1,0:T(8,128)(2,1)S(1)} %copy-done.11, bf16[8192,128]{1,0:T(8,128)(2,1)} %all-gather.8.cloned.1.call-done, f32[8192,512]{1,0:T(8,128)} %copy-done.2, f32[512]{0:T(512)S(1)} %broadcast_maximum_fusion, s32[512]{0:T(512)S(1)} %dynamic_slice.3, s32[512]{0:T(512)S(1)} %iota_add_fusion, ...), kind=kOutput, calls=%fused_computation.19 | convolution fusion | flops 1376911360 | bytes 21536768 | tf_op jit(solution)/shard_map/dot_general | solution.py:103
  193.6 4.0 copy.22
  197.7 198.6 %reduce-scatter.7.cloned.1.call-done = bf16[128,512]{1,0:T(8,128)(2,1)} async-done(((bf16[2048,512]{1,0:T(8,128)(2,1)}), bf16[128,512]{1,0:T(8,128)(2,1)}) %reduce-scatter.7.cloned.1.call-update) | async-done | bytes 131088
  398.3 85.9 %all-gather.12.cloned.1.call-done = bf16[512,2048]{1,0:T(8,128)(2,1)} async-done(((bf16[512,128]{1,0:T(8,128)(2,1)}), bf16[512,2048]{1,0:T(8,128)(2,1)}) %all-gather.12.cloned.1.call-update) | async-done | bytes 2097168 | tf_op jit(solution)/shard_map/all_gather | solution.py:108
  484.2 2.1 fusion.10
  486.3 3.5 fusion.32
  489.8 6.1 convolution_convert_fusion.1
  495.9 4.0 copy.24
  502.8 195.9 %reduce-scatter.9.cloned.1.call-done = bf16[128,512]{1,0:T(8,128)(2,1)} async-done(((bf16[2048,512]{1,0:T(8,128)(2,1)}), bf16[128,512]{1,0:T(8,128)(2,1)}) %reduce-scatter.9.cloned.1.call-update) | async-done | bytes 131088
  700.5 150.5 %all-reduce.4.cloned.1.call-done = bf16[512,512]{1,0:T(8,128)(2,1)} async-done(((bf16[512,512]{1,0:T(8,128)(2,1)}), bf16[512,512]{1,0:T(8,128)(2,1)}) %all-reduce.4.cloned.1.call-update) | async-done | bytes 524304 | tf_op jit(solution)/shard_map/psum | solution.py:127
  851.0 92.6 %all-gather.14.cloned.1.call-done = bf16[512,2048]{1,0:T(8,128)(2,1)} async-done(((bf16[512,128]{1,0:T(8,128)(2,1)}), bf16[512,2048]{1,0:T(8,128)(2,1)}) %all-gather.14.cloned.1.call-update) | async-done | bytes 2097168 | tf_op jit(solution)/shard_map/all_gather | solution.py:125
  943.6 4.3 multiply_reduce_fusion
  951.5 30.9 %psum.39 = bf16[]{:T(256)} all-reduce(bf16[]{:T(256)} %get-tuple-element.18), channel_id=1, replica_groups=mesh['dp'=16,'tensor'=16] {'dp'}, use_global_device_ids=true, to_apply=%region_12.13 | all-reduce | flops 1 | bytes 4 | tf_op jit(solution)/shard_map/psum | solution.py:148
  983.0 90.9 %all-reduce.6.cloned.1.call-done = (bf16[512,128]{1,0:T(8,128)(2,1)}, bf16[512,128]{1,0:T(8,128)(2,1)}, bf16[128,512]{1,0:T(8,128)(2,1)}) async-done(((bf16[512,128]{1,0:T(8,128)(2,1)}, bf16[512,128]{1,0:T(8,128)(2,1)}, bf16[128,512]{1,0:T(8,128)(2,1)}), (bf16[512,128]{1,0:T(8,128)(2,1)}, bf16[512,128]{1,0:T(8,128)(2,1)}, bf16[128,512]{1,0:T(8,128)(2,1)})) %all-reduce.6.cloned.1.call-update) | async-done | bytes 393232 | tf_op jit(solution)/shard_map/psum | solution.py:145
  1077.1 1.6 convert_element_type.149
  (73 shorter events, 18.5 us)
Async XLA Ops:
  7.2 482.7 %copy-start = (bf16[512,2048]{1,0:T(8,128)(2,1)S(1)}, bf16[512,2048]{1,0:T(8,128)(2,1)}, u32[]{:S(2)}) copy-start(bf16[512,2048]{1,0:T(8,128)(2,1)} %param.28) | copy-start | bytes 6291460
  7.2 93.3 %copy-start.6 = (bf16[2048,128]{1,0:T(8,128)(2,1)S(1)}, bf16[2048,128]{1,0:T(8,128)(2,1)}, u32[]{:S(2)}) copy-start(bf16[2048,128]{1,0:T(8,128)(2,1)} %param.22) | copy-start | bytes 1572868
  7.2 89.0 %all-gather.6.cloned.1.call-start = ((), (), s32[]{:S(2)}) async-start(), calls=%async_computation.2 | async-start | bytes 2228224 | tf_op jit(solution)/shard_map/all_gather | solution.py:52
  7.9 132.7 %all-gather.10.cloned.1.call-start = ((), (), s32[]{:S(2)}) async-start(), calls=%async_computation.4 | async-start | bytes 2228224 | tf_op jit(solution)/shard_map/all_gather | solution.py:73
  8.7 93.1 %copy-start.7 = (bf16[2048,128]{1,0:T(8,128)(2,1)S(1)}, bf16[2048,128]{1,0:T(8,128)(2,1)}, u32[]{:S(2)}) copy-start(bf16[2048,128]{1,0:T(8,128)(2,1)} %param.23) | copy-start | bytes 1572868
  100.5 1.3 copy-start.1
  101.8 5.3 copy-start.10
  103.9 75.7 %all-gather.8.cloned.1.call-start = ((), (), s32[]{:S(2)}) async-start(), calls=%async_computation.3 | async-start | bytes 2228224 | tf_op jit(solution)/shard_map/all_gather | solution.py:74
  107.0 289.3 %reduce-scatter.7.cloned.1.call-start = ((), (), s32[]{:S(2)}) async-start(), calls=%async_computation.8 | async-start | bytes 2228224
  146.3 5.7 copy-start.2
  152.0 27.6 %copy-start.11 = (bf16[128,2048]{1,0:T(8,128)(2,1)S(1)}, bf16[128,2048]{1,0:T(8,128)(2,1)}, u32[]{:S(2)}) copy-start(bf16[128,2048]{1,0:T(8,128)(2,1)} %param.25) | copy-start | bytes 1572868
  193.6 203.7 %copy-start.5 = (bf16[512,128]{1,0:T(8,128)(2,1)S(1)}, bf16[512,128]{1,0:T(8,128)(2,1)}, u32[]{:S(2)}) copy-start(bf16[512,128]{1,0:T(8,128)(2,1)} %param.17) | copy-start | bytes 393220
  193.6 292.7 %copy-start.13 = (f32[2048]{0:T(1024)S(1)}, f32[2048]{0:T(1024)}, u32[]{:S(2)}) copy-start(f32[2048]{0:T(1024)} %param.21) | copy-start | bytes 24580
  197.6 286.6 %all-gather.12.cloned.1.call-start = ((), (), s32[]{:S(2)}) async-start(), calls=%async_computation.5 | async-start | bytes 2228224 | tf_op jit(solution)/shard_map/all_gather | solution.py:108
  398.1 300.7 %reduce-scatter.9.cloned.1.call-start = ((), (), s32[]{:S(2)}) async-start(), calls=%async_computation.9 | async-start | bytes 2228224
  495.9 4.1 copy-start.3
  495.9 4.3 copy-start.9
  495.9 4.7 copy-start.12
  495.9 5.7 copy-start.8
  499.9 199.8 %copy-start.4 = (bf16[512,128]{1,0:T(8,128)(2,1)S(1)}, bf16[512,128]{1,0:T(8,128)(2,1)}, u32[]{:S(2)}) copy-start(bf16[512,128]{1,0:T(8,128)(2,1)} %add_convert_fusion.1) | copy-start | bytes 393220
  500.0 351.0 %all-reduce.4.cloned.1.call-start = ((), (), s32[]{:S(2)}) async-start(), calls=%async_computation.6 | async-start | bytes 1048576 | tf_op jit(solution)/shard_map/psum | solution.py:127
  502.8 440.8 %all-gather.14.cloned.1.call-start = ((), (), s32[]{:S(2)}) async-start(), calls=%async_computation.7 | async-start | bytes 2228224 | tf_op jit(solution)/shard_map/all_gather | solution.py:125
  700.5 373.4 %all-reduce.6.cloned.1.call-start = ((), (), s32[]{:S(2)}) async-start(), calls=%async_computation.10 | async-start | bytes 786432 | tf_op jit(solution)/shard_map/psum | solution.py:145
  947.9 2.4 copy-start.14
Sparse Core Ops, SparseCore 0:
  10.5 85.6 all-gather.5
  104.0 36.5 all-gather.9
  143.0 36.5 all-gather.7
  197.7 198.5 reduce-scatter.6
  399.2 84.9 all-gather.11
  500.1 198.5 reduce-scatter.8
  701.3 149.6 all-reduce.3
  854.3 89.2 all-gather.13
  951.6 122.2 all-reduce.5
where the time goes:
time: 1090 us
  waiting for transfers between devices  958 us (88%)
  matrix products  44.3 us (4%)
  blocking collectives  30.9 us (3%)
  other arithmetic  20.5 us (2%)
  local copies, waits for them, and re-layouts  16.3 us (1%)
  between operations  15.8 us (1%)
    unnamed x11, waiting for transfers between devices  395 us
    psum x1, waiting for transfers between devices, local(): lax.psum(student_part.astype(jnp.bfloat16), 'tensor').astype(jnp.float32)  150 us
    all_gather x1, waiting for transfers between devices, local(): teacher_full = lax.all_gather(teacher_out, 'tensor', axis=1, tiled=True)  92.6 us
    psum x1, waiting for transfers between devices, local(): lax.psum(grad_gate_part.astype(jnp.bfloat16), 'dp').astype(jnp.float32)  90.9 us
    all_gather x1, waiting for transfers between devices, local(): lax.all_gather(tokens, 'tensor', axis=1, tiled=True).astype(jnp.float32)  87.6 us
    all_gather x1, waiting for transfers between devices, local(): mixed = lax.all_gather(mixed_own, 'tensor', axis=1, tiled=True)  85.9 us
    all_gather x1, waiting for transfers between devices, local(): key_block = lax.all_gather(keys_flat, 'dp', axis=0, tiled=True)  33.4 us
    psum x1, blocking collectives, local(): lax.psum(square_sum.astype(jnp.bfloat16), 'dp').astype(jnp.float32)  30.9 us
  transfers between devices with their start and end apart: 9, of which 9 were waited for; matrix products, arithmetic and copies ran while one was open for 2% of the time, Pallas kernels for 0%

commit v1 on v0

v1 whole, which is shorter than its diff:
```python
import functools

import jax
import jax.numpy as jnp
from jax import lax
from jax.experimental import pallas as pl
from jax.experimental.pallas import tpu as pltpu
from jax.sharding import PartitionSpec as P

HD = 128
NZ = 8
NY = 4
MESH = pl.DeviceIdType.MESH
VM = pl.BlockSpec(memory_space=pltpu.VMEM)
SM = pl.BlockSpec(memory_space=pltpu.SMEM)
LIMIT = 56 * 1024 * 1024
F32 = jnp.float32
BF16 = jnp.bfloat16


def params(collective_id):
    return pltpu.CompilerParams(
        collective_id=collective_id, has_side_effects=True, vmem_limit_bytes=LIMIT
    )


def remote(src, dst, send_sem, recv_sem, device):
    return pltpu.make_async_remote_copy(
        src_ref=src,
        dst_ref=dst,
        send_sem=send_sem,
        recv_sem=recv_sem,
        device_id=device,
        device_id_type=MESH,
    )


def greet(devices):
    barrier = pltpu.get_barrier_semaphore()
    for device in devices:
        pl.semaphore_signal(barrier, inc=1, device_id=device, device_id_type=MESH)
    pl.semaphore_wait(barrier, len(devices))


def places():
    dp, tensor = lax.axis_index("dp"), lax.axis_index("tensor")
    x_hi, z = tensor // NZ, lax.rem(tensor, NZ)
    return dp, tensor, x_hi, z


def turn(z, by, size):
    return lax.rem(z + by + size, size)


def carries(way, far, half):
    return far < 4 or half == way


class Ring:
    def __init__(self, ref, at, z, device, send_sem, recv_sem):
        self.ref, self.at, self.z = ref, at, z
        self.next = (device(turn(z, 1, NZ)), device(turn(z, -1, NZ)))
        self.send_sem, self.recv_sem = send_sem, recv_sem
        self.sent = []

    def copy(self, way, far, half, hops):
        sign = 1 if way == 0 else -1
        block = self.ref.at[self.at(turn(self.z, -sign * hops, NZ), half)]
        return remote(
            block,
            block,
            self.send_sem.at[way, far - 1, half],
            self.recv_sem.at[way, far - 1, half],
            self.next[way],
        )

    def send(self, way, far, half):
        copy = self.copy(way, far, half, far - 1)
        copy.start()
        self.sent.append(copy)

    def arrived(self, way, far, half):
        self.copy(way, far, half, far).wait_recv()

    def finish(self):
        for copy in self.sent:
            copy.wait_send()


def gather_body(order, x_ref, out_ref, send_sem, recv_sem, x_send, x_recv):
    dp, tensor, x_hi, z = places()
    partner = (dp, (1 - x_hi) * NZ + z)

    def device(zz):
        return (dp, x_hi * NZ + zz)

    def at(zz, half):
        xx = x_hi if half == 0 else 1 - x_hi
        return xx * NZ + zz if order == "tensor" else zz * 2 + xx

    ring = Ring(out_ref, at, z, device, send_sem, recv_sem)
    out_ref[at(z, 0)] = x_ref[...]
    greet([partner, ring.next[0], ring.next[1]])
    own = out_ref.at[at(z, 0)]
    other = out_ref.at[at(z, 1)]
    cross = remote(own, own, x_send, x_recv, partner)
    cross.start()
    for half in range(2):
        if half == 1:
            remote(other, other, x_send, x_recv, partner).wait_recv()
        for way in range(2):
            ring.send(way, 1, half)
    for far in range(2, 5):
        for half in range(2):
            for way in range(2):
                if carries(way, far, half):
                    ring.arrived(way, far - 1, half)
                    ring.send(way, far, half)
    for way in range(2):
        ring.arrived(way, 3, 1 - way)
        ring.arrived(way, 4, way)
    cross.wait_send()
    ring.finish()


def tensor_gather(block, order, collective_id):
    return pl.pallas_call(
        functools.partial(gather_body, order),
        out_shape=jax.ShapeDtypeStruct((2 * NZ,) + block.shape, block.dtype),
        in_specs=[VM],
        out_specs=VM,
        scratch_shapes=[
            pltpu.SemaphoreType.DMA((2, 4, 2)),
            pltpu.SemaphoreType.DMA((2, 4, 2)),
            pltpu.SemaphoreType.DMA,
            pltpu.SemaphoreType.DMA,
        ],
        compiler_params=params(collective_id),
        name="tensor_gather",
    )(block)


def scatter_body(
    part_ref, out_ref, sbuf, rbuf, xsend_buf, xrecv_buf, send_sem, recv_sem, x_send, x_recv
):
    dp, tensor, x_hi, z = places()
    partner = (dp, (1 - x_hi) * NZ + z)
    nexts = ((dp, x_hi * NZ + turn(z, 1, NZ)), (dp, x_hi * NZ + turn(z, -1, NZ)))

    def at(zz, half):
        return zz * 2 + (x_hi if half == 0 else 1 - x_hi)

    greet([partner, nexts[0], nexts[1]])
    sent = []

    def copy(way, far, half, src):
        return remote(
            src,
            rbuf.at[way, far - 1, half],
            send_sem.at[way, far - 1, half],
            recv_sem.at[way, far - 1, half],
            nexts[way],
        )

    def arrived(way, far, half):
        copy(way, far, half, rbuf.at[way, far - 1, half]).wait_recv()

    for far in range(4, 0, -1):
        for half in (1, 0):
            for way in range(2):
                if not carries(way, far, half):
                    continue
                place = at(turn(z, far if way == 0 else -far, NZ), half)
                if far == 4 or (far == 3 and half != way):
                    src = part_ref.at[place]
                else:
                    arrived(way, far + 1, half)
                    sbuf[way, far - 1, half] = (
                        part_ref[place].astype(F32) + rbuf[way, far, half].astype(F32)
                    ).astype(BF16)
                    src = sbuf.at[way, far - 1, half]
                one = copy(way, far, half, src)
                one.start()
                sent.append(one)

    def total(half):
        for way in range(2):
            arrived(way, 1, half)
        return (
            part_ref[at(z, half)].astype(F32)
            + rbuf[0, 0, half].astype(F32)
            + rbuf[1, 0, half].astype(F32)
        )

    xsend_buf[...] = total(1).astype(BF16)
    cross = remote(xsend_buf, xrecv_buf, x_send, x_recv, partner)
    cross.start()
    mine = total(0)
    cross.wait_recv()
    out_ref[...] = mine + xrecv_buf[...].astype(F32)
    cross.wait_send()
    for one in sent:
        one.wait_send()


def tensor_scatter(part, collective_id):
    block = part.shape[1:]
    return pl.pallas_call(
        scatter_body,
        out_shape=jax.ShapeDtypeStruct(block, F32),
        in_specs=[VM],
        out_specs=VM,
        scratch_shapes=[
            pltpu.VMEM((2, 4, 2) + block, BF16),
            pltpu.VMEM((2, 4, 2) + block, BF16),
            pltpu.VMEM(block, BF16),
            pltpu.VMEM(block, BF16),
            pltpu.SemaphoreType.DMA((2, 4, 2)),
            pltpu.SemaphoreType.DMA((2, 4, 2)),
            pltpu.SemaphoreType.DMA,
            pltpu.SemaphoreType.DMA,
        ],
        compiler_params=params(collective_id),
        name="tensor_scatter",
    )(part)


def dp_gather_body(x_ref, out_ref, y_send, y_recv, x_send, x_recv, c_send, c_recv):
    dp, tensor, _, _ = places()
    x_lo, y, core = dp // (2 * NY), lax.rem(dp // 2, NY), lax.rem(dp, 2)

    def index(xx, yy, cc):
        return xx * 2 * NY + yy * 2 + cc

    def at(yy, half, cc):
        return index(x_lo if half == 0 else 1 - x_lo, yy, cc)

    partner = (index(1 - x_lo, y, core), tensor)
    sibling = (index(x_lo, y, 1 - core), tensor)
    nexts = (
        (index(x_lo, turn(y, 1, NY), core), tensor),
        (index(x_lo, turn(y, -1, NY), core), tensor),
    )
    out_ref[at(y, 0, core)] = x_ref[...]
    greet([partner, sibling, nexts[0], nexts[1]])
    sent = []

    def start(copy):
        copy.start()
        sent.append(copy)

    def share(yy, half, slot):
        block = out_ref.at[at(yy, half, core)]
        start(remote(block, block, c_send.at[slot], c_recv.at[slot], sibling))

    def copy(way, far, half, hops):
        block = out_ref.at[at(turn(y, -hops if way == 0 else hops, NY), half, core)]
        return remote(
            block,
            block,
            y_send.at[way, far - 1, half],
            y_recv.at[way, far - 1, half],
            nexts[way],
        )

    own = out_ref.at[at(y, 0, core)]
    other = out_ref.at[at(y, 1, core)]
    start(remote(own, own, x_send, x_recv, partner))
    for way in range(2):
        start(copy(way, 1, 0, 0))
    share(y, 0, 0)
    remote(other, other, x_send, x_recv, partner).wait_recv()
    for way in range(2):
        start(copy(way, 1, 1, 0))
    share(y, 1, 1)
    slot = 2
    origins = []
    for half in range(2):
        for way in range(2):
            copy(way, 1, half, 1).wait_recv()
            if half == way:
                start(copy(way, 2, half, 1))
            origin = turn(y, -1 if way == 0 else 1, NY)
            share(origin, half, slot)
            slot += 1
    for way in range(2):
        copy(way, 2, way, 2).wait_recv()
        share(turn(y, 2, NY), way, slot)
        slot += 1
    arrivals = [(0, 0), (0, 1), (-1, 0), (1, 0), (-1, 1), (1, 1), (2, 0), (2, 1)]
    for slot, (by, half) in enumerate(arrivals):
        block = out_ref.at[at(turn(y, by, NY), half, 1 - core)]
        remote(block, block, c_send.at[slot], c_recv.at[slot], sibling).wait_recv()
    for one in sent:
        one.wait_send()


def dp_gather(block, collective_id):
    return pl.pallas_call(
        dp_gather_body,
        out_shape=jax.ShapeDtypeStruct((4 * NY,) + block.shape, block.dtype),
        in_specs=[VM],
        out_specs=VM,
        scratch_shapes=[
            pltpu.SemaphoreType.DMA((2, 2, 2)),
            pltpu.SemaphoreType.DMA((2, 2, 2)),
            pltpu.SemaphoreType.DMA,
            pltpu.SemaphoreType.DMA,
            pltpu.SemaphoreType.DMA((8,)),
            pltpu.SemaphoreType.DMA((8,)),
        ],
        compiler_params=params(collective_id),
        name="dp_gather",
    )(block)


def dp_sum_body(
    part_ref,
    square_ref,
    out_ref,
    total_ref,
    inbox,
    squares,
    result,
    send1,
    recv1,
    send2,
    recv2,
    send3,
    recv3,
):
    dp, tensor, _, _ = places()
    size = 4 * NY
    peers = [turn(dp, by, size) for by in range(1, size)]
    greet([(peer, tensor) for peer in peers])
    sent = []

    def start(copy):
        copy.start()
        sent.append(copy)

    for by, peer in enumerate(peers):
        start(
            remote(part_ref.at[peer], inbox.at[by], send1.at[by], recv1.at[by], (peer, tensor))
        )
        start(remote(square_ref, squares.at[by], send2.at[by], recv2.at[by], (peer, tensor)))
    total = part_ref[dp].astype(F32)
    for by, peer in enumerate(peers):
        remote(
            part_ref.at[peer], inbox.at[by], send1.at[by], recv1.at[by], (peer, tensor)
        ).wait_recv()
        total = total + inbox[by].astype(F32)
    result[dp] = total.astype(BF16)
    mine = result.at[dp]
    for by, peer in enumerate(peers):
        start(remote(mine, mine, send3.at[by], recv3.at[by], (peer, tensor)))
    square = square_ref[...]
    for by, peer in enumerate(peers):
        remote(square_ref, squares.at[by], send2.at[by], recv2.at[by], (peer, tensor)).wait_recv()
        square = square + squares[by]
    total_ref[...] = square
    for by, peer in enumerate(peers):
        origin = turn(dp, -(by + 1), size)
        block = result.at[origin]
        remote(block, block, send3.at[by], recv3.at[by], (peer, tensor)).wait_recv()
    out_ref[...] = result[...].astype(F32)
    for one in sent:
        one.wait_send()


def dp_sum(part, square, collective_id):
    size = 4 * NY
    return pl.pallas_call(
        dp_sum_body,
        out_shape=(
            jax.ShapeDtypeStruct(part.shape, F32),
            jax.ShapeDtypeStruct(square.shape, F32),
        ),
        in_specs=[VM, VM],
        out_specs=(VM, VM),
        scratch_shapes=[
            pltpu.VMEM((size - 1,) + part.shape[1:], BF16),
            pltpu.VMEM((size - 1,) + square.shape, F32),
            pltpu.VMEM(part.shape, BF16),
        ]
        + [pltpu.SemaphoreType.DMA((size - 1,))] * 6,
        compiler_params=params(collective_id),
        name="dp_sum",
    )(part, square)


def spread_body(
    scaled_ref,
    teacher_ref,
    out_ref,
    columns_ref,
    send_sem,
    recv_sem,
    x_send,
    x_recv,
    t_send,
    t_recv,
):
    dp, tensor, x_hi, z = places()
    partner = (dp, (1 - x_hi) * NZ + z)
    size = 2 * NZ
    row = z * 2 + x_hi

    def device(zz):
        return (dp, x_hi * NZ + zz)

    def at(zz, half):
        return zz * 2 + (x_hi if half == 0 else 1 - x_hi)

    ring = Ring(out_ref, at, z, device, send_sem, recv_sem)
    out_ref[row] = scaled_ref[...]
    peers = [turn(tensor, by, size) for by in range(1, size)]
    greet([(dp, peer) for peer in peers])
    own = out_ref.at[at(z, 0)]
    other = out_ref.at[at(z, 1)]
    cross = remote(own, own, x_send, x_recv, partner)
    cross.start()
    for half in range(2):
        if half == 1:
            remote(other, other, x_send, x_recv, partner).wait_recv()
        for way in range(2):
            ring.send(way, 1, half)
    sent = []
    for by, peer in enumerate(peers):
        one = remote(
            teacher_ref.at[peer],
            columns_ref.at[row],
            t_send.at[by],
            t_recv.at[by],
            (dp, peer),
        )
        one.start()
        sent.append(one)
    columns_ref[row] = teacher_ref[tensor]
    for far in range(2, 5):
        for half in range(2):
            for way in range(2):
                if carries(way, far, half):
                    ring.arrived(way, far - 1, half)
                    ring.send(way, far, half)
    for way in range(2):
        ring.arrived(way, 3, 1 - way)
        ring.arrived(way, 4, way)
    for by, peer in enumerate(peers):
        origin = turn(tensor, -(by + 1), size)
        theirs = columns_ref.at[lax.rem(origin, NZ) * 2 + origin // NZ]
        remote(theirs, theirs, t_send.at[by], t_recv.at[by], (dp, peer)).wait_recv()
    cross.wait_send()
    for one in sent:
        one.wait_send()
    ring.finish()


def spread(scaled, teacher, collective_id):
    size = 2 * NZ
    return pl.pallas_call(
        spread_body,
        out_shape=(
            jax.ShapeDtypeStruct((size,) + scaled.shape, scaled.dtype),
            jax.ShapeDtypeStruct((size,) + teacher.shape[1:], teacher.dtype),
        ),
        in_specs=[VM, VM],
        out_specs=(VM, VM),
        scratch_shapes=[
            pltpu.SemaphoreType.DMA((2, 4, 2)),
            pltpu.SemaphoreType.DMA((2, 4, 2)),
            pltpu.SemaphoreType.DMA,
            pltpu.SemaphoreType.DMA,
            pltpu.SemaphoreType.DMA((size - 1,)),
            pltpu.SemaphoreType.DMA((size - 1,)),
        ],
        compiler_params=params(collective_id),
        name="spread",
    )(scaled, teacher)


def attention_body(tile, bounds, query_ref, pair_ref, start_ref, out_ref):
    rows = query_ref.shape[0]
    span = pair_ref.shape[2]
    mine = bounds[0]
    factor = HD ** (-0.5) * 1.4426950408889634
    for index in range(rows // tile):
        at = pl.ds(index * tile, tile)
        query = query_ref[at, :]
        start = start_ref[at, :]
        position = mine * rows + index * tile + lax.broadcasted_iota(jnp.int32, (tile, 1), 0)

        def step(masked, j, carry):
            peak, denom, accum = carry
            scores = lax.dot_general(
                query, pair_ref[j, 0], (((1,), (1,)), ((), ())), preferred_element_type=F32
            )
            if masked:
                column = j * span + lax.broadcasted_iota(jnp.int32, (tile, span), 1)
                allowed = (column >= start) & (column <= position)
                scores = jnp.where(allowed, scores, -1e30)
            new_peak = jnp.maximum(peak, jnp.max(scores, axis=1, keepdims=True))
            weights = jnp.exp2((scores - new_peak) * factor)
            if masked:
                weights = jnp.where(allowed, weights, 0.0)
            scale = jnp.exp2((peak - new_peak) * factor)
            denom = denom * scale + jnp.sum(weights, axis=1, keepdims=True)
            accum = accum * scale + jnp.dot(
                weights.astype(BF16), pair_ref[j, 1], preferred_element_type=F32
            )
            return new_peak, denom, accum

        carry = (
            jnp.full((tile, 1), -1e30, F32),
            jnp.zeros((tile, 1), F32),
            jnp.zeros((tile, HD), F32),
        )
        low, inner = bounds[1 + 2 * index], bounds[2 + 2 * index]
        carry = lax.fori_loop(low, inner, functools.partial(step, True), carry)
        carry = lax.fori_loop(inner, mine, functools.partial(step, False), carry)
        peak, denom, accum = step(True, mine, carry)
        out_ref[at, :] = (accum / denom).astype(BF16)


def attention(query, pairs, starts, first_row):
    rows, span, tile = query.shape[0], pairs.shape[2], 256
    mine = first_row // rows
    bounds = [mine]
    for index in range(rows // tile):
        bounds.append(starts[index * tile] // span)
        last = starts[(index + 1) * tile - 1]
        bounds.append(jnp.minimum((last + span - 1) // span, mine))
    return pl.pallas_call(
        functools.partial(attention_body, tile),
        out_shape=jax.ShapeDtypeStruct(query.shape, BF16),
        in_specs=[SM, VM, VM, VM],
        out_specs=VM,
        compiler_params=pltpu.CompilerParams(vmem_limit_bytes=LIMIT),
        name="attention",
    )(jnp.stack(bounds).astype(jnp.int32), query, pairs, starts[:, None])


def rms_scale(values):
    return values * lax.rsqrt(jnp.mean(values * values, axis=-1, keepdims=True) + 1e-05)


def frequencies(head_dim):
    indices = jnp.arange(head_dim // 2).astype(F32)
    return jnp.exp(-jnp.log(500000.0) * 2.0 * indices / head_dim)


def local(
    tokens,
    series_ids,
    offsets,
    norm_gain,
    mlp_gain,
    w_query,
    w_key,
    w_value,
    w_out,
    w_gate,
    w_up,
    w_down,
    projector,
    student_in,
    s_gate,
    s_up,
    s_down,
):
    rows = tokens.shape[0]
    size = 2 * NZ
    own = rows // size
    dp, tensor, x_hi, z = places()
    first_row = dp * rows
    my_rows = (z * 2 + x_hi) * own

    angles = offsets.astype(F32)[:, None] * frequencies(HD)[None, :]
    cosine, sine = jnp.cos(angles), jnp.sin(angles)

    def rotary(values):
        a, b = values[:, : HD // 2], values[:, HD // 2 :]
        return jnp.concatenate([a * cosine - b * sine, a * sine + b * cosine], axis=1).astype(BF16)

    student_full = student_in.astype(F32)
    student_normed = rms_scale(student_full).astype(BF16)
    s_gate_out = jnp.dot(student_normed, s_gate, preferred_element_type=F32)
    s_up_out = jnp.dot(student_normed, s_up, preferred_element_type=F32)
    sigmoid_gate = jax.nn.sigmoid(s_gate_out)
    s_hidden = (s_gate_out * sigmoid_gate * s_up_out).astype(BF16)
    student_part = jnp.dot(s_hidden, s_down, preferred_element_type=F32).astype(BF16)
    student_sum = tensor_scatter(student_part.reshape(size, own, -1), 1)

    blocks = tensor_gather(tokens, "tensor", 2)
    tokens_full = jnp.transpose(blocks, (1, 0, 2)).reshape(rows, -1)
    normed = (rms_scale(tokens_full.astype(F32)) * norm_gain).astype(BF16)
    query = rotary(jnp.dot(normed, w_query, preferred_element_type=F32))
    key = rotary(jnp.dot(normed, w_key, preferred_element_type=F32))
    value = jnp.dot(normed, w_value, preferred_element_type=F32).astype(BF16)
    pairs = dp_gather(jnp.stack([key, value]), 3)

    series = jnp.arange(8, dtype=jnp.int32)
    series_start = jnp.sum((series_ids[None, :] < series[:, None]).astype(jnp.int32), axis=1)
    query_series = lax.dynamic_slice_in_dim(series_ids, first_row, rows, 0)
    starts = jnp.sum(
        jnp.where(query_series[:, None] == series[None, :], series_start[None, :], 0), axis=1
    )
    attended = attention(query, pairs, starts, first_row)

    partial_out = jnp.dot(attended, w_out, preferred_element_type=F32).astype(BF16)
    own_sum = tensor_scatter(partial_out.reshape(size, own, -1), 4)
    my_tokens = lax.dynamic_slice_in_dim(tokens_full, my_rows, own, 0).astype(F32)
    mixed = (my_tokens + own_sum).astype(BF16)
    normed_two = (rms_scale(mixed.astype(F32)) * mlp_gain).astype(BF16)
    normed_two = tensor_gather(normed_two, "rows", 5).reshape(rows, -1)

    gate_out = jnp.dot(normed_two, w_gate, preferred_element_type=F32)
    up_out = jnp.dot(normed_two, w_up, preferred_element_type=F32)
    hidden = (jax.nn.silu(gate_out) * up_out).astype(BF16)
    mlp_part = jnp.dot(hidden, w_down, preferred_element_type=F32).astype(BF16)
    mlp_sum = tensor_scatter(mlp_part.reshape(size, own, -1), 6)
    teacher = (mixed.astype(F32) + mlp_sum).astype(BF16)

    target = jnp.dot(teacher, projector, preferred_element_type=F32)
    my_student = lax.dynamic_slice_in_dim(student_in, my_rows, own, 0).astype(F32)
    difference = my_student + student_sum - target
    total_rows = rows * lax.axis_size("dp")
    scaled = (difference * total_rows ** (-0.5)).astype(BF16)
    teacher_columns = jnp.transpose(teacher.reshape(own, size, -1), (1, 0, 2))
    scaled, teacher_out = spread(scaled, teacher_columns, 7)
    scaled = scaled.reshape(rows, -1)
    teacher_out = teacher_out.reshape(rows, -1)

    grad_hidden = jnp.einsum("rc,kc->rk", scaled, s_down, preferred_element_type=F32)
    grad_up_in = (grad_hidden * s_gate_out * sigmoid_gate).astype(BF16)
    grad_gate_in = (
        grad_hidden * s_up_out * sigmoid_gate * (1.0 + s_gate_out * (1.0 - sigmoid_gate))
    ).astype(BF16)
    grads = [
        jnp.einsum("rc,rk->ck", left, right, preferred_element_type=F32).astype(BF16)
        for left, right in (
            (student_normed, grad_gate_in),
            (student_normed, grad_up_in),
            (scaled, s_hidden),
        )
    ]
    units = grads[0].shape[1]
    parts = jnp.stack([one.reshape(size, -1, units) for one in grads], axis=1)
    parts = parts.reshape(size, -1, units)
    squares = jnp.square(scaled.astype(F32))
    squares = jnp.sum(squares.reshape(-1, 8, 128), axis=0)
    sums, square_total = dp_sum(parts, squares, 8)
    sums = sums.reshape(size, 3, -1, units)
    grad_gate, grad_up, grad_down = (sums[:, i].reshape(-1, units) for i in range(3))
    error = jnp.sum(square_total) / student_in.shape[1]
    return (teacher_out, grad_gate, grad_up, grad_down.T, error)


def solution(mesh):
    in_specs = (
        P("dp", "tensor"),
        P(),
        P("dp"),
        P(),
        P(),
        P(None, "tensor"),
        P(None, "tensor"),
        P(None, "tensor"),
        P("tensor", None),
        P(None, "tensor"),
        P(None, "tensor"),
        P("tensor", None),
        P(),
        P("dp", None),
        P(None, "tensor"),
        P(None, "tensor"),
        P("tensor", None),
    )
    out_specs = (P("dp", "tensor"), P(None, "tensor"), P(None, "tensor"), P("tensor", None), P())
    return jax.shard_map(local, mesh=mesh, in_specs=in_specs, out_specs=out_specs, check_vma=False)
```

time: 1090 us -> 286 us (0.26)
  waiting for transfers between devices: 958 us -> 0 us
  Pallas kernels: 0 us -> 228 us
  blocking collectives: 30.9 us -> 0 us
  matrix products: 44.3 us -> 21 us
    unnamed x11 -> x0, waiting for transfers between devices: 395 us -> none
    all_gather x5 -> x0, waiting for transfers between devices: 321 us -> none  [the longest x1 92.6 us: local(): teacher_full = lax.all_gather(teacher_out, 'tensor', axis=1, tiled=True)]
    psum x2 -> x0, waiting for transfers between devices: 241 us -> none  [the longest x1 150 us: local(): lax.psum(student_part.astype(jnp.bfloat16), 'tensor').astype(jnp.float32)]
    pallas_call x0 -> x9, Pallas kernels: none -> 228 us  [the longest x3 72.5 us: tensor_scatter(): pl.pallas_call(scatter_body, out_shape=jax.ShapeDtypeStruct(block, F32),...]
    psum x1 -> x0, blocking collectives: 30.9 us -> none  [local(): lax.psum(square_sum.astype(jnp.bfloat16), 'dp').astype(jnp.float32)]
    dot_general x15 -> x14, matrix products: 44.3 us -> 21 us  [the longest x1 6.01 us: local(): mlp_part = jnp.dot(hidden, w_down, preferred_element_type=F32).astype(BF16)]
    unnamed x34 -> x46, local copies, waits for them, and re-layouts: 16.3 us -> 2.4 us
  transfers between devices with their start and end apart: 9 -> 0, of which waited for: 9 -> 0; matrix products, arithmetic and copies ran while one was open for 2% -> 0% of each run, Pallas kernels for 0% -> 0%
where the time goes in v1:
time: 286 us
  Pallas kernels  228 us (80%)
  matrix products  21 us (7%)
  other arithmetic  15.2 us (5%)
  local copies, waits for them, and re-layouts  11.6 us (4%)
  between operations  9.39 us (3%)
    pallas_call x3, Pallas kernels, tensor_scatter(): pl.pallas_call(scatter_body, out_shape=jax.ShapeDtypeStruct(block, F32),...  72.5 us
    pallas_call x2, Pallas kernels, tensor_gather(): pl.pallas_call(functools.partial(gather_body, order), out_shape=jax.Shape...  57.7 us
    pallas_call x1, Pallas kernels, dp_sum(): pl.pallas_call(dp_sum_body, out_shape=(jax.ShapeDtypeStruct(part.shape, F...  46.1 us
    pallas_call x1, Pallas kernels, dp_gather(): pl.pallas_call(dp_gather_body, out_shape=jax.ShapeDtypeStruct((4 * NY,) +...  29.3 us
    pallas_call x1, Pallas kernels, spread(): pl.pallas_call(spread_body, out_shape=(jax.ShapeDtypeStruct((size,) + sca...  17.8 us
    dot_general x1, matrix products, local(): mlp_part = jnp.dot(hidden, w_down, preferred_element_type=F32).astype(BF16)  6.01 us

profile of v1, /device:TPU:1, one launch (start us, length us, event | category | flops | bytes accessed | tf_op | source)
XLA Modules:
  0.0 285.6 jit_solution(14513037163661018116)
XLA Ops:
  10.4 31.7 %tensor_gather.2 = bf16[16,512,128]{2,1,0:T(8,128)(2,1)} custom-call(bf16[512,128]{1,0:T(8,128)(2,1)} %x_ref.1), custom_call_target="tpu_custom_call" | custom-call | tf_op jit(solution)/shard_map/tensor_gather/pallas_call | solution.py:127
  42.0 2.2 multiply_reduce_fusion
  47.1 1.3 fusion.30
  50.0 29.3 %dp_gather.1.pair_ref = bf16[16,2,512,128]{3,2,1,0:T(8,128)(2,1)} custom-call(bf16[2,512,128]{2,1,0:T(8,128)(2,1)} %pad_maximum_fusion.1.x_ref), custom_call_target="tpu_custom_call" | custom-call | tf_op jit(solution)/shard_map/dp_gather/pallas_call | solution.py:299
  80.9 5.0 %attention.1 = bf16[512,128]{1,0:T(8,128)(2,1)} custom-call(s32[5]{0:T(128)} %stack.33.bounds, bf16[512,128]{1,0:T(8,128)(2,1)} %pad_maximum_fusion.2.query_ref, bf16[16,2,512,128]{3,2,1,0:T(8,128)(2,1)} %dp_gather.1.pair_ref, s32[512,1]{1,0:T(8,128)} %copy.48.start_ref), custom_call_target="tpu_custom_call" | custom-call | tf_op jit(solution)/shard_map/attention/pallas_call | solution.py:533
  85.9 2.9 %convolution_convert_fusion = bf16[512,2048]{1,0:T(8,128)(2,1)} fusion(bf16[512,128]{1,0:T(8,128)(2,1)} %attention.1, bf16[128,2048]{1,0:T(8,128)(2,1)S(1)} %copy-done.11), kind=kOutput, calls=%fused_computation.2 | convolution fusion | flops 269484032 | bytes 2752512 | tf_op jit(solution)/shard_map/dot_general | solution.py:610
  88.9 30.8 %tensor_scatter.4 = f32[32,2048]{1,0:T(8,128)} custom-call(bf16[16,32,2048]{2,1,0:T(8,128)(2,1)} %bitcast.80), custom_call_target="tpu_custom_call" | custom-call | tf_op jit(solution)/shard_map/tensor_scatter/pallas_call | solution.py:208
  119.7 1.9 copy_bitcast_fusion
  122.6 26.1 %tensor_gather.3 = bf16[16,32,2048]{2,1,0:T(8,128)(2,1)} custom-call(bf16[32,2048]{1,0:T(8,128)(2,1)} %fusion.25.x_ref), custom_call_target="tpu_custom_call" | custom-call | tf_op jit(solution)/shard_map/tensor_gather/pallas_call | solution.py:127
  148.7 2.8 fusion.46
  151.5 6.0 %convolution_convert_fusion.1 = bf16[512,2048]{1,0:T(8,128)(2,1)} fusion(bf16[512,2048]{1,0:T(8,128)(2,1)S(1)} %copy-done, bf16[512,2048]{1,0:T(8,128)(2,1)} %bitcast.86, bf16[2048,512]{1,0:T(8,128)(2,1)} %param.27, f32[512,512]{1,0:T(8,128)S(1)} %fusion.46), kind=kOutput, calls=%fused_computation.3 | convolution fusion | flops 2150105088 | bytes 9437184 | tf_op jit(solution)/shard_map/dot_general | solution.py:620
  157.5 25.2 %tensor_scatter.5 = f32[32,2048]{1,0:T(8,128)} custom-call(bf16[16,32,2048]{2,1,0:T(8,128)(2,1)} %bitcast.83), custom_call_target="tpu_custom_call" | custom-call | tf_op jit(solution)/shard_map/tensor_scatter/pallas_call | solution.py:208
  182.7 1.7 bitcast_bitcast_fusion.teacher_ref
  185.0 1.0 multiply_convert_fusion.3
  186.0 1.1 convolution_convert_fusion.2
  187.1 16.5 %tensor_scatter.3 = f32[32,512]{1,0:T(8,128)} custom-call(bf16[16,32,512]{2,1,0:T(8,128)(2,1)} %bitcast.84), custom_call_target="tpu_custom_call" | custom-call | tf_op jit(solution)/shard_map/tensor_scatter/pallas_call | solution.py:208
  203.7 1.9 fusion.3.scaled_ref
  205.6 17.8 %spread.1 = (bf16[16,32,512]{2,1,0:T(8,128)(2,1)}, bf16[16,32,128]{2,1,0:T(8,128)(2,1)}) custom-call(bf16[32,512]{1,0:T(8,128)(2,1)} %fusion.3.scaled_ref, bf16[16,32,128]{2,1,0:T(8,128)(2,1)} %bitcast_bitcast_fusion.teacher_ref), custom_call_target="tpu_custom_call" | custom-call | tf_op jit(solution)/shard_map/spread/pallas_call | solution.py:461
  223.4 2.2 convert_multiply_fusion.2
  225.7 2.3 square.8
  228.0 2.1 reduce_sum.68.square_ref
  230.4 1.6 convolution_convert_fusion.5
  233.6 46.1 %dp_sum.1 = (f32[16,96,128]{2,1,0:T(8,128)}, f32[8,128]{1,0:T(8,128)}) custom-call(bf16[16,96,128]{2,1,0:T(8,128)(2,1)} %bitcast.87, f32[8,128]{1,0:T(8,128)} %reduce_sum.68.square_ref), custom_call_target="tpu_custom_call" | custom-call | tf_op jit(solution)/shard_map/dp_sum/pallas_call | solution.py:373
  279.8 2.0 fusion.42
  (72 shorter events, 14.7 us)
Async XLA Ops:
  0.6 150.9 %copy-start = (bf16[512,2048]{1,0:T(8,128)(2,1)S(1)}, bf16[512,2048]{1,0:T(8,128)(2,1)}, u32[]{:S(2)}) copy-start(bf16[512,2048]{1,0:T(8,128)(2,1)} %param.28) | copy-start | bytes 6291460
  10.4 33.9 %copy-start.16 = (f32[2048]{0:T(1024)S(1)}, f32[2048]{0:T(1024)}, u32[]{:S(2)}) copy-start(f32[2048]{0:T(1024)} %param.20) | copy-start | bytes 24580
  42.0 2.3 copy-start.1
  44.3 1.0 copy-start.8
  45.3 1.0 copy-start.9
  46.4 0.7 copy-start.19
  46.4 2.0 copy-start.10
  80.9 5.0 %copy-start.11 = (bf16[128,2048]{1,0:T(8,128)(2,1)S(1)}, bf16[128,2048]{1,0:T(8,128)(2,1)}, u32[]{:S(2)}) copy-start(bf16[128,2048]{1,0:T(8,128)(2,1)} %param.25) | copy-start | bytes 1572868
  119.7 2.0 copy-start.6
  119.7 2.1 copy-start.17
  121.6 27.0 %copy-start.20 = (bf16[2048,512]{1,0:T(8,128)(2,1)S(1)}, bf16[2048,512]{1,0:T(8,128)(2,1)}, u32[]{:S(2)}) copy-start(bf16[2048,512]{1,0:T(8,128)(2,1)} %param.26) | copy-start | bytes 6291460
  157.5 26.9 %copy-start.4 = (bf16[512,512]{1,0:T(8,128)(2,1)S(1)}, bf16[512,512]{1,0:T(8,128)(2,1)}, u32[]{:S(2)}) copy-start(bf16[512,512]{1,0:T(8,128)(2,1)} %param.30) | copy-start | bytes 1572868
  157.5 27.1 %copy-start.14 = (bf16[512,128]{1,0:T(8,128)(2,1)S(1)}, bf16[512,128]{1,0:T(8,128)(2,1)}, u32[]{:S(2)}) copy-start(bf16[512,128]{1,0:T(8,128)(2,1)} %param.31) | copy-start | bytes 393220
  157.5 27.4 %copy-start.21 = (bf16[512,128]{1,0:T(8,128)(2,1)S(1)}, bf16[512,128]{1,0:T(8,128)(2,1)}, u32[]{:S(2)}) copy-start(bf16[512,128]{1,0:T(8,128)(2,1)} %param.32) | copy-start | bytes 393220
  182.7 3.3 %copy-start.7 = (bf16[128,512]{1,0:T(8,128)(2,1)S(1)}, bf16[128,512]{1,0:T(8,128)(2,1)}, u32[]{:S(2)}) copy-start(bf16[128,512]{1,0:T(8,128)(2,1)} %param.33) | copy-start | bytes 393220
  184.6 19.1 %copy-start.3 = (f32[32,2048]{1,0:T(8,128)S(1)}, f32[32,2048]{1,0:T(8,128)}, u32[]{:S(2)}) copy-start(f32[32,2048]{1,0:T(8,128)} %tensor_scatter.5) | copy-start | bytes 786436
  184.6 19.1 %copy-start.5 = (bf16[2048,512]{1,0:T(8,128)(2,1)S(1)}, bf16[2048,512]{1,0:T(8,128)(2,1)}, u32[]{:S(2)}) copy-start(bf16[2048,512]{1,0:T(8,128)(2,1)} %param.29) | copy-start | bytes 6291460
  185.0 20.6 %copy-start.12 = (f32[512,128]{1,0:T(8,128)}, f32[512,128]{1,0:T(8,128)S(1)}, u32[]{:S(2)}) copy-start(f32[512,128]{1,0:T(8,128)S(1)} %fusion.40) | copy-start | bytes 786436
  223.4 6.6 %copy-start.2 = (bf16[16,32,512]{2,1,0:T(8,128)(2,1)S(1)}, bf16[16,32,512]{2,1,0:T(8,128)(2,1)}, u32[]{:S(2)}) copy-start(bf16[16,32,512]{2,1,0:T(8,128)(2,1)} %get-tuple-element.10) | copy-start | bytes 1572868
  230.1 1.9 copy-start.13
  232.5 51.4 %copy-start.15 = (bf16[16,32,128]{2,1,0:T(8,128)(2,1)S(1)}, bf16[16,32,128]{2,1,0:T(8,128)(2,1)}, u32[]{:S(2)}) copy-start(bf16[16,32,128]{2,1,0:T(8,128)(2,1)} %get-tuple-element.9) | copy-start | bytes 393220
  279.7 2.8 copy-start.18

commit v2 on v0

v2 whole, which is shorter than its diff:
```python
import functools

import jax
import jax.numpy as jnp
from jax import lax
from jax.experimental import pallas as pl
from jax.experimental.pallas import tpu as pltpu
from jax.sharding import PartitionSpec as P

HD = 128
NZ = 8
NY = 4
MESH = pl.DeviceIdType.MESH
VM = pl.BlockSpec(memory_space=pltpu.VMEM)
SM = pl.BlockSpec(memory_space=pltpu.SMEM)
LIMIT = 56 * 1024 * 1024
F32 = jnp.float32
BF16 = jnp.bfloat16


def params(collective_id):
    return pltpu.CompilerParams(
        collective_id=collective_id, has_side_effects=True, vmem_limit_bytes=LIMIT
    )


def remote(src, dst, send_sem, recv_sem, device):
    return pltpu.make_async_remote_copy(
        src_ref=src,
        dst_ref=dst,
        send_sem=send_sem,
        recv_sem=recv_sem,
        device_id=device,
        device_id_type=MESH,
    )


def greet(devices):
    barrier = pltpu.get_barrier_semaphore()
    for device in devices:
        pl.semaphore_signal(barrier, inc=1, device_id=device, device_id_type=MESH)
    pl.semaphore_wait(barrier, len(devices))


def places():
    dp, tensor = lax.axis_index("dp"), lax.axis_index("tensor")
    x_hi, z = tensor // NZ, lax.rem(tensor, NZ)
    return dp, tensor, x_hi, z


def turn(z, by, size):
    return lax.rem(z + by + size, size)


def dma(*shape):
    return pltpu.SemaphoreType.DMA(shape)


def call(body, name, collective_id, inputs, outputs, scratch, specs=None):
    return pl.pallas_call(
        body,
        out_shape=tuple(jax.ShapeDtypeStruct(shape, kind) for shape, kind in outputs),
        in_specs=specs or [VM] * len(inputs),
        out_specs=tuple([VM] * len(outputs)),
        scratch_shapes=scratch,
        compiler_params=params(collective_id),
        name=name,
    )(*inputs)


class Sent:
    def __init__(self):
        self.copies = []

    def start(self, copy):
        copy.start()
        self.copies.append(copy)

    def finish(self):
        for copy in self.copies:
            copy.wait_send()


def on_ring(way, far, sub):
    return far < 4 or (way == 1) == (sub == 1)


def towards(way, by):
    return by if way == 0 else -by


RING_SEMS = [dma(2, 4, 3), dma(2, 4, 3), dma(9), dma(9)]


def mix_gather(ref, at, half, sems, hook=lambda step: None):
    ring_send, ring_recv, x_send, x_recv = sems
    dp, tensor, x_hi, z = places()
    partner = (dp, (1 - x_hi) * NZ + z)
    nexts = tuple((dp, x_hi * NZ + turn(z, by, NZ)) for by in (1, -1))
    sent = Sent()

    def view(zz, sub):
        plane = x_hi if sub < 2 else 1 - x_hi
        return ref.at[at(zz, plane), pl.ds((sub % 2) * half, half)]

    def ring(way, far, sub, hops):
        block = view(turn(z, -towards(way, hops), NZ), sub)
        sems = ring_send.at[way, far - 1, sub], ring_recv.at[way, far - 1, sub]
        return remote(block, block, *sems, nexts[way])

    def cross(zz, sub, slot):
        block = view(zz, sub)
        return remote(block, block, x_send.at[slot], x_recv.at[slot], partner)

    def slot(way, far):
        return 1 + far + 3 * way if way == 0 else 4 + far

    sent.start(cross(z, 0, 0))
    for sub in range(2):
        for way in range(2):
            sent.start(ring(way, 1, sub, 0))
    sent.start(cross(z, 1, 1))
    hook(0)
    cross(z, 2, 0).wait_recv()
    for way in range(2):
        sent.start(ring(way, 1, 2, 0))
    for far in range(2, 5):
        hook(far - 1)
        for sub in range(3):
            for way in range(2):
                ring(way, far - 1, sub, far - 1).wait_recv()
                if on_ring(way, far, sub):
                    sent.start(ring(way, far, sub, far - 1))
                if sub == 1:
                    origin = turn(z, -towards(way, far - 1), NZ)
                    sent.start(cross(origin, 1, slot(way, far - 1)))
    ring(1, 4, 1, 4).wait_recv()
    sent.start(cross(turn(z, 4, NZ), 1, slot(1, 4)))
    for sub in (0, 2):
        ring(0, 4, sub, 4).wait_recv()
    cross(z, 3, 1).wait_recv()
    for way in range(2):
        for far in range(1, 4 + way):
            cross(turn(z, -towards(way, far), NZ), 3, slot(way, far)).wait_recv()
    sent.finish()


def scatter_scratch(half, width):
    return [
        pltpu.VMEM((2, 4, 3, half, width), BF16),
        pltpu.VMEM((2, 4, 3, half, width), BF16),
        pltpu.VMEM((8, half, width), BF16),
        pltpu.VMEM((half, width), BF16),
        pltpu.VMEM((half, width), BF16),
        dma(2, 4, 3),
        dma(2, 4, 3),
        dma(9),
        dma(9),
    ]


def mix_scatter(part, make, scratch):
    sbuf, rbuf, xbuf, xlast, xgot, ring_send, ring_recv, x_send, x_recv = scratch
    half = sbuf.shape[3]
    dp, tensor, x_hi, z = places()
    partner = (dp, (1 - x_hi) * NZ + z)
    nexts = tuple((dp, x_hi * NZ + turn(z, by, NZ)) for by in (1, -1))
    sent = Sent()

    def view(zz, sub):
        plane = x_hi if sub < 2 else 1 - x_hi
        return part.at[zz * 2 + plane, pl.ds((sub % 2) * half, half)]

    def slot(way, far):
        return 7 if far == 4 else 1 + 3 * way + far - 1

    def cross(zz, at):
        return remote(view(zz, 3), xbuf.at[at], x_send.at[at], x_recv.at[at], partner)

    def ring(way, far, sub, source):
        sems = ring_send.at[way, far - 1, sub], ring_recv.at[way, far - 1, sub]
        return remote(source, rbuf.at[way, far - 1, sub], *sems, nexts[way])

    def arrived(way, far, sub):
        ring(way, far, sub, rbuf.at[way, far - 1, sub]).wait_recv()
        return rbuf[way, far - 1, sub].astype(F32)

    def crossed(at):
        cross(z, at).wait_recv()
        return xbuf[at].astype(F32)

    def send(way, far, sub):
        source = view(turn(z, towards(way, far), NZ), sub)
        extra = []
        if far < 4 and on_ring(way, far + 1, sub):
            extra.append(arrived(way, far + 1, sub))
        if sub == 1:
            extra.append(crossed(slot(way, far)))
        if extra:
            total = source[...].astype(F32)
            for one in extra:
                total = total + one
            sbuf[way, far - 1, sub] = total.astype(BF16)
            source = sbuf.at[way, far - 1, sub]
        sent.start(ring(way, far, sub, source))

    far4 = turn(z, 4, NZ)
    make([far4])
    sent.start(cross(far4, 7))
    for sub in (0, 2):
        send(0, 4, sub)
    for far in (3, 2, 1):
        places_now = [turn(z, by, NZ) for by in (far, -far)]
        make(places_now)
        for way in range(2):
            sent.start(cross(places_now[way], slot(way, far)))
        if far == 3:
            for sub in (0, 2):
                send(1, 3, sub)
            send(1, 4, 1)
        for sub in (2, 0, 1):
            for way in range(2):
                if not (far == 3 and way == 1 and sub != 1):
                    send(way, far, sub)
    make([z])
    sent.start(cross(z, 0))

    def total(sub):
        return view(z, sub)[...].astype(F32) + arrived(0, 1, sub) + arrived(1, 1, sub)

    xlast[...] = total(2).astype(BF16)
    last = remote(xlast, xgot, x_send.at[8], x_recv.at[8], partner)
    sent.start(last)
    second = total(1) + crossed(0)
    first = total(0)
    last.wait_recv()
    first = first + xgot[...].astype(F32)
    return first, second, sent


def rms(values):
    return values * lax.rsqrt(jnp.mean(values * values, axis=-1, keepdims=True) + 1e-05)


def project_body(
    tokens_ref,
    gain_ref,
    cos_ref,
    sin_ref,
    wq_ref,
    wk_ref,
    wv_ref,
    student_ref,
    s_gate_ref,
    s_up_ref,
    s_down_ref,
    query_ref,
    pair_ref,
    my_tokens_ref,
    part_ref,
    normed_t_ref,
    hidden_t_ref,
    gate_ref,
    up_ref,
    blocks,
    normed,
    weights,
    *sems,
):
    dp, tensor, x_hi, z = places()
    rows = tokens_ref.shape[0]
    own = rows // (2 * NZ)
    blocks[tensor] = tokens_ref[...]
    greet(
        [
            (dp, (1 - x_hi) * NZ + z),
            (dp, x_hi * NZ + turn(z, 1, NZ)),
            (dp, x_hi * NZ + turn(z, -1, NZ)),
        ]
    )

    def student(step):
        at = pl.ds(step * 128, 128)
        values = rms(student_ref[at, :].astype(F32))
        normed_t_ref[:, at] = values.T.astype(BF16)
        values = values.astype(BF16)
        gate = jnp.dot(values, s_gate_ref[...], preferred_element_type=F32)
        up = jnp.dot(values, s_up_ref[...], preferred_element_type=F32)
        gate_ref[at, :] = gate
        up_ref[at, :] = up
        hidden = gate * jax.nn.sigmoid(gate) * up
        hidden_t_ref[:, at] = hidden.T.astype(BF16)
        out = jnp.dot(hidden.astype(BF16), s_down_ref[...], preferred_element_type=F32)
        for index in range(128 // own):
            block = out[index * own : (index + 1) * own].astype(BF16)
            part_ref[index % 2, step * (64 // own) + index // 2] = block

    def hook(step):
        if step == 0:
            weights[:, :HD] = wq_ref[...]
            weights[:, HD : 2 * HD] = wk_ref[...]
            weights[:, 2 * HD :] = wv_ref[...]
        student(step)

    mix_gather(blocks, lambda zz, plane: plane * NZ + zz, rows // 2, sems, hook)
    my_rows = pl.multiple_of((z * 2 + x_hi) * own, own)
    for index in range(2 * NZ):
        my_tokens_ref[:, index * HD : (index + 1) * HD] = blocks[index, pl.ds(my_rows, own)]
    tile = 128

    @pl.loop(0, rows // tile)
    def _(step):
        at = pl.ds(pl.multiple_of(step * tile, tile), tile)
        square = jnp.zeros((tile, HD), F32)
        for index in range(2 * NZ):
            value = blocks[index, at].astype(F32)
            square = square + value * value
        mean = jnp.sum(square, axis=1, keepdims=True) / (2 * NZ * HD)
        scale = lax.rsqrt(mean + 1e-05)
        for index in range(2 * NZ):
            lanes = slice(index * HD, (index + 1) * HD)
            value = blocks[index, at].astype(F32) * scale * gain_ref[:, lanes]
            normed[at, lanes] = value.astype(BF16)

    tile = 256

    @pl.loop(0, rows // tile)
    def _(step):
        at = pl.ds(pl.multiple_of(step * tile, tile), tile)
        out = jnp.dot(normed[at, :], weights[...], preferred_element_type=F32)
        cosine, sine = cos_ref[at, :], sin_ref[at, :]

        def rotary(values):
            return (values * cosine + pltpu.roll(values, HD // 2, 1) * sine).astype(BF16)

        query_ref[at, :] = rotary(out[:, :HD])
        pair_ref[0, at, :] = rotary(out[:, HD : 2 * HD])
        pair_ref[1, at, :] = out[:, 2 * HD :].astype(BF16)


def exchange_body(
    pair_ref,
    w_out_ref,
    part_ref,
    out_ref,
    wide_ref,
    sum_ref,
    x_got,
    z_out,
    z_in,
    k_x_send,
    k_x_recv,
    k_y_send,
    k_y_recv,
    k_c_send,
    k_c_recv,
    w_send,
    w_recv,
    wc_send,
    wc_recv,
    s_x_send,
    s_x_recv,
    s_z_send,
    s_z_recv,
):
    dp, tensor, x_hi, z = places()
    x_lo, y, core = dp // (2 * NY), lax.rem(dp // 2, NY), lax.rem(dp, 2)

    def index(xx, yy, cc):
        return xx * 2 * NY + yy * 2 + cc

    def at(yy, half, cc):
        return index(x_lo if half == 0 else 1 - x_lo, yy, cc)

    k_partner = (index(1 - x_lo, y, core), tensor)
    sibling = (index(x_lo, y, 1 - core), tensor)
    y_nexts = tuple((index(x_lo, turn(y, by, NY), core), tensor) for by in (1, -1))
    z_peers = [(dp, x_hi * NZ + turn(z, by, NZ)) for by in range(1, NZ)]
    z_nexts = (z_peers[0], z_peers[-1])
    s_partner = (dp, (1 - x_hi) * NZ + z)
    out_ref[at(y, 0, core)] = pair_ref[...]
    wide_ref[z] = w_out_ref[...]
    greet([k_partner, sibling, s_partner, *y_nexts, *z_peers])
    sent = Sent()
    deep = w_out_ref.shape[0] // 4

    def share(by, half, slot):
        block = out_ref.at[at(turn(y, by, NY), half, core)]
        sent.start(remote(block, block, k_c_send.at[slot], k_c_recv.at[slot], sibling))

    def k_copy(way, far, half, hops):
        block = out_ref.at[at(turn(y, -towards(way, hops), NY), half, core)]
        sems = k_y_send.at[way, far - 1, half], k_y_recv.at[way, far - 1, half]
        return remote(block, block, *sems, y_nexts[way])

    def w_copy(way, far, sub, hops):
        first = pl.multiple_of(core * 2 * deep + sub * deep, deep)
        block = wide_ref.at[turn(z, -towards(way, hops), NZ), pl.ds(first, deep)]
        sems = w_send.at[way, far - 1, sub], w_recv.at[way, far - 1, sub]
        return remote(block, block, *sems, z_nexts[way])

    def w_share(by, slot, cc):
        first = pl.multiple_of(cc * 2 * deep, 2 * deep)
        block = wide_ref.at[turn(z, by, NZ), pl.ds(first, 2 * deep)]
        return remote(block, block, wc_send.at[slot], wc_recv.at[slot], sibling)

    def w_forward(far, sub):
        for way in range(2):
            if far < 4 or sub == way:
                w_copy(way, far, sub, far).wait_recv()
            if far < 3 or (far == 3 and sub == way):
                sent.start(w_copy(way, far + 1, sub, far))

    own = out_ref.at[at(y, 0, core)]
    other = out_ref.at[at(y, 1, core)]
    sent.start(remote(own, own, k_x_send, k_x_recv, k_partner))
    for way in range(2):
        sent.start(k_copy(way, 1, 0, 0))
    for sub in range(2):
        for way in range(2):
            sent.start(w_copy(way, 1, sub, 0))
    s_cross = remote(part_ref.at[1 - x_hi], x_got, s_x_send, s_x_recv, s_partner)
    sent.start(s_cross)
    share(0, 0, 0)

    w_forward(1, 0)
    remote(other, other, k_x_send, k_x_recv, k_partner).wait_recv()
    for way in range(2):
        sent.start(k_copy(way, 1, 1, 0))
    share(0, 1, 1)
    w_forward(1, 1)
    for way in range(2):
        sent.start(w_share(towards(way, -1), way, core))
    s_cross.wait_recv()
    z_out[...] = (part_ref[x_hi].astype(F32) + x_got[...].astype(F32)).astype(BF16)
    for by in range(1, NZ):
        sent.start(
            remote(
                z_out.at[turn(z, by, NZ)],
                z_in.at[by - 1],
                s_z_send.at[by - 1],
                s_z_recv.at[by - 1],
                z_peers[by - 1],
            )
        )

    def k_arrivals(half):
        for way in range(2):
            k_copy(way, 1, half, 1).wait_recv()
            if half == way:
                sent.start(k_copy(way, 2, half, 1))
            share(towards(way, -1), half, 2 + 2 * half + way)

    k_arrivals(0)
    w_forward(2, 0)
    w_forward(2, 1)
    for way in range(2):
        sent.start(w_share(towards(way, -2), 2 + way, core))
    k_arrivals(1)
    w_forward(3, 0)
    w_forward(3, 1)
    for way in range(2):
        sent.start(w_share(towards(way, -3), 4 + way, core))
    for way in range(2):
        k_copy(way, 2, way, 2).wait_recv()
        share(2, way, 6 + way)
    total = z_out[z].astype(F32)
    for by in range(1, NZ):
        got = z_in.at[by - 1]
        remote(got, got, s_z_send.at[by - 1], s_z_recv.at[by - 1], z_peers[by - 1]).wait_recv()
        total = total + z_in[by - 1].astype(F32)
    sum_ref[...] = total
    for sub in range(2):
        w_forward(4, sub)
    sent.start(w_share(4, 6, core))
    for slot, (by, half) in enumerate(
        [(0, 0), (0, 1), (-1, 0), (1, 0), (-1, 1), (1, 1), (2, 0), (2, 1)]
    ):
        block = out_ref.at[at(turn(y, by, NY), half, 1 - core)]
        remote(block, block, k_c_send.at[slot], k_c_recv.at[slot], sibling).wait_recv()
    for slot, by in enumerate([-1, 1, -2, 2, -3, 3, 4]):
        w_share(by, slot, 1 - core).wait_recv()
    sent.finish()


def starts_at(begins, position):
    found = jnp.zeros_like(position)
    for begin in begins:
        found = jnp.where(begin <= position, jnp.maximum(found, begin), found)
    return found


def attention_body(tile, begin_ref, query_ref, pair_ref, out_ref):
    rows = query_ref.shape[0]
    span = pair_ref.shape[2]
    mine = begin_ref[8]
    factor = HD ** (-0.5) * 1.4426950408889634
    begins = [begin_ref[index] for index in range(8)]
    tiles = rows // tile
    queries = [query_ref[index * tile : (index + 1) * tile, :] for index in range(tiles)]
    positions = [
        mine * rows + index * tile + lax.broadcasted_iota(jnp.int32, (tile, 1), 0)
        for index in range(tiles)
    ]
    starts = [starts_at(begins, position) for position in positions]
    first = starts_at(begins, mine * rows)
    last = starts_at(begins, mine * rows + rows - 1)
    low = first // span
    inner = jnp.minimum((last + span - 1) // span, mine)

    def step(masked, j, carries):
        found = []
        for query, position, start, (peak, denom, accum) in zip(
            queries, positions, starts, carries, strict=True
        ):
            scores = lax.dot_general(
                query, pair_ref[j, 0], (((1,), (1,)), ((), ())), preferred_element_type=F32
            )
            if masked:
                column = j * span + lax.broadcasted_iota(jnp.int32, (tile, span), 1)
                allowed = (column >= start) & (column <= position)
                scores = jnp.where(allowed, scores, -1e30)
            new_peak = jnp.maximum(peak, jnp.max(scores, axis=1, keepdims=True))
            weights = jnp.exp2((scores - new_peak) * factor)
            if masked:
                weights = jnp.where(allowed, weights, 0.0)
            scale = jnp.exp2((peak - new_peak) * factor)
            denom = denom * scale + jnp.sum(weights, axis=1, keepdims=True)
            accum = accum * scale + jnp.dot(
                weights.astype(BF16), pair_ref[j, 1], preferred_element_type=F32
            )
            found.append((new_peak, denom, accum))
        return tuple(found)

    state = tuple(
        (
            jnp.full((tile, 1), -1e30, F32),
            jnp.zeros((tile, 1), F32),
            jnp.zeros((tile, HD), F32),
        )
        for _ in range(tiles)
    )
    state = lax.fori_loop(low, inner, functools.partial(step, True), state)
    state = lax.fori_loop(inner, mine, functools.partial(step, False), state)
    state = step(True, mine, state)
    for index, (_, denom, accum) in enumerate(state):
        out_ref[index * tile : (index + 1) * tile, :] = (accum / denom).astype(BF16)


def attention(begins, query, pairs):
    return pl.pallas_call(
        functools.partial(attention_body, 256),
        out_shape=jax.ShapeDtypeStruct(query.shape, BF16),
        in_specs=[SM, VM, VM],
        out_specs=VM,
        compiler_params=pltpu.CompilerParams(vmem_limit_bytes=LIMIT),
        name="attention",
    )(begins, query, pairs)


def layer_body(
    total_rows,
    attended_ref,
    wide_ref,
    my_tokens_ref,
    gain_ref,
    w_gate_hbm,
    w_up_hbm,
    w_down_hbm,
    projector_hbm,
    student_ref,
    student_sum_ref,
    teacher_ref,
    scaled_ref,
    w_gate,
    w_up,
    w_down,
    projector,
    load_sem,
    heads,
    a_send,
    a_recv,
    out_send,
    out_recv,
    o_send,
    o_recv,
    partial,
    blocks,
    hidden,
    parts,
    *rest,
):
    gather_sems, scatter = rest[:4], rest[4:]
    dp, tensor, x_hi, z = places()
    own, width = my_tokens_ref.shape
    pair = 2 * own
    partner = (dp, (1 - x_hi) * NZ + z)
    z_peers = [(dp, x_hi * NZ + turn(z, by, NZ)) for by in range(1, NZ)]
    loads = []
    for index, (far, near) in enumerate(
        (
            (w_gate_hbm, w_gate),
            (w_up_hbm, w_up),
            (w_down_hbm, w_down),
            (projector_hbm, projector),
        )
    ):
        load = pltpu.make_async_copy(far, near, load_sem.at[index])
        load.start()
        loads.append(load)
    greet([partner, *z_peers])
    sent = Sent()

    def rows_of(zz):
        return pl.ds(pl.multiple_of(zz * pair, pair), pair)

    for by in range(1, NZ):
        sent.start(
            remote(
                attended_ref.at[rows_of(turn(z, by, NZ))],
                heads.at[z],
                a_send.at[by - 1],
                a_recv.at[by - 1],
                z_peers[by - 1],
            )
        )
    heads[z] = attended_ref[rows_of(z), :]
    for by in range(1, NZ):
        block = heads.at[turn(z, -by, NZ)]
        remote(block, block, a_send.at[by - 1], a_recv.at[by - 1], z_peers[by - 1]).wait_recv()
    chunk = 512
    joined = jnp.concatenate([heads[index] for index in range(NZ)], axis=1)
    depth = joined.shape[1]

    @pl.loop(0, width // chunk)
    def _(step):
        at = pl.ds(pl.multiple_of(step * chunk, chunk), chunk)
        partial[:, at] = jnp.dot(
            joined,
            wide_ref[:, :, at].reshape(depth, chunk),
            preferred_element_type=F32,
        )

    def half_rows(plane):
        return pl.ds(pl.multiple_of(plane * own, own), own)

    out_send[...] = partial[half_rows(1 - x_hi), :].astype(BF16)
    swap = remote(out_send, out_recv, o_send, o_recv, partner)
    sent.start(swap)
    mine = partial[half_rows(x_hi), :] + my_tokens_ref[...].astype(F32)
    swap.wait_recv()
    mixed = (mine + out_recv[...].astype(F32)).astype(BF16)
    blocks[z * 2 + x_hi] = (rms(mixed.astype(F32)) * gain_ref[...]).astype(BF16)

    mix_gather(blocks, lambda zz, plane: zz * 2 + plane, own // 2, gather_sems)
    loads[0].wait()
    loads[1].wait()
    group = 8

    @pl.loop(0, 2 * NZ // group)
    def _(step):
        value = blocks[pl.ds(step * group, group)].reshape(group * own, width)
        gate = jnp.dot(value, w_gate[...], preferred_element_type=F32)
        up = jnp.dot(value, w_up[...], preferred_element_type=F32)
        found = (gate * jax.nn.sigmoid(gate) * up).astype(BF16)
        hidden[pl.ds(step * (group // 2), group // 2)] = found.reshape(group // 2, pair, -1)

    loads[2].wait()

    def make(zs):
        value = jnp.concatenate([hidden[zz] for zz in zs], axis=0)

        @pl.loop(0, width // chunk)
        def _(step):
            at = pl.ds(pl.multiple_of(step * chunk, chunk), chunk)
            out = jnp.dot(value, w_down[:, at], preferred_element_type=F32).astype(BF16)
            for index, zz in enumerate(zs):
                for plane in range(2):
                    first = index * pair + plane * own
                    parts[zz * 2 + plane, :, at] = out[first : first + own]

    first, second, more = mix_scatter(parts, make, scatter)
    teacher = mixed.astype(F32) + jnp.concatenate([first, second], axis=0)
    teacher = teacher.astype(BF16)
    teacher_ref[...] = teacher
    loads[3].wait()
    target = jnp.dot(teacher, projector[...], preferred_element_type=F32)
    difference = student_ref[...].astype(F32) + student_sum_ref[...] - target
    scaled_ref[...] = (difference * total_rows ** (-0.5)).astype(BF16)
    sent.finish()
    more.finish()


def student_body(
    scaled_ref,
    teacher_ref,
    normed_t_ref,
    hidden_t_ref,
    gate_ref,
    up_ref,
    s_down_ref,
    columns_ref,
    sums_ref,
    error_ref,
    gathered,
    parts,
    inbox,
    send_sem,
    recv_sem,
    x_send,
    x_recv,
    t_send,
    t_recv,
    send1,
    recv1,
    send2,
    recv2,
):
    dp, tensor, x_hi, z = places()
    size = 2 * NZ
    row = z * 2 + x_hi
    own = scaled_ref.shape[0]
    partner = (dp, (1 - x_hi) * NZ + z)
    nexts = tuple((dp, x_hi * NZ + turn(z, by, NZ)) for by in (1, -1))
    t_peers = [turn(tensor, by, size) for by in range(1, size)]
    d_peers = [turn(dp, by, size) for by in range(1, size)]
    gathered[row] = scaled_ref[...]
    greet([(dp, peer) for peer in t_peers] + [(peer, tensor) for peer in d_peers])
    sent = Sent()

    def view(zz, half):
        return gathered.at[zz * 2 + (x_hi if half == 0 else 1 - x_hi)]

    def ring(way, far, half, hops):
        block = view(turn(z, -towards(way, hops), NZ), half)
        sems = send_sem.at[way, far - 1, half], recv_sem.at[way, far - 1, half]
        return remote(block, block, *sems, nexts[way])

    sent.start(remote(view(z, 0), view(z, 0), x_send, x_recv, partner))
    for way in range(2):
        sent.start(ring(way, 1, 0, 0))
    remote(view(z, 1), view(z, 1), x_send, x_recv, partner).wait_recv()
    for way in range(2):
        sent.start(ring(way, 1, 1, 0))
    for by, peer in enumerate(t_peers):
        sent.start(
            remote(
                teacher_ref.at[:, pl.ds(pl.multiple_of(peer * HD, HD), HD)],
                columns_ref.at[row],
                t_send.at[by],
                t_recv.at[by],
                (dp, peer),
            )
        )
    columns_ref[row] = teacher_ref[:, pl.ds(pl.multiple_of(tensor * HD, HD), HD)]
    for far in range(2, 5):
        for half in range(2):
            for way in range(2):
                ring(way, far - 1, half, far - 1).wait_recv()
                if far < 4 or half == way:
                    sent.start(ring(way, far, half, far - 1))
    for way in range(2):
        ring(way, 4, way, 4).wait_recv()
    scaled = gathered[...].reshape(size * own, -1)
    gate, up = gate_ref[...], up_ref[...]
    sigmoid = jax.nn.sigmoid(gate)
    grad_hidden = lax.dot_general(
        scaled, s_down_ref[...], (((1,), (1,)), ((), ())), preferred_element_type=F32
    )
    grad_up = (grad_hidden * gate * sigmoid).astype(BF16)
    grad_gate = (grad_hidden * up * sigmoid * (1.0 + gate * (1.0 - sigmoid))).astype(BF16)
    both = jnp.concatenate([grad_gate, grad_up], axis=1)
    both = jnp.dot(normed_t_ref[...], both, preferred_element_type=F32).astype(BF16)
    down = jnp.dot(hidden_t_ref[...], scaled, preferred_element_type=F32).astype(BF16)
    units = gate.shape[1]
    parts[:, :own] = both[:, :units].reshape(size, own, units)
    parts[:, own : 2 * own] = both[:, units:].reshape(size, own, units)
    down = jnp.concatenate([down[:, at : at + HD] for at in range(0, down.shape[1], HD)], axis=0)
    parts[:, 2 * own : 3 * own] = down.reshape(size, own, HD)
    squares = scaled.astype(F32)
    squares = jnp.sum((squares * squares).reshape(-1, 8, scaled.shape[1]), axis=0)
    squares = sum(squares[:, at : at + HD] for at in range(0, scaled.shape[1], HD))
    high = squares.astype(BF16)
    low = (squares - high.astype(F32)).astype(BF16)
    both = jnp.concatenate([high, low], axis=0)
    parts[:, 3 * own :] = jnp.broadcast_to(both[None], (size,) + both.shape)

    def origin(by):
        return turn(dp, -(by + 1), size)

    inbox[dp] = parts[dp]
    for by, peer in enumerate(d_peers):
        sent.start(
            remote(parts.at[peer], inbox.at[dp], send1.at[by], recv1.at[by], (peer, tensor))
        )
    for by, peer in enumerate(d_peers):
        block = inbox.at[origin(by)]
        remote(block, block, send1.at[by], recv1.at[by], (peer, tensor)).wait_recv()
    total = inbox[0].astype(F32)
    for index in range(1, size):
        total = total + inbox[index].astype(F32)
    sums_ref[dp] = total[: 3 * own].astype(BF16)
    error_ref[...] = total[3 * own : 3 * own + 8] + total[3 * own + 8 :]
    for by, peer in enumerate(d_peers):
        block = sums_ref.at[dp]
        sent.start(remote(block, block, send2.at[by], recv2.at[by], (peer, tensor)))
    for by, peer in enumerate(t_peers):
        source = turn(tensor, -(by + 1), size)
        block = columns_ref.at[lax.rem(source, NZ) * 2 + source // NZ]
        remote(block, block, t_send.at[by], t_recv.at[by], (dp, peer)).wait_recv()
    for by, peer in enumerate(d_peers):
        block = sums_ref.at[origin(by)]
        remote(block, block, send2.at[by], recv2.at[by], (peer, tensor)).wait_recv()
    sent.finish()


def finish_body(columns_ref, sums_ref, squares_ref, teacher_ref, gate_ref, up_ref, down_ref, error_ref):
    rows, width = teacher_ref.shape
    own = rows // (2 * NZ)
    teacher_ref[...] = columns_ref[...].reshape(rows, width)
    sums = sums_ref[...].astype(F32)
    gate_ref[...] = sums[:, :own].reshape(-1, width)
    up_ref[...] = sums[:, own : 2 * own].reshape(-1, width)
    down = sums[:, 2 * own :].reshape(-1, width)
    for index in range(down.shape[0] // width):
        lanes = slice(index * width, (index + 1) * width)
        down_ref[:, lanes] = down[lanes]
    total = jnp.sum(jnp.sum(squares_ref[...], axis=0, keepdims=True), axis=1, keepdims=True)
    error_ref[...] = total / down_ref.shape[1]


def finish(columns, sums, squares):
    own, units = columns.shape[1:]
    rows = 2 * NZ * own
    shapes = (
        ((rows, units), BF16),
        ((rows, units), F32),
        ((rows, units), F32),
        ((units, rows), F32),
        ((1, 1), F32),
    )
    return pl.pallas_call(
        finish_body,
        out_shape=tuple(jax.ShapeDtypeStruct(shape, kind) for shape, kind in shapes),
        in_specs=[VM] * 3,
        out_specs=(VM,) * 5,
        compiler_params=pltpu.CompilerParams(vmem_limit_bytes=LIMIT),
        name="finish",
    )(columns, sums, squares)


def frequencies(head_dim):
    indices = jnp.arange(head_dim // 2).astype(F32)
    return jnp.exp(-jnp.log(500000.0) * 2.0 * indices / head_dim)


def local(
    tokens,
    series_ids,
    offsets,
    norm_gain,
    mlp_gain,
    w_query,
    w_key,
    w_value,
    w_out,
    w_gate,
    w_up,
    w_down,
    projector,
    student_in,
    s_gate,
    s_up,
    s_down,
):
    rows = tokens.shape[0]
    size = 2 * NZ
    own = rows // size
    width = projector.shape[0]
    narrow = student_in.shape[1]
    units = s_gate.shape[1]
    ff = w_gate.shape[1]
    dp, tensor, x_hi, z = places()
    my_rows = (z * 2 + x_hi) * own

    angles = offsets.astype(F32)[:, None] * frequencies(HD)[None, :]
    cosine, sine = jnp.cos(angles), jnp.sin(angles)
    cosine = jnp.concatenate([cosine, cosine], axis=1)
    sine = jnp.concatenate([-sine, sine], axis=1)
    series = jnp.arange(8, dtype=jnp.int32)
    begins = jnp.sum((series_ids[None, :] < series[:, None]).astype(jnp.int32), axis=1)
    begins = jnp.concatenate([begins, dp[None].astype(jnp.int32)])
    my_student = lax.dynamic_slice_in_dim(student_in, my_rows, own, 0)

    query, pair, my_tokens, part, normed_t, hidden_t, gate, up = call(
        project_body,
        "project",
        1,
        (
            tokens,
            norm_gain[None],
            cosine,
            sine,
            w_query,
            w_key,
            w_value,
            student_in,
            s_gate,
            s_up,
            s_down,
        ),
        (
            ((rows, HD), BF16),
            ((2, rows, HD), BF16),
            ((own, width), BF16),
            ((2, NZ, own, narrow), BF16),
            ((narrow, rows), BF16),
            ((units, rows), BF16),
            ((rows, units), F32),
            ((rows, units), F32),
        ),
        [
            pltpu.VMEM((size, rows, HD), BF16),
            pltpu.VMEM((rows, width), BF16),
            pltpu.VMEM((width, 3 * HD), BF16),
            *RING_SEMS,
        ],
    )
    pairs, wide, student_sum = call(
        exchange_body,
        "exchange",
        2,
        (pair, w_out, part),
        (
            ((4 * NY, 2, rows, HD), BF16),
            ((NZ,) + w_out.shape, BF16),
            ((own, narrow), F32),
        ),
        [
            pltpu.VMEM((NZ, own, narrow), BF16),
            pltpu.VMEM((NZ, own, narrow), BF16),
            pltpu.VMEM((NZ - 1, own, narrow), BF16),
            pltpu.SemaphoreType.DMA,
            pltpu.SemaphoreType.DMA,
            dma(2, 2, 2),
            dma(2, 2, 2),
            dma(8),
            dma(8),
            dma(2, 4, 2),
            dma(2, 4, 2),
            dma(7),
            dma(7),
            pltpu.SemaphoreType.DMA,
            pltpu.SemaphoreType.DMA,
            dma(7),
            dma(7),
        ],
    )
    attended = attention(begins, query, pairs)
    teacher, scaled = call(
        functools.partial(layer_body, rows * lax.axis_size("dp")),
        "layer",
        3,
        (
            attended,
            wide,
            my_tokens,
            mlp_gain[None],
            w_gate,
            w_up,
            w_down,
            projector,
            my_student,
            student_sum,
        ),
        (((own, width), BF16), ((own, narrow), BF16)),
        [
            pltpu.VMEM(w_gate.shape, BF16),
            pltpu.VMEM(w_up.shape, BF16),
            pltpu.VMEM(w_down.shape, BF16),
            pltpu.VMEM(projector.shape, BF16),
            dma(4),
            pltpu.VMEM((NZ, 2 * own, HD), BF16),
            dma(7),
            dma(7),
            pltpu.VMEM((own, width), BF16),
            pltpu.VMEM((own, width), BF16),
            pltpu.SemaphoreType.DMA,
            pltpu.SemaphoreType.DMA,
            pltpu.VMEM((2 * own, width), F32),
            pltpu.VMEM((size, own, width), BF16),
            pltpu.VMEM((NZ, 2 * own, ff), BF16),
            pltpu.VMEM((size, own, width), BF16),
            *RING_SEMS,
            *scatter_scratch(own // 2, width),
        ],
        [VM] * 4 + [pl.BlockSpec(memory_space=pl.ANY)] * 4 + [VM] * 2,
    )
    columns, sums, squares = call(
        student_body,
        "student",
        4,
        (scaled, teacher, normed_t, hidden_t, gate, up, s_down),
        (
            ((size, own, HD), BF16),
            ((size, 3 * own, units), BF16),
            ((8, HD), F32),
        ),
        [
            pltpu.VMEM((size, own, narrow), BF16),
            pltpu.VMEM((size, 3 * own + 16, units), BF16),
            pltpu.VMEM((size, 3 * own + 16, units), BF16),
            dma(2, 4, 2),
            dma(2, 4, 2),
            pltpu.SemaphoreType.DMA,
            pltpu.SemaphoreType.DMA,
            dma(size - 1),
            dma(size - 1),
            dma(size - 1),
            dma(size - 1),
            dma(size - 1),
            dma(size - 1),
        ],
    )
    teacher_out, grad_gate, grad_up, grad_down, error = finish(columns, sums, squares)
    return (teacher_out, grad_gate, grad_up, grad_down, error.reshape(()))


def solution(mesh):
    in_specs = (
        P("dp", "tensor"),
        P(),
        P("dp"),
        P(),
        P(),
        P(None, "tensor"),
        P(None, "tensor"),
        P(None, "tensor"),
        P("tensor", None),
        P(None, "tensor"),
        P(None, "tensor"),
        P("tensor", None),
        P(),
        P("dp", None),
        P(None, "tensor"),
        P(None, "tensor"),
        P("tensor", None),
    )
    out_specs = (P("dp", "tensor"), P(None, "tensor"), P(None, "tensor"), P("tensor", None), P())
    return jax.shard_map(local, mesh=mesh, in_specs=in_specs, out_specs=out_specs, check_vma=False)
```

time: 1090 us -> 206 us (0.19)
  waiting for transfers between devices: 958 us -> 0 us
  Pallas kernels: 0 us -> 199 us
  matrix products: 44.3 us -> 0 us
  blocking collectives: 30.9 us -> 0 us
  other arithmetic: 20.5 us -> 4.21 us
  between operations: 15.8 us -> 0.68 us
  local copies, waits for them, and re-layouts: 16.3 us -> 1.37 us
    unnamed x11 -> x0, waiting for transfers between devices: 395 us -> none
    all_gather x5 -> x0, waiting for transfers between devices: 321 us -> none  [the longest x1 92.6 us: local(): teacher_full = lax.all_gather(teacher_out, 'tensor', axis=1, tiled=True)]
    psum x2 -> x0, waiting for transfers between devices: 241 us -> none  [the longest x1 150 us: local(): lax.psum(student_part.astype(jnp.bfloat16), 'tensor').astype(jnp.float32)]
    pallas_call x0 -> x6, Pallas kernels: none -> 199 us  [the longest x4 192 us: call(): pl.pallas_call(body, out_shape=tuple((jax.ShapeDtypeStruct(shape, kind) f...]
    dot_general x15 -> x0, matrix products: 44.3 us -> none  [the longest x1 14 us: local(): partial_out = jnp.dot(attended, w_out, preferred_element_type=jnp.float32)]
    psum x1 -> x0, blocking collectives: 30.9 us -> none  [local(): lax.psum(square_sum.astype(jnp.bfloat16), 'dp').astype(jnp.float32)]
    unnamed x34 -> x0, local copies, waits for them, and re-layouts: 16.3 us -> none
  transfers between devices with their start and end apart: 9 -> 0, of which waited for: 9 -> 0; matrix products, arithmetic and copies ran while one was open for 2% -> 0% of each run, Pallas kernels for 0% -> 0%
where the time goes in v2:
time: 206 us
  Pallas kernels  199 us (97%)
  other arithmetic  4.21 us (2%)
    pallas_call x4, Pallas kernels, call(): pl.pallas_call(body, out_shape=tuple((jax.ShapeDtypeStruct(shape, kind) f...  192 us
    pallas_call x1, Pallas kernels, attention(): pl.pallas_call(functools.partial(attention_body, 256), out_shape=jax.Shap...  5.46 us

profile of v2, /device:TPU:1, one launch (start us, length us, event | category | flops | bytes accessed | tf_op | source)
XLA Modules:
  0.0 205.7 jit_solution(14372019270134451500)
XLA Ops:
  0.6 0.9 convert_reduce_fusion
  1.6 0.6 pad_add_fusion.begin_ref
  2.2 0.7 convert_element_type.14
  2.9 1.0 fusion
  3.9 1.0 pad_maximum_fusion
  4.9 32.4 %project.1 = (bf16[512,128]{1,0:T(8,128)(2,1)}, bf16[2,512,128]{2,1,0:T(8,128)(2,1)}, bf16[32,2048]{1,0:T(8,128)(2,1)}, bf16[2,8,32,512]{3,2,1,0:T(8,128)(2,1)},...) custom-call(bf16[512,128]{1,0:T(8,128)(2,1)} %tokens_ref.1, ...), custom_call_target="tpu_custom_call" | custom-call | tf_op jit(solution)/shard_map/project/pallas_call | solution.py:60
  37.3 42.4 %exchange.1 = (bf16[16,2,512,128]{3,2,1,0:T(8,128)(2,1)}, bf16[8,128,2048]{2,1,0:T(8,128)(2,1)}, f32[32,512]{1,0:T(8,128)}) custom-call(bf16[2,512,128]{2,1,0:T(8,128)(2,1)} %get-tuple-element.27.pair_ref, bf16[128,2048]{1,0:T(8,128)(2,1)} %w_out_ref.1, bf16[2,8,32,512]{3,2,1,0:T(8,128)(2,1)} %get-tuple-element.28.part_ref), custom_call_target="tpu_custom_call" | custom-call | tf_op jit(solution)/shard_map/exchange/pallas_call | solution.py:60
  79.7 5.5 %attention.1.attended_ref = bf16[512,128]{1,0:T(8,128)(2,1)} custom-call(s32[9]{0:T(128)} %pad_add_fusion.begin_ref, bf16[512,128]{1,0:T(8,128)(2,1)} %get-tuple-element.26.query_ref, bf16[16,2,512,128]{3,2,1,0:T(8,128)(2,1)} %get-tuple-element.29.pair_ref), custom_call_target="tpu_custom_call" | custom-call | tf_op jit(solution)/shard_map/attention/pallas_call | solution.py:551
  85.1 1.4 constant_dynamic-slice_fusion.student_ref
  86.5 63.7 %layer.1 = (bf16[32,2048]{1,0:T(8,128)(2,1)}, bf16[32,512]{1,0:T(8,128)(2,1)}) custom-call(bf16[512,128]{1,0:T(8,128)(2,1)} %attention.1.attended_ref, bf16[8,128,2048]{2,1,0:T(8,128)(2,1)} %get-tuple-element.30.wide_ref, bf16[32,2048]{1,0:T(8,128)(2,1)} %get-tuple-element.31.my_tokens_ref, f32[1,2048]{1,0:T(1,128)} %bitcast.5, ...), custom_call_target="tpu_custom_call" | custom-call | tf_op jit(solution)/shard_map/layer/pallas_call | solution.py:60
  150.2 53.5 %student.1 = (bf16[16,32,128]{2,1,0:T(8,128)(2,1)}, bf16[16,96,128]{2,1,0:T(8,128)(2,1)}, f32[8,128]{1,0:T(8,128)}) custom-call(bf16[32,512]{1,0:T(8,128)(2,1)} %get-tuple-element.33.scaled_ref, bf16[32,2048]{1,0:T(8,128)(2,1)} %get-tuple-element.34.teacher_ref, bf16[512,512]{1,0:T(8,128)(2,1)} %get-tuple-element.35.normed_t_ref, ...), custom_call_target="tpu_custom_call" | custom-call | tf_op jit(solution)/shard_map/student/pallas_call | solution.py:60
  203.8 2.0 finish.1
  (1 shorter events, 0.0 us)

commit v3 on v2

v3 whole, which is shorter than its diff:
```python
import functools

import jax
import jax.numpy as jnp
from jax import lax
from jax.experimental import pallas as pl
from jax.experimental.pallas import tpu as pltpu
from jax.sharding import PartitionSpec as P

HD = 128
NZ = 8
NY = 4
MESH = pl.DeviceIdType.MESH
VM = pl.BlockSpec(memory_space=pltpu.VMEM)
SM = pl.BlockSpec(memory_space=pltpu.SMEM)
LIMIT = 56 * 1024 * 1024
F32 = jnp.float32
BF16 = jnp.bfloat16


def params(collective_id):
    return pltpu.CompilerParams(
        collective_id=collective_id, has_side_effects=True, vmem_limit_bytes=LIMIT
    )


def remote(src, dst, send_sem, recv_sem, device):
    return pltpu.make_async_remote_copy(
        src_ref=src,
        dst_ref=dst,
        send_sem=send_sem,
        recv_sem=recv_sem,
        device_id=device,
        device_id_type=MESH,
    )


def greet(devices, meanwhile=None):
    barrier = pltpu.get_barrier_semaphore()
    for device in devices:
        pl.semaphore_signal(barrier, inc=1, device_id=device, device_id_type=MESH)
    if meanwhile is not None:
        meanwhile()
    pl.semaphore_wait(barrier, len(devices))


def places():
    dp, tensor = lax.axis_index("dp"), lax.axis_index("tensor")
    x_hi, z = tensor // NZ, lax.rem(tensor, NZ)
    return dp, tensor, x_hi, z


def turn(z, by, size):
    return lax.rem(z + by + size, size)


def dma(*shape):
    return pltpu.SemaphoreType.DMA(shape)


def call(body, name, collective_id, inputs, outputs, scratch, specs=None):
    return pl.pallas_call(
        body,
        out_shape=tuple(jax.ShapeDtypeStruct(shape, kind) for shape, kind in outputs),
        in_specs=specs or [VM] * len(inputs),
        out_specs=tuple([VM] * len(outputs)),
        scratch_shapes=scratch,
        compiler_params=params(collective_id),
        name=name,
    )(*inputs)


class Sent:
    def __init__(self):
        self.copies = []

    def start(self, copy):
        copy.start()
        self.copies.append(copy)

    def finish(self):
        for copy in self.copies:
            copy.wait_send()


def on_ring(way, far, sub):
    return far < 4 or (way == 1) == (sub == 1)


def towards(way, by):
    return by if way == 0 else -by


RING_SEMS = [dma(2, 4, 3), dma(2, 4, 3), dma(9), dma(9)]


def mix_gather(ref, at, half, sems, hook=lambda step: None, ready=None):
    ring_send, ring_recv, x_send, x_recv = sems
    dp, tensor, x_hi, z = places()
    partner = (dp, (1 - x_hi) * NZ + z)
    nexts = tuple((dp, x_hi * NZ + turn(z, by, NZ)) for by in (1, -1))
    sent = Sent()

    def view(zz, sub):
        plane = x_hi if sub < 2 else 1 - x_hi
        return ref.at[at(zz, plane), pl.ds((sub % 2) * half, half)]

    def ring(way, far, sub, hops):
        block = view(turn(z, -towards(way, hops), NZ), sub)
        sems = ring_send.at[way, far - 1, sub], ring_recv.at[way, far - 1, sub]
        return remote(block, block, *sems, nexts[way])

    def cross(zz, sub, slot):
        block = view(zz, sub)
        return remote(block, block, x_send.at[slot], x_recv.at[slot], partner)

    def slot(way, far):
        return 1 + far + 3 * way if way == 0 else 4 + far

    def crossed(far):
        if far == 0:
            cross(z, 3, 1).wait_recv()
        for way in range(2):
            if 0 < far < 4 + way:
                cross(turn(z, -towards(way, far), NZ), 3, slot(way, far)).wait_recv()

    sent.start(cross(z, 0, 0))
    for sub in range(2):
        for way in range(2):
            sent.start(ring(way, 1, sub, 0))
    sent.start(cross(z, 1, 1))
    hook(0)
    cross(z, 2, 0).wait_recv()
    for way in range(2):
        sent.start(ring(way, 1, 2, 0))
    for far in range(2, 5):
        hook(far - 1)
        for sub in range(3):
            for way in range(2):
                ring(way, far - 1, sub, far - 1).wait_recv()
                if on_ring(way, far, sub):
                    sent.start(ring(way, far, sub, far - 1))
                if sub == 1:
                    origin = turn(z, -towards(way, far - 1), NZ)
                    sent.start(cross(origin, 1, slot(way, far - 1)))
        if far == 3:
            crossed(0)
            crossed(1)
            if ready:
                ready((0, 1))
        if far == 4:
            crossed(2)
            if ready:
                ready((2,))
    ring(1, 4, 1, 4).wait_recv()
    sent.start(cross(turn(z, 4, NZ), 1, slot(1, 4)))
    for sub in (0, 2):
        ring(0, 4, sub, 4).wait_recv()
    crossed(4)
    crossed(3)
    sent.finish()


def scatter_scratch(half, width):
    return [
        pltpu.VMEM((2, 4, 3, half, width), BF16),
        pltpu.VMEM((2, 4, 3, half, width), BF16),
        pltpu.VMEM((8, half, width), BF16),
        pltpu.VMEM((half, width), BF16),
        pltpu.VMEM((half, width), BF16),
        dma(2, 4, 3),
        dma(2, 4, 3),
        dma(9),
        dma(9),
    ]


def mix_scatter(part, make, scratch):
    sbuf, rbuf, xbuf, xlast, xgot, ring_send, ring_recv, x_send, x_recv = scratch
    half = sbuf.shape[3]
    dp, tensor, x_hi, z = places()
    partner = (dp, (1 - x_hi) * NZ + z)
    nexts = tuple((dp, x_hi * NZ + turn(z, by, NZ)) for by in (1, -1))
    sent = Sent()

    def view(zz, sub):
        plane = x_hi if sub < 2 else 1 - x_hi
        return part.at[zz * 2 + plane, pl.ds((sub % 2) * half, half)]

    def slot(way, far):
        return 7 if far == 4 else 1 + 3 * way + far - 1

    def cross(zz, at):
        return remote(view(zz, 3), xbuf.at[at], x_send.at[at], x_recv.at[at], partner)

    def ring(way, far, sub, source):
        sems = ring_send.at[way, far - 1, sub], ring_recv.at[way, far - 1, sub]
        return remote(source, rbuf.at[way, far - 1, sub], *sems, nexts[way])

    def arrived(way, far, sub):
        ring(way, far, sub, rbuf.at[way, far - 1, sub]).wait_recv()
        return rbuf[way, far - 1, sub].astype(F32)

    def crossed(at):
        cross(z, at).wait_recv()
        return xbuf[at].astype(F32)

    def send(way, far, sub):
        source = view(turn(z, towards(way, far), NZ), sub)
        extra = []
        if far < 4 and on_ring(way, far + 1, sub):
            extra.append(arrived(way, far + 1, sub))
        if sub == 1:
            extra.append(crossed(slot(way, far)))
        if extra:
            total = source[...].astype(F32)
            for one in extra:
                total = total + one
            sbuf[way, far - 1, sub] = total.astype(BF16)
            source = sbuf.at[way, far - 1, sub]
        sent.start(ring(way, far, sub, source))

    far4 = turn(z, 4, NZ)
    make([far4])
    sent.start(cross(far4, 7))
    for sub in (0, 2):
        send(0, 4, sub)
    for far in (3, 2, 1):
        places_now = [turn(z, by, NZ) for by in (far, -far)]
        make(places_now)
        for way in range(2):
            sent.start(cross(places_now[way], slot(way, far)))
        if far == 3:
            for sub in (0, 2):
                send(1, 3, sub)
            send(1, 4, 1)
        for sub in (2, 0, 1):
            for way in range(2):
                if not (far == 3 and way == 1 and sub != 1):
                    send(way, far, sub)
    make([z])
    sent.start(cross(z, 0))

    def total(sub):
        return view(z, sub)[...].astype(F32) + arrived(0, 1, sub) + arrived(1, 1, sub)

    xlast[...] = total(2).astype(BF16)
    last = remote(xlast, xgot, x_send.at[8], x_recv.at[8], partner)
    sent.start(last)
    second = total(1) + crossed(0)
    first = total(0)
    last.wait_recv()
    first = first + xgot[...].astype(F32)
    return first, second, sent


def rms(values):
    return values * lax.rsqrt(jnp.mean(values * values, axis=-1, keepdims=True) + 1e-05)


def project_body(
    tokens_ref,
    gain_ref,
    cos_ref,
    sin_ref,
    wq_ref,
    wk_ref,
    wv_ref,
    student_ref,
    s_gate_ref,
    s_up_ref,
    s_down_ref,
    query_ref,
    pair_ref,
    my_tokens_ref,
    part_ref,
    normed_t_ref,
    hidden_t_ref,
    gate_ref,
    up_ref,
    blocks,
    normed,
    weights,
    *sems,
):
    dp, tensor, x_hi, z = places()
    rows = tokens_ref.shape[0]
    own = rows // (2 * NZ)
    blocks[tensor] = tokens_ref[...]
    greet(
        [
            (dp, (1 - x_hi) * NZ + z),
            (dp, x_hi * NZ + turn(z, 1, NZ)),
            (dp, x_hi * NZ + turn(z, -1, NZ)),
        ]
    )

    def student(step):
        at = pl.ds(step * 128, 128)
        values = rms(student_ref[at, :].astype(F32))
        normed_t_ref[:, at] = values.T.astype(BF16)
        values = values.astype(BF16)
        gate = jnp.dot(values, s_gate_ref[...], preferred_element_type=F32)
        up = jnp.dot(values, s_up_ref[...], preferred_element_type=F32)
        sigmoid = jax.nn.sigmoid(gate)
        gate_ref[at, :] = up * sigmoid * (1.0 + gate * (1.0 - sigmoid))
        up_ref[at, :] = gate * sigmoid
        hidden = gate * sigmoid * up
        hidden_t_ref[:, at] = hidden.T.astype(BF16)
        out = jnp.dot(hidden.astype(BF16), s_down_ref[...], preferred_element_type=F32)
        for index in range(128 // own):
            block = out[index * own : (index + 1) * own].astype(BF16)
            part_ref[index % 2, step * (64 // own) + index // 2] = block

    def hook(step):
        if step == 0:
            weights[:, :HD] = wq_ref[...]
            weights[:, HD : 2 * HD] = wk_ref[...]
            weights[:, 2 * HD :] = wv_ref[...]
        student(step)

    mix_gather(blocks, lambda zz, plane: plane * NZ + zz, rows // 2, sems, hook)
    my_rows = pl.multiple_of((z * 2 + x_hi) * own, own)
    for index in range(2 * NZ):
        my_tokens_ref[:, index * HD : (index + 1) * HD] = blocks[index, pl.ds(my_rows, own)]
    tile = 128

    @pl.loop(0, rows // tile)
    def _(step):
        at = pl.ds(pl.multiple_of(step * tile, tile), tile)
        square = jnp.zeros((tile, HD), F32)
        for index in range(2 * NZ):
            value = blocks[index, at].astype(F32)
            square = square + value * value
        mean = jnp.sum(square, axis=1, keepdims=True) / (2 * NZ * HD)
        scale = lax.rsqrt(mean + 1e-05)
        for index in range(2 * NZ):
            lanes = slice(index * HD, (index + 1) * HD)
            value = blocks[index, at].astype(F32) * scale * gain_ref[:, lanes]
            normed[at, lanes] = value.astype(BF16)

    tile = 256

    @pl.loop(0, rows // tile)
    def _(step):
        at = pl.ds(pl.multiple_of(step * tile, tile), tile)
        out = jnp.dot(normed[at, :], weights[...], preferred_element_type=F32)
        cosine, sine = cos_ref[at, :], sin_ref[at, :]

        def rotary(values):
            return (values * cosine + pltpu.roll(values, HD // 2, 1) * sine).astype(BF16)

        query_ref[at, :] = rotary(out[:, :HD])
        pair_ref[0, at, :] = rotary(out[:, HD : 2 * HD])
        pair_ref[1, at, :] = out[:, 2 * HD :].astype(BF16)


def starts_at(begins, position):
    found = jnp.zeros_like(position)
    for begin in begins:
        found = jnp.where(begin <= position, jnp.maximum(found, begin), found)
    return found


R1, R2, R3, X0, X1, H1, H2, H3, OWN = range(9)


class Refs:
    def __init__(self, names, refs):
        for name, ref in zip(names, refs, strict=True):
            setattr(self, name, ref)


def attend(r, mine, j, diagonal, tile=256):
    rows, span = r.query.shape[0], r.pairs.shape[2]
    factor = HD ** (-0.5) * 1.4426950408889634
    key, value = r.pairs[j, 0], r.pairs[j, 1]
    for index in range(rows // tile):
        at = slice(index * tile, (index + 1) * tile)
        scores = lax.dot_general(
            r.query[at, :], key, (((1,), (1,)), ((), ())), preferred_element_type=F32
        )
        column = lax.broadcasted_iota(jnp.int32, (tile, span), 1)
        allowed = column >= r.start[at, :1] - j * span
        if diagonal:
            row = index * tile + lax.broadcasted_iota(jnp.int32, (tile, span), 0)
            allowed = allowed & (column <= row)
        scores = jnp.where(allowed, scores, -1e30)
        top = jnp.max(scores, axis=1, keepdims=True)
        if not diagonal:
            old = r.peak[at, :1]
            top = jnp.maximum(old, top)
        weights = jnp.exp2((scores - top) * factor)
        denom = jnp.sum(weights, axis=1, keepdims=True)
        accum = jnp.dot(weights.astype(BF16), value, preferred_element_type=F32)
        if not diagonal:
            scale = jnp.exp2((old - top) * factor)
            denom = denom + r.denom[at, :1] * scale
            accum = accum + r.accum[at, :] * scale
        r.peak[at, :] = jnp.broadcast_to(top, (tile, HD))
        r.denom[at, :] = jnp.broadcast_to(denom, (tile, HD))
        r.accum[at, :] = accum


def exchange(r, sent):
    dp, tensor, x_hi, z = places()
    x_lo, y, core = dp // (2 * NY), lax.rem(dp // 2, NY), lax.rem(dp, 2)

    def index(xx, yy, cc):
        return xx * 2 * NY + yy * 2 + cc

    k_partner = (index(1 - x_lo, y, core), tensor)
    sibling = (index(x_lo, y, 1 - core), tensor)
    up, down = ((index(x_lo, turn(y, by, NY), core), tensor) for by in (1, -1))
    z_peers = [(dp, x_hi * NZ + turn(z, by, NZ)) for by in range(1, NZ)]
    z_nexts = (z_peers[0], z_peers[-1])
    s_partner = (dp, (1 - x_hi) * NZ + z)
    deep = r.w_out.shape[0] // 4
    first, second = x_lo == 0, x_lo == 1

    def chip(by):
        return turn(y, by, NY)

    arrives = {
        R1: (y >= 1, x_lo, chip(-1)),
        R2: (y >= 2, x_lo, chip(-2)),
        R3: (y == 3, x_lo, chip(1)),
        X0: (second, 0, y),
        X1: (second & (y >= 1), 0, chip(-1)),
        H1: (second & (y <= 2), 0, chip(1)),
        H2: (second & (y <= 1), 0, chip(2)),
        H3: (second & (y == 0), 0, chip(-1)),
        OWN: (None, x_lo, y),
    }

    def k_copy(event, part, xx, yy, device):
        block = r.pairs.at[index(xx, yy, core), part]
        return remote(block, block, r.k_send.at[event, part], r.k_recv.at[event, part], device)

    later = []

    def when(condition, copy):
        @pl.when(condition)
        def _():
            copy.start()

        later.append((condition, copy))

    def k_wait(event, part):
        condition, xx, yy = arrives[event]

        @pl.when(condition)
        def _():
            k_copy(event, part, xx, yy, up).wait_recv()

    def c_copy(event, cc):
        _, xx, yy = arrives[event]
        block = r.pairs.at[index(xx, yy, cc)]
        return remote(block, block, r.c_send.at[event], r.c_recv.at[event], sibling)

    def share(event):
        condition = arrives[event][0]
        if condition is None:
            sent.start(c_copy(event, core))
        else:
            when(condition, c_copy(event, core))

    def shared(*events):
        for event in events:
            condition = arrives[event][0]
            if condition is None:
                c_copy(event, 1 - core).wait_recv()
            else:

                @pl.when(condition)
                def _(event=event):
                    c_copy(event, 1 - core).wait_recv()

    def work(*events):
        found = []
        for event in events:
            condition, xx, yy = arrives[event]
            for cc in (core, 1 - core):
                if event == OWN and cc is core:
                    continue
                j = index(xx, yy, cc)
                needed = (j < dp) & (j >= dp - 10)
                found.append((j, needed if condition is None else needed & condition))

        @pl.loop(0, len(found))
        def _(step):
            j, needed = found[0]
            needed = needed.astype(jnp.int32)
            for number, (jj, wanted) in enumerate(found[1:], 1):
                j = jnp.where(step == number, jj, j)
                needed = jnp.where(step == number, wanted.astype(jnp.int32), needed)

            @pl.when(needed == 1)
            def _():
                attend(r, dp, j, False)

    def w_copy(way, far, sub, hops):
        top = pl.multiple_of(core * 2 * deep + sub * deep, deep)
        block = r.wide.at[turn(z, -towards(way, hops), NZ), pl.ds(top, deep)]
        sems = r.w_send.at[way, far - 1, sub], r.w_recv.at[way, far - 1, sub]
        return remote(block, block, *sems, z_nexts[way])

    def w_share(by, slot, cc):
        top = pl.multiple_of(cc * 2 * deep, 2 * deep)
        block = r.wide.at[turn(z, by, NZ), pl.ds(top, 2 * deep)]
        return remote(block, block, r.wc_send.at[slot], r.wc_recv.at[slot], sibling)

    def w_forward(far, sub):
        for way in range(2):
            if far < 4 or sub == way:
                w_copy(way, far, sub, far).wait_recv()
            if far < 3 or (far == 3 and sub == way):
                sent.start(w_copy(way, far + 1, sub, far))

    def w_spread(far):
        for way in range(2):
            sent.start(w_share(towards(way, -far), 2 * (far - 1) + way, core))

    for part in range(2):
        when(y <= 2, k_copy(R1, part, x_lo, y, up))
        when(y == 0, k_copy(R3, part, x_lo, y, down))
        when(first, k_copy(X0, part, 0, y, k_partner))
    share(OWN)
    for sub in range(2):
        for way in range(2):
            sent.start(w_copy(way, 1, sub, 0))
    s_cross = remote(r.part.at[1 - x_hi], r.s_got, r.sx_send, r.sx_recv, s_partner)
    sent.start(s_cross)
    for part in range(2):
        k_wait(R1, part)
        when((y >= 1) & (y <= 2), k_copy(R2, part, x_lo, chip(-1), up))
        when(first & (y >= 1), k_copy(X1, part, 0, chip(-1), k_partner))
        k_wait(X0, part)
        when(second & (y >= 1), k_copy(H1, part, 0, y, down))
        when(second & (y == 3), k_copy(H3, part, 0, y, up))
        w_forward(1, part)
    share(R1)
    share(X0)
    w_spread(1)
    s_cross.wait_recv()
    r.s_out[...] = (r.part[x_hi].astype(F32) + r.s_got[...].astype(F32)).astype(BF16)
    k_wait(R3, 0)
    k_wait(R3, 1)
    share(R3)
    shared(OWN, R1)
    work(OWN, R1)
    w_forward(2, 0)
    for part in range(2):
        k_wait(H1, part)
        when(second & (y >= 1) & (y <= 2), k_copy(H2, part, 0, chip(1), down))
    share(H1)
    w_forward(2, 1)
    w_spread(2)
    shared(X0, R3)
    work(X0, R3)
    for event in (X1, R2, H3):
        k_wait(event, 0)
        k_wait(event, 1)
        share(event)
    w_forward(3, 0)
    shared(H1)
    work(H1)
    w_forward(3, 1)
    w_spread(3)
    k_wait(H2, 0)
    k_wait(H2, 1)
    share(H2)
    shared(X1, R2, H3)
    work(X1, R2, H3)
    w_forward(4, 0)
    w_forward(4, 1)
    sent.start(w_share(4, 6, core))
    shared(H2)
    work(H2)
    r.attended[...] = (r.accum[...] / r.denom[...]).astype(BF16)

    def finish():
        for condition, copy in later:

            @pl.when(condition)
            def _(copy=copy):
                copy.wait_send()

    def wide_whole():
        for slot, by in enumerate([-1, 1, -2, 2, -3, 3, 4]):
            w_share(by, slot, 1 - core).wait_recv()

    return wide_whole, finish


def layer_body(names, total_rows, *refs):
    r = Refs(names, refs)
    dp, tensor, x_hi, z = places()
    size = 2 * NZ
    own, width = r.my_tokens.shape
    pair = 2 * own
    rows = size * own
    row = z * 2 + x_hi
    partner = (dp, (1 - x_hi) * NZ + z)
    z_peers = [(dp, x_hi * NZ + turn(z, by, NZ)) for by in range(1, NZ)]
    t_peers = [turn(tensor, by, size) for by in range(1, size)]
    d_peers = [turn(dp, by, size) for by in range(1, size)]
    loads = []
    for index, name in enumerate(("w_gate", "w_up", "w_down", "projector")):
        far, near = getattr(r, name + "_hbm"), getattr(r, name)
        loads.append(pltpu.make_async_copy(far, near, r.load_sem.at[index]))
        loads[-1].start()
    r.pairs[dp] = r.pair[...]
    r.wide[z] = r.w_out[...]

    def diagonal():
        position = dp * rows + lax.broadcasted_iota(jnp.int32, (rows, HD), 0)
        r.start[...] = starts_at([r.begin[at] for at in range(8)], position)
        attend(r, dp, dp, True)

    greet([(dp, peer) for peer in t_peers] + [(peer, tensor) for peer in d_peers], diagonal)
    sent = Sent()
    wide_whole, finish_exchange = exchange(r, sent)

    def rows_of(zz):
        return pl.ds(pl.multiple_of(zz * pair, pair), pair)

    for by in range(1, NZ):
        sent.start(
            remote(
                r.attended.at[rows_of(turn(z, by, NZ))],
                r.heads.at[z],
                r.a_send.at[by - 1],
                r.a_recv.at[by - 1],
                z_peers[by - 1],
            )
        )
    for by in range(1, NZ):
        sent.start(
            remote(
                r.s_out.at[turn(z, by, NZ)],
                r.s_in.at[by - 1],
                r.sz_send.at[by - 1],
                r.sz_recv.at[by - 1],
                z_peers[by - 1],
            )
        )
    r.heads[z] = r.attended[rows_of(z), :]
    wide_whole()
    for by in range(1, NZ):
        block = r.heads.at[turn(z, -by, NZ)]
        remote(block, block, r.a_send.at[by - 1], r.a_recv.at[by - 1], z_peers[by - 1]).wait_recv()
    chunk = 512
    joined = jnp.concatenate([r.heads[index] for index in range(NZ)], axis=1)
    depth = joined.shape[1]

    @pl.loop(0, width // chunk)
    def _(step):
        at = pl.ds(pl.multiple_of(step * chunk, chunk), chunk)
        r.partial[:, at] = jnp.dot(
            joined, r.wide[:, :, at].reshape(depth, chunk), preferred_element_type=F32
        )

    def half_rows(plane):
        return pl.ds(pl.multiple_of(plane * own, own), own)

    r.out_send[...] = r.partial[half_rows(1 - x_hi), :].astype(BF16)
    swap = remote(r.out_send, r.out_recv, r.o_send, r.o_recv, partner)
    sent.start(swap)
    mine = r.partial[half_rows(x_hi), :] + r.my_tokens[...].astype(F32)
    swap.wait_recv()
    mixed = (mine + r.out_recv[...].astype(F32)).astype(BF16)
    r.mixed[...] = mixed
    r.blocks[row] = (rms(mixed.astype(F32)) * r.mlp_gain[...]).astype(BF16)

    waited = []

    def units(zs):
        if not waited:
            loads[0].wait()
            loads[1].wait()
            waited.append(True)
        value = jnp.concatenate(
            [r.blocks[pl.ds(zz * 2, 2)].reshape(pair, width) for zz in zs], axis=0
        )
        gate = jnp.dot(value, r.w_gate[...], preferred_element_type=F32)
        up = jnp.dot(value, r.w_up[...], preferred_element_type=F32)
        found = (gate * jax.nn.sigmoid(gate) * up).astype(BF16)
        for at, zz in enumerate(zs):
            r.hidden[zz] = found[at * pair : (at + 1) * pair]

    def ready(distances):
        zs = []
        for by in distances:
            zs += [z] if by == 0 else [turn(z, by, NZ), turn(z, -by, NZ)]
        units(zs)

    mix_gather(
        r.blocks,
        lambda zz, plane: zz * 2 + plane,
        own // 2,
        (r.g_send, r.g_recv, r.gx_send, r.gx_recv),
        ready=ready,
    )
    student_sum = r.s_out[z].astype(F32)
    for by in range(1, NZ):
        got = r.s_in.at[by - 1]
        remote(got, got, r.sz_send.at[by - 1], r.sz_recv.at[by - 1], z_peers[by - 1]).wait_recv()
        student_sum = student_sum + r.s_in[by - 1].astype(F32)
    r.predicted[...] = r.student[...].astype(F32) + student_sum
    loads[2].wait()
    fresh = [2]

    def make(zs):
        if fresh:
            fresh.pop() if len(zs) == 2 else None
            units(zs)
        value = jnp.concatenate([r.hidden[zz] for zz in zs], axis=0)

        @pl.loop(0, width // chunk)
        def _(step):
            at = pl.ds(pl.multiple_of(step * chunk, chunk), chunk)
            out = jnp.dot(value, r.w_down[:, at], preferred_element_type=F32).astype(BF16)
            for index, zz in enumerate(zs):
                for plane in range(2):
                    top = index * pair + plane * own
                    r.parts[zz * 2 + plane, :, at] = out[top : top + own]

    scratch = (r.sbuf, r.rbuf, r.xbuf, r.xlast, r.xgot, r.r_send, r.r_recv, r.rx_send, r.rx_recv)
    top, bottom, more = mix_scatter(r.parts, make, scratch)
    teacher = r.mixed[...].astype(F32) + jnp.concatenate([top, bottom], axis=0)
    teacher = teacher.astype(BF16)
    r.teacher[...] = teacher
    loads[3].wait()
    target = jnp.dot(teacher, r.projector[...], preferred_element_type=F32)
    scaled = ((r.predicted[...] - target) * total_rows ** (-0.5)).astype(BF16)

    def place(by, plane):
        return r.gathered.at[turn(z, by, NZ) * 2 + plane]

    def across(by, plane):
        block = place(by, plane)
        at = by % NZ
        return remote(block, block, r.px_send.at[at], r.px_recv.at[at], partner)

    def along(by, device):
        block = place(-by if device is None else 0, x_hi)
        sems = r.p_send.at[by - 1], r.p_recv.at[by - 1]
        return remote(block, block, *sems, z_peers[by - 1])

    r.gathered[row] = scaled
    for by in (4, 3, 5, 2, 6, 1, 7):
        sent.start(along(by, True))
    sent.start(across(0, x_hi))
    for by, peer in enumerate(t_peers):
        sent.start(
            remote(
                r.teacher.at[:, pl.ds(pl.multiple_of(peer * HD, HD), HD)],
                r.columns.at[row],
                r.t_send.at[by],
                r.t_recv.at[by],
                (dp, peer),
            )
        )
    r.columns[row] = r.teacher[:, pl.ds(pl.multiple_of(tensor * HD, HD), HD)]
    for by in (1, 7, 2, 6, 3, 5, 4):
        along(by, None).wait_recv()
        sent.start(across(-by, x_hi))
    for by in (0, 1, 7, 2, 6, 3, 5, 4):
        across(-by, 1 - x_hi).wait_recv()

    scaled = r.gathered[...].reshape(rows, -1)
    grad_hidden = lax.dot_general(
        scaled, r.s_down[...], (((1,), (1,)), ((), ())), preferred_element_type=F32
    )
    both = jnp.concatenate(
        [(grad_hidden * r.by_gate[...]).astype(BF16), (grad_hidden * r.by_up[...]).astype(BF16)],
        axis=1,
    )
    both = jnp.dot(r.normed_t[...], both, preferred_element_type=F32).astype(BF16)
    down = jnp.dot(r.hidden_t[...], scaled, preferred_element_type=F32).astype(BF16)
    count = grad_hidden.shape[1]
    r.grads[:, :own] = both[:, :count].reshape(size, own, count)
    r.grads[:, own:pair] = both[:, count:].reshape(size, own, count)
    down = jnp.concatenate([down[:, at : at + HD] for at in range(0, down.shape[1], HD)], axis=0)
    r.grads[:, pair : 3 * own] = down.reshape(size, own, HD)
    squares = scaled.astype(F32)
    squares = jnp.sum((squares * squares).reshape(-1, 8, scaled.shape[1]), axis=0)
    squares = sum(squares[:, at : at + HD] for at in range(0, scaled.shape[1], HD))
    high = squares.astype(BF16)
    low = (squares - high.astype(F32)).astype(BF16)
    both = jnp.concatenate([high, low], axis=0)
    r.grads[:, 3 * own :] = jnp.broadcast_to(both[None], (size,) + both.shape)

    def origin(by):
        return turn(dp, -(by + 1), size)

    r.inbox[dp] = r.grads[dp]
    for by, peer in enumerate(d_peers):
        sems = r.send1.at[by], r.recv1.at[by]
        sent.start(remote(r.grads.at[peer], r.inbox.at[dp], *sems, (peer, tensor)))
    for by, peer in enumerate(d_peers):
        block = r.inbox.at[origin(by)]
        remote(block, block, r.send1.at[by], r.recv1.at[by], (peer, tensor)).wait_recv()
    total = r.inbox[0].astype(F32)
    for index in range(1, size):
        total = total + r.inbox[index].astype(F32)
    r.sums[dp] = total[: 3 * own].astype(BF16)
    r.error[...] = total[3 * own : 3 * own + 8] + total[3 * own + 8 :]
    for by, peer in enumerate(d_peers):
        block = r.sums.at[dp]
        sent.start(remote(block, block, r.send2.at[by], r.recv2.at[by], (peer, tensor)))
    for by, peer in enumerate(t_peers):
        source = turn(tensor, -(by + 1), size)
        block = r.columns.at[lax.rem(source, NZ) * 2 + source // NZ]
        remote(block, block, r.t_send.at[by], r.t_recv.at[by], (dp, peer)).wait_recv()
    for by, peer in enumerate(d_peers):
        block = r.sums.at[origin(by)]
        remote(block, block, r.send2.at[by], r.recv2.at[by], (peer, tensor)).wait_recv()
    finish_exchange()
    sent.finish()
    more.finish()


def finish_body(columns_ref, sums_ref, squares_ref, teacher_ref, gate_ref, up_ref, down_ref, error_ref):
    rows, width = teacher_ref.shape
    own = rows // (2 * NZ)
    teacher_ref[...] = columns_ref[...].reshape(rows, width)
    sums = sums_ref[...].astype(F32)
    gate_ref[...] = sums[:, :own].reshape(-1, width)
    up_ref[...] = sums[:, own : 2 * own].reshape(-1, width)
    down = sums[:, 2 * own :].reshape(-1, width)
    for index in range(down.shape[0] // width):
        lanes = slice(index * width, (index + 1) * width)
        down_ref[:, lanes] = down[lanes]
    total = jnp.sum(jnp.sum(squares_ref[...], axis=0, keepdims=True), axis=1, keepdims=True)
    error_ref[...] = total / down_ref.shape[1]


def finish(columns, sums, squares):
    own, units = columns.shape[1:]
    rows = 2 * NZ * own
    shapes = (
        ((rows, units), BF16),
        ((rows, units), F32),
        ((rows, units), F32),
        ((units, rows), F32),
        ((1, 1), F32),
    )
    return pl.pallas_call(
        finish_body,
        out_shape=tuple(jax.ShapeDtypeStruct(shape, kind) for shape, kind in shapes),
        in_specs=[VM] * 3,
        out_specs=(VM,) * 5,
        compiler_params=pltpu.CompilerParams(vmem_limit_bytes=LIMIT),
        name="finish",
    )(columns, sums, squares)


def frequencies(head_dim):
    indices = jnp.arange(head_dim // 2).astype(F32)
    return jnp.exp(-jnp.log(500000.0) * 2.0 * indices / head_dim)


def local(
    tokens,
    series_ids,
    offsets,
    norm_gain,
    mlp_gain,
    w_query,
    w_key,
    w_value,
    w_out,
    w_gate,
    w_up,
    w_down,
    projector,
    student_in,
    s_gate,
    s_up,
    s_down,
):
    rows = tokens.shape[0]
    size = 2 * NZ
    own = rows // size
    width = projector.shape[0]
    narrow = student_in.shape[1]
    units = s_gate.shape[1]
    ff = w_gate.shape[1]
    dp, tensor, x_hi, z = places()
    my_rows = (z * 2 + x_hi) * own

    angles = offsets.astype(F32)[:, None] * frequencies(HD)[None, :]
    cosine, sine = jnp.cos(angles), jnp.sin(angles)
    cosine = jnp.concatenate([cosine, cosine], axis=1)
    sine = jnp.concatenate([-sine, sine], axis=1)
    series = jnp.arange(8, dtype=jnp.int32)
    begins = jnp.sum((series_ids[None, :] < series[:, None]).astype(jnp.int32), axis=1)
    begins = jnp.concatenate([begins, dp[None].astype(jnp.int32)])
    my_student = lax.dynamic_slice_in_dim(student_in, my_rows, own, 0)

    query, pair, my_tokens, part, normed_t, hidden_t, by_gate, by_up = call(
        project_body,
        "project",
        1,
        (
            tokens,
            norm_gain[None],
            cosine,
            sine,
            w_query,
            w_key,
            w_value,
            student_in,
            s_gate,
            s_up,
            s_down,
        ),
        (
            ((rows, HD), BF16),
            ((2, rows, HD), BF16),
            ((own, width), BF16),
            ((2, NZ, own, narrow), BF16),
            ((narrow, rows), BF16),
            ((units, rows), BF16),
            ((rows, units), F32),
            ((rows, units), F32),
        ),
        [
            pltpu.VMEM((size, rows, HD), BF16),
            pltpu.VMEM((rows, width), BF16),
            pltpu.VMEM((width, 3 * HD), BF16),
            *RING_SEMS,
        ],
    )
    inputs = {
        "begin": begins,
        "query": query,
        "pair": pair,
        "w_out": w_out,
        "part": part,
        "my_tokens": my_tokens,
        "mlp_gain": mlp_gain[None],
        "w_gate_hbm": w_gate,
        "w_up_hbm": w_up,
        "w_down_hbm": w_down,
        "projector_hbm": projector,
        "student": my_student,
        "normed_t": normed_t,
        "hidden_t": hidden_t,
        "by_gate": by_gate,
        "by_up": by_up,
        "s_down": s_down,
    }
    outputs = {
        "columns": ((size, own, HD), BF16),
        "sums": ((size, 3 * own, units), BF16),
        "error": ((8, HD), F32),
    }
    one = pltpu.SemaphoreType.DMA
    half = own // 2
    scratch = {
        "pairs": pltpu.VMEM((4 * NY, 2, rows, HD), BF16),
        "wide": pltpu.VMEM((NZ,) + w_out.shape, BF16),
        "start": pltpu.VMEM((rows, HD), jnp.int32),
        "peak": pltpu.VMEM((rows, HD), F32),
        "denom": pltpu.VMEM((rows, HD), F32),
        "accum": pltpu.VMEM((rows, HD), F32),
        "attended": pltpu.VMEM((rows, HD), BF16),
        "k_send": dma(9, 2),
        "k_recv": dma(9, 2),
        "c_send": dma(9),
        "c_recv": dma(9),
        "w_send": dma(2, 4, 2),
        "w_recv": dma(2, 4, 2),
        "wc_send": dma(7),
        "wc_recv": dma(7),
        "s_got": pltpu.VMEM((NZ, own, narrow), BF16),
        "s_out": pltpu.VMEM((NZ, own, narrow), BF16),
        "s_in": pltpu.VMEM((NZ - 1, own, narrow), BF16),
        "sx_send": one,
        "sx_recv": one,
        "sz_send": dma(7),
        "sz_recv": dma(7),
        "w_gate": pltpu.VMEM(w_gate.shape, BF16),
        "w_up": pltpu.VMEM(w_up.shape, BF16),
        "w_down": pltpu.VMEM(w_down.shape, BF16),
        "projector": pltpu.VMEM(projector.shape, BF16),
        "load_sem": dma(4),
        "heads": pltpu.VMEM((NZ, 2 * own, HD), BF16),
        "a_send": dma(7),
        "a_recv": dma(7),
        "out_send": pltpu.VMEM((own, width), BF16),
        "out_recv": pltpu.VMEM((own, width), BF16),
        "o_send": one,
        "o_recv": one,
        "partial": pltpu.VMEM((2 * own, width), F32),
        "mixed": pltpu.VMEM((own, width), BF16),
        "blocks": pltpu.VMEM((size, own, width), BF16),
        "hidden": pltpu.VMEM((NZ, 2 * own, ff), BF16),
        "parts": pltpu.VMEM((size, own, width), BF16),
        "predicted": pltpu.VMEM((own, narrow), F32),
        "g_send": dma(2, 4, 3),
        "g_recv": dma(2, 4, 3),
        "gx_send": dma(9),
        "gx_recv": dma(9),
    }
    names = ("sbuf", "rbuf", "xbuf", "xlast", "xgot", "r_send", "r_recv", "rx_send", "rx_recv")
    scratch.update(zip(names, scatter_scratch(half, width), strict=True))
    scratch.update(
        {
            "teacher": pltpu.VMEM((own, width), BF16),
            "gathered": pltpu.VMEM((size, own, narrow), BF16),
            "px_send": dma(8),
            "px_recv": dma(8),
            "p_send": dma(7),
            "p_recv": dma(7),
            "t_send": dma(size - 1),
            "t_recv": dma(size - 1),
            "grads": pltpu.VMEM((size, 3 * own + 16, units), BF16),
            "inbox": pltpu.VMEM((size, 3 * own + 16, units), BF16),
            "send1": dma(size - 1),
            "recv1": dma(size - 1),
            "send2": dma(size - 1),
            "recv2": dma(size - 1),
        }
    )
    specs = {"begin": SM}
    far = pl.BlockSpec(memory_space=pl.ANY)
    columns, sums, squares = call(
        functools.partial(
            layer_body, (*inputs, *outputs, *scratch), rows * lax.axis_size("dp")
        ),
        "layer",
        2,
        tuple(inputs.values()),
        tuple(outputs.values()),
        list(scratch.values()),
        [far if name.endswith("_hbm") else specs.get(name, VM) for name in inputs],
    )
    teacher_out, grad_gate, grad_up, grad_down, error = finish(columns, sums, squares)
    return (teacher_out, grad_gate, grad_up, grad_down, error.reshape(()))


def solution(mesh):
    in_specs = (
        P("dp", "tensor"),
        P(),
        P("dp"),
        P(),
        P(),
        P(None, "tensor"),
        P(None, "tensor"),
        P(None, "tensor"),
        P("tensor", None),
        P(None, "tensor"),
        P(None, "tensor"),
        P("tensor", None),
        P(),
        P("dp", None),
        P(None, "tensor"),
        P(None, "tensor"),
        P("tensor", None),
    )
    out_specs = (P("dp", "tensor"), P(None, "tensor"), P(None, "tensor"), P("tensor", None), P())
    return jax.shard_map(local, mesh=mesh, in_specs=in_specs, out_specs=out_specs, check_vma=False)
```

time: 206 us -> 176 us (0.85)
  Pallas kernels: 199 us -> 169 us
    pallas_call x4 -> x2, Pallas kernels: 192 us -> 167 us  [call(): pl.pallas_call(body, out_shape=tuple((jax.ShapeDtypeStruct(shape, kind) f...]
    pallas_call x1 -> x0, Pallas kernels: 5.46 us -> none  [attention(): pl.pallas_call(functools.partial(attention_body, 256), out_shape=jax.Shap...]
where the time goes in v3:
time: 176 us; the launch traced here: 175 us
  Pallas kernels  169 us (96%)
  other arithmetic  4.21 us (2%)
    pallas_call x2, Pallas kernels, call(): pl.pallas_call(body, out_shape=tuple((jax.ShapeDtypeStruct(shape, kind) f...  167 us

profile of v3, /device:TPU:1, one launch (start us, length us, event | category | flops | bytes accessed | tf_op | source)
XLA Modules:
  0.0 175.4 jit_solution(11472348470834851389)
XLA Ops:
  0.7 0.9 convert_reduce_fusion
  1.6 0.6 pad_add_fusion.refs_0_
  2.2 0.7 convert_element_type.14
  2.9 1.4 constant_dynamic-slice_fusion.refs_11_
  4.3 1.0 fusion
  5.2 1.0 pad_maximum_fusion
  6.2 32.5 %project.1 = (bf16[512,128]{1,0:T(8,128)(2,1)}, bf16[2,512,128]{2,1,0:T(8,128)(2,1)}, bf16[32,2048]{1,0:T(8,128)(2,1)}, bf16[2,8,32,512]{3,2,1,0:T(8,128)(2,1)},...) custom-call(bf16[512,128]{1,0:T(8,128)(2,1)} %tokens_ref.1, ...), custom_call_target="tpu_custom_call" | custom-call | tf_op jit(solution)/shard_map/project/pallas_call | solution.py:62
  38.8 134.6 %layer.1 = (bf16[16,32,128]{2,1,0:T(8,128)(2,1)}, bf16[16,96,128]{2,1,0:T(8,128)(2,1)}, f32[8,128]{1,0:T(8,128)}) custom-call(s32[9]{0:T(128)} %pad_add_fusion.refs_0_, bf16[512,128]{1,0:T(8,128)(2,1)} %get-tuple-element.21.refs_1_, bf16[2,512,128]{2,1,0:T(8,128)(2,1)} %get-tuple-element.22.refs_2_, bf16[128,2048]{1,0:T(8,128)(2,1)} %refs_3_.1, ...), custom_call_target="tpu_custom_call" | custom-call | tf_op jit(solution)/shard_map/layer/pallas_call | solution.py:62
  173.4 2.0 %finish.1 = (bf16[512,128]{1,0:T(8,128)(2,1)}, f32[512,128]{1,0:T(8,128)}, f32[512,128]{1,0:T(8,128)}, f32[128,512]{1,0:T(8,128)}, f32[1,1]{1,0:T(1,128)}) custom-call(bf16[16,32,128]{2,1,0:T(8,128)(2,1)} %get-tuple-element.29.columns_ref, bf16[16,96,128]{2,1,0:T(8,128)(2,1)} %get-tuple-element.30.sums_ref, f32[8,128]{1,0:T(8,128)} %get-tuple-element.31.squares_ref), custom_call_target="tpu_custom_call" | custom-call | tf_op jit(solution)/shard_map/finish/pallas_call | solution.py:850
  (1 shorter events, 0.0 us)

commit v4 on v3

--- a/solution.py
+++ b/solution.py
@@ -12,7 +12,6 @@
 NY = 4
 MESH = pl.DeviceIdType.MESH
 VM = pl.BlockSpec(memory_space=pltpu.VMEM)
-SM = pl.BlockSpec(memory_space=pltpu.SMEM)
 LIMIT = 56 * 1024 * 1024
 F32 = jnp.float32
 BF16 = jnp.bfloat16
@@ -89,9 +88,6 @@
 
 def towards(way, by):
     return by if way == 0 else -by
-
-
-RING_SEMS = [dma(2, 4, 3), dma(2, 4, 3), dma(9), dma(9)]
 
 
 def mix_gather(ref, at, half, sems, hook=lambda step: None, ready=None):
@@ -258,71 +254,40 @@
     return values * lax.rsqrt(jnp.mean(values * values, axis=-1, keepdims=True) + 1e-05)
 
 
-def project_body(
-    tokens_ref,
-    gain_ref,
-    cos_ref,
-    sin_ref,
-    wq_ref,
-    wk_ref,
-    wv_ref,
-    student_ref,
-    s_gate_ref,
-    s_up_ref,
-    s_down_ref,
-    query_ref,
-    pair_ref,
-    my_tokens_ref,
-    part_ref,
-    normed_t_ref,
-    hidden_t_ref,
-    gate_ref,
-    up_ref,
-    blocks,
-    normed,
-    weights,
-    *sems,
-):
+def project(r, after):
     dp, tensor, x_hi, z = places()
-    rows = tokens_ref.shape[0]
+    rows = r.tokens.shape[0]
     own = rows // (2 * NZ)
-    blocks[tensor] = tokens_ref[...]
-    greet(
-        [
-            (dp, (1 - x_hi) * NZ + z),
-            (dp, x_hi * NZ + turn(z, 1, NZ)),
-            (dp, x_hi * NZ + turn(z, -1, NZ)),
-        ]
-    )
 
     def student(step):
         at = pl.ds(step * 128, 128)
-        values = rms(student_ref[at, :].astype(F32))
-        normed_t_ref[:, at] = values.T.astype(BF16)
+        values = rms(r.student[at, :].astype(F32))
+        r.normed_t[:, at] = values.T.astype(BF16)
         values = values.astype(BF16)
-        gate = jnp.dot(values, s_gate_ref[...], preferred_element_type=F32)
-        up = jnp.dot(values, s_up_ref[...], preferred_element_type=F32)
+        gate = jnp.dot(values, r.s_gate[...], preferred_element_type=F32)
+        up = jnp.dot(values, r.s_up[...], preferred_element_type=F32)
         sigmoid = jax.nn.sigmoid(gate)
-        gate_ref[at, :] = up * sigmoid * (1.0 + gate * (1.0 - sigmoid))
-        up_ref[at, :] = gate * sigmoid
+        r.by_gate[at, :] = up * sigmoid * (1.0 + gate * (1.0 - sigmoid))
+        r.by_up[at, :] = gate * sigmoid
         hidden = gate * sigmoid * up
-        hidden_t_ref[:, at] = hidden.T.astype(BF16)
-        out = jnp.dot(hidden.astype(BF16), s_down_ref[...], preferred_element_type=F32)
+        r.hidden_t[:, at] = hidden.T.astype(BF16)
+        out = jnp.dot(hidden.astype(BF16), r.s_down[...], preferred_element_type=F32)
         for index in range(128 // own):
             block = out[index * own : (index + 1) * own].astype(BF16)
-            part_ref[index % 2, step * (64 // own) + index // 2] = block
+            r.part[index % 2, step * (64 // own) + index // 2] = block
 
     def hook(step):
         if step == 0:
-            weights[:, :HD] = wq_ref[...]
-            weights[:, HD : 2 * HD] = wk_ref[...]
-            weights[:, 2 * HD :] = wv_ref[...]
+            r.weights[:, :HD] = r.w_query[...]
+            r.weights[:, HD : 2 * HD] = r.w_key[...]
+            r.weights[:, 2 * HD :] = r.w_value[...]
         student(step)
 
-    mix_gather(blocks, lambda zz, plane: plane * NZ + zz, rows // 2, sems, hook)
+    mix_gather(r.tok, lambda zz, plane: plane * NZ + zz, rows // 2, (r.q_send, r.q_recv, r.qx_send, r.qx_recv), hook)
+    after()
     my_rows = pl.multiple_of((z * 2 + x_hi) * own, own)
     for index in range(2 * NZ):
-        my_tokens_ref[:, index * HD : (index + 1) * HD] = blocks[index, pl.ds(my_rows, own)]
+        r.my_tokens[:, index * HD : (index + 1) * HD] = r.tok[index, pl.ds(my_rows, own)]
     tile = 128
 
     @pl.loop(0, rows // tile)
@@ -330,36 +295,41 @@
         at = pl.ds(pl.multiple_of(step * tile, tile), tile)
         square = jnp.zeros((tile, HD), F32)
         for index in range(2 * NZ):
-            value = blocks[index, at].astype(F32)
+            value = r.tok[index, at].astype(F32)
             square = square + value * value
         mean = jnp.sum(square, axis=1, keepdims=True) / (2 * NZ * HD)
         scale = lax.rsqrt(mean + 1e-05)
         for index in range(2 * NZ):
             lanes = slice(index * HD, (index + 1) * HD)
-            value = blocks[index, at].astype(F32) * scale * gain_ref[:, lanes]
-            normed[at, lanes] = value.astype(BF16)
+            value = r.tok[index, at].astype(F32) * scale * r.norm_gain[:, lanes]
+            r.normed[at, lanes] = value.astype(BF16)
 
     tile = 256
 
     @pl.loop(0, rows // tile)
     def _(step):
         at = pl.ds(pl.multiple_of(step * tile, tile), tile)
-        out = jnp.dot(normed[at, :], weights[...], preferred_element_type=F32)
-        cosine, sine = cos_ref[at, :], sin_ref[at, :]
+        out = jnp.dot(r.normed[at, :], r.weights[...], preferred_element_type=F32)
+        cosine, sine = r.cosine[at, :], r.sine[at, :]
 
         def rotary(values):
             return (values * cosine + pltpu.roll(values, HD // 2, 1) * sine).astype(BF16)
 
-        query_ref[at, :] = rotary(out[:, :HD])
-        pair_ref[0, at, :] = rotary(out[:, HD : 2 * HD])
-        pair_ref[1, at, :] = out[:, 2 * HD :].astype(BF16)
-
-
-def starts_at(begins, position):
-    found = jnp.zeros_like(position)
-    for begin in begins:
+        r.query[at, :] = rotary(out[:, :HD])
+        r.pairs[dp, 0, at, :] = rotary(out[:, HD : 2 * HD])
+        r.pairs[dp, 1, at, :] = out[:, 2 * HD :].astype(BF16)
+
+
+def find_starts(r):
+    dp = lax.axis_index("dp")
+    rows = r.start.shape[0]
+    position = (dp * rows + lax.broadcasted_iota(jnp.int32, r.start.shape, 0)).astype(F32)
+    found = jnp.zeros(r.start.shape, F32)
+    for number in range(1, 8):
+        before = jnp.where(r.series[...] < number, 1.0, 0.0)
+        begin = jnp.sum(jnp.sum(before, axis=0, keepdims=True), axis=1, keepdims=True)
         found = jnp.where(begin <= position, jnp.maximum(found, begin), found)
-    return found
+    r.start[...] = found.astype(jnp.int32)
 
 
 R1, R2, R3, X0, X1, H1, H2, H3, OWN = range(9)
@@ -521,63 +491,67 @@
         for way in range(2):
             sent.start(w_share(towards(way, -far), 2 * (far - 1) + way, core))
 
-    for part in range(2):
-        when(y <= 2, k_copy(R1, part, x_lo, y, up))
-        when(y == 0, k_copy(R3, part, x_lo, y, down))
-        when(first, k_copy(X0, part, 0, y, k_partner))
-    share(OWN)
-    for sub in range(2):
-        for way in range(2):
-            sent.start(w_copy(way, 1, sub, 0))
-    s_cross = remote(r.part.at[1 - x_hi], r.s_got, r.sx_send, r.sx_recv, s_partner)
-    sent.start(s_cross)
-    for part in range(2):
-        k_wait(R1, part)
-        when((y >= 1) & (y <= 2), k_copy(R2, part, x_lo, chip(-1), up))
-        when(first & (y >= 1), k_copy(X1, part, 0, chip(-1), k_partner))
-        k_wait(X0, part)
-        when(second & (y >= 1), k_copy(H1, part, 0, y, down))
-        when(second & (y == 3), k_copy(H3, part, 0, y, up))
-        w_forward(1, part)
-    share(R1)
-    share(X0)
-    w_spread(1)
-    s_cross.wait_recv()
-    r.s_out[...] = (r.part[x_hi].astype(F32) + r.s_got[...].astype(F32)).astype(BF16)
-    k_wait(R3, 0)
-    k_wait(R3, 1)
-    share(R3)
-    shared(OWN, R1)
-    work(OWN, R1)
-    w_forward(2, 0)
-    for part in range(2):
-        k_wait(H1, part)
-        when(second & (y >= 1) & (y <= 2), k_copy(H2, part, 0, chip(1), down))
-    share(H1)
-    w_forward(2, 1)
-    w_spread(2)
-    shared(X0, R3)
-    work(X0, R3)
-    for event in (X1, R2, H3):
-        k_wait(event, 0)
-        k_wait(event, 1)
-        share(event)
-    w_forward(3, 0)
-    shared(H1)
-    work(H1)
-    w_forward(3, 1)
-    w_spread(3)
-    k_wait(H2, 0)
-    k_wait(H2, 1)
-    share(H2)
-    shared(X1, R2, H3)
-    work(X1, R2, H3)
-    w_forward(4, 0)
-    w_forward(4, 1)
-    sent.start(w_share(4, 6, core))
-    shared(H2)
-    work(H2)
-    r.attended[...] = (r.accum[...] / r.denom[...]).astype(BF16)
+    def begin_wide():
+        for sub in range(2):
+            for way in range(2):
+                sent.start(w_copy(way, 1, sub, 0))
+
+    def arrive():
+        for part in range(2):
+            when(y <= 2, k_copy(R1, part, x_lo, y, up))
+            when(y == 0, k_copy(R3, part, x_lo, y, down))
+            when(first, k_copy(X0, part, 0, y, k_partner))
+        share(OWN)
+        s_cross = remote(r.part.at[1 - x_hi], r.s_got, r.sx_send, r.sx_recv, s_partner)
+        sent.start(s_cross)
+        w_forward(1, 0)
+        w_forward(1, 1)
+        w_spread(1)
+        attend(r, dp, dp, True)
+        for part in range(2):
+            k_wait(R1, part)
+            when((y >= 1) & (y <= 2), k_copy(R2, part, x_lo, chip(-1), up))
+            when(first & (y >= 1), k_copy(X1, part, 0, chip(-1), k_partner))
+            k_wait(X0, part)
+            when(second & (y >= 1), k_copy(H1, part, 0, y, down))
+            when(second & (y == 3), k_copy(H3, part, 0, y, up))
+            w_forward(2, part)
+        share(R1)
+        share(X0)
+        w_spread(2)
+        k_wait(R3, 0)
+        k_wait(R3, 1)
+        share(R3)
+        s_cross.wait_recv()
+        r.s_out[...] = (r.part[x_hi].astype(F32) + r.s_got[...].astype(F32)).astype(BF16)
+        shared(OWN, R1)
+        work(OWN, R1)
+        for part in range(2):
+            k_wait(H1, part)
+            when(second & (y >= 1) & (y <= 2), k_copy(H2, part, 0, chip(1), down))
+        share(H1)
+        w_forward(3, 0)
+        shared(X0)
+        work(X0)
+        w_forward(3, 1)
+        w_spread(3)
+        for event in (X1, R2, H3):
+            k_wait(event, 0)
+            k_wait(event, 1)
+            share(event)
+        shared(R3, H1)
+        work(R3, H1)
+        w_forward(4, 0)
+        w_forward(4, 1)
+        sent.start(w_share(4, 6, core))
+        k_wait(H2, 0)
+        k_wait(H2, 1)
+        share(H2)
+        shared(X1, R2, H3)
+        work(X1, R2, H3)
+        shared(H2)
+        work(H2)
+        r.attended[...] = (r.accum[...] / r.denom[...]).astype(BF16)
 
     def finish():
         for condition, copy in later:
@@ -590,17 +564,18 @@
         for slot, by in enumerate([-1, 1, -2, 2, -3, 3, 4]):
             w_share(by, slot, 1 - core).wait_recv()
 
-    return wide_whole, finish
+    return begin_wide, arrive, wide_whole, finish
 
 
 def layer_body(names, total_rows, *refs):
     r = Refs(names, refs)
     dp, tensor, x_hi, z = places()
     size = 2 * NZ
-    own, width = r.my_tokens.shape
+    rows, width = r.tokens.shape[0], r.w_query.shape[0]
+    own = rows // size
     pair = 2 * own
-    rows = size * own
     row = z * 2 + x_hi
+    my_rows = pl.ds(pl.multiple_of(row * own, own), own)
     partner = (dp, (1 - x_hi) * NZ + z)
     z_peers = [(dp, x_hi * NZ + turn(z, by, NZ)) for by in range(1, NZ)]
     t_peers = [turn(tensor, by, size) for by in range(1, size)]
@@ -610,17 +585,16 @@
         far, near = getattr(r, name + "_hbm"), getattr(r, name)
         loads.append(pltpu.make_async_copy(far, near, r.load_sem.at[index]))
         loads[-1].start()
-    r.pairs[dp] = r.pair[...]
     r.wide[z] = r.w_out[...]
-
-    def diagonal():
-        position = dp * rows + lax.broadcasted_iota(jnp.int32, (rows, HD), 0)
-        r.start[...] = starts_at([r.begin[at] for at in range(8)], position)
-        attend(r, dp, dp, True)
-
-    greet([(dp, peer) for peer in t_peers] + [(peer, tensor) for peer in d_peers], diagonal)
+    r.tok[tensor] = r.tokens[...]
+    greet(
+        [(dp, peer) for peer in t_peers] + [(peer, tensor) for peer in d_peers],
+        lambda: find_starts(r),
+    )
     sent = Sent()
-    wide_whole, finish_exchange = exchange(r, sent)
+    begin_wide, arrive, wide_whole, finish_exchange = exchange(r, sent)
+    project(r, begin_wide)
+    arrive()
 
     def rows_of(zz):
         return pl.ds(pl.multiple_of(zz * pair, pair), pair)
@@ -707,7 +681,7 @@
         got = r.s_in.at[by - 1]
         remote(got, got, r.sz_send.at[by - 1], r.sz_recv.at[by - 1], z_peers[by - 1]).wait_recv()
         student_sum = student_sum + r.s_in[by - 1].astype(F32)
-    r.predicted[...] = r.student[...].astype(F32) + student_sum
+    r.predicted[...] = r.student[my_rows, :].astype(F32) + student_sum
     loads[2].wait()
     fresh = [2]
 
@@ -888,69 +862,28 @@
     narrow = student_in.shape[1]
     units = s_gate.shape[1]
     ff = w_gate.shape[1]
-    dp, tensor, x_hi, z = places()
-    my_rows = (z * 2 + x_hi) * own
-
     angles = offsets.astype(F32)[:, None] * frequencies(HD)[None, :]
     cosine, sine = jnp.cos(angles), jnp.sin(angles)
     cosine = jnp.concatenate([cosine, cosine], axis=1)
     sine = jnp.concatenate([-sine, sine], axis=1)
-    series = jnp.arange(8, dtype=jnp.int32)
-    begins = jnp.sum((series_ids[None, :] < series[:, None]).astype(jnp.int32), axis=1)
-    begins = jnp.concatenate([begins, dp[None].astype(jnp.int32)])
-    my_student = lax.dynamic_slice_in_dim(student_in, my_rows, own, 0)
-
-    query, pair, my_tokens, part, normed_t, hidden_t, by_gate, by_up = call(
-        project_body,
-        "project",
-        1,
-        (
-            tokens,
-            norm_gain[None],
-            cosine,
-            sine,
-            w_query,
-            w_key,
-            w_value,
-            student_in,
-            s_gate,
-            s_up,
-            s_down,
-        ),
-        (
-            ((rows, HD), BF16),
-            ((2, rows, HD), BF16),
-            ((own, width), BF16),
-            ((2, NZ, own, narrow), BF16),
-            ((narrow, rows), BF16),
-            ((units, rows), BF16),
-            ((rows, units), F32),
-            ((rows, units), F32),
-        ),
-        [
-            pltpu.VMEM((size, rows, HD), BF16),
-            pltpu.VMEM((rows, width), BF16),
-            pltpu.VMEM((width, 3 * HD), BF16),
-            *RING_SEMS,
-        ],
-    )
     inputs = {
-        "begin": begins,
-        "query": query,
-        "pair": pair,
+        "tokens": tokens,
+        "series": series_ids.reshape(-1, HD),
+        "norm_gain": norm_gain[None],
+        "cosine": cosine,
+        "sine": sine,
+        "w_query": w_query,
+        "w_key": w_key,
+        "w_value": w_value,
         "w_out": w_out,
-        "part": part,
-        "my_tokens": my_tokens,
         "mlp_gain": mlp_gain[None],
         "w_gate_hbm": w_gate,
         "w_up_hbm": w_up,
         "w_down_hbm": w_down,
         "projector_hbm": projector,
-        "student": my_student,
-        "normed_t": normed_t,
-        "hidden_t": hidden_t,
-        "by_gate": by_gate,
-        "by_up": by_up,
+        "student": student_in,
+        "s_gate": s_gate,
+        "s_up": s_up,
         "s_down": s_down,
     }
     outputs = {
@@ -961,6 +894,20 @@
     one = pltpu.SemaphoreType.DMA
     half = own // 2
     scratch = {
+        "tok": pltpu.VMEM((size, rows, HD), BF16),
+        "normed": pltpu.VMEM((rows, width), BF16),
+        "weights": pltpu.VMEM((width, 3 * HD), BF16),
+        "query": pltpu.VMEM((rows, HD), BF16),
+        "my_tokens": pltpu.VMEM((own, width), BF16),
+        "part": pltpu.VMEM((2, NZ, own, narrow), BF16),
+        "normed_t": pltpu.VMEM((narrow, rows), BF16),
+        "hidden_t": pltpu.VMEM((units, rows), BF16),
+        "by_gate": pltpu.VMEM((rows, units), F32),
+        "by_up": pltpu.VMEM((rows, units), F32),
+        "q_send": dma(2, 4, 3),
+        "q_recv": dma(2, 4, 3),
+        "qx_send": dma(9),
+        "qx_recv": dma(9),
         "pairs": pltpu.VMEM((4 * NY, 2, rows, HD), BF16),
         "wide": pltpu.VMEM((NZ,) + w_out.shape, BF16),
         "start": pltpu.VMEM((rows, HD), jnp.int32),
@@ -1026,18 +973,17 @@
             "recv2": dma(size - 1),
         }
     )
-    specs = {"begin": SM}
     far = pl.BlockSpec(memory_space=pl.ANY)
     columns, sums, squares = call(
         functools.partial(
             layer_body, (*inputs, *outputs, *scratch), rows * lax.axis_size("dp")
         ),
         "layer",
-        2,
+        1,
         tuple(inputs.values()),
         tuple(outputs.values()),
         list(scratch.values()),
-        [far if name.endswith("_hbm") else specs.get(name, VM) for name in inputs],
+        [far if name.endswith("_hbm") else VM for name in inputs],
     )
     teacher_out, grad_gate, grad_up, grad_down, error = finish(columns, sums, squares)
     return (teacher_out, grad_gate, grad_up, grad_down, error.reshape(()))

time: 176 us -> 164 us (0.932)
  Pallas kernels: 169 us -> 160 us
    pallas_call x2 -> x1, Pallas kernels: 167 us -> 158 us  [call(): pl.pallas_call(body, out_shape=tuple((jax.ShapeDtypeStruct(shape, kind) f...]
where the time goes in v4:
time: 164 us
  Pallas kernels  160 us (98%)
  other arithmetic  2.68 us (2%)
    pallas_call x1, Pallas kernels, call(): pl.pallas_call(body, out_shape=tuple((jax.ShapeDtypeStruct(shape, kind) f...  158 us

profile of v4, /device:TPU:1, one launch (start us, length us, event | category | flops | bytes accessed | tf_op | source)
XLA Modules:
  0.0 163.6 jit_solution(884933192067492773)
XLA Ops:
  0.6 0.7 convert_element_type.10
  1.3 1.0 fusion
  2.3 1.0 pad_maximum_fusion
  3.3 158.3 %layer.1 = (bf16[16,32,128]{2,1,0:T(8,128)(2,1)}, bf16[16,96,128]{2,1,0:T(8,128)(2,1)}, f32[8,128]{1,0:T(8,128)}) custom-call(bf16[512,128]{1,0:T(8,128)(2,1)} %refs_0_.1, s32[64,128]{1,0:T(8,128)} %bitcast.4, f32[1,2048]{1,0:T(1,128)} %bitcast.5, f32[512,128]{1,0:T(8,128)} %get-tuple-element.24.refs_3_, f32[512,128]{1,0:T(8,128)} %get-tuple-element.25.refs_4_, ...), custom_call_target="tpu_custom_call" | custom-call | tf_op jit(solution)/shard_map/layer/pallas_call | solution.py:61
  161.6 2.0 %finish.1 = (bf16[512,128]{1,0:T(8,128)(2,1)}, f32[512,128]{1,0:T(8,128)}, f32[512,128]{1,0:T(8,128)}, f32[128,512]{1,0:T(8,128)}, f32[1,1]{1,0:T(1,128)}) custom-call(bf16[16,32,128]{2,1,0:T(8,128)(2,1)} %get-tuple-element.13.columns_ref, bf16[16,96,128]{2,1,0:T(8,128)(2,1)} %get-tuple-element.14.sums_ref, f32[8,128]{1,0:T(8,128)} %get-tuple-element.15.squares_ref), custom_call_target="tpu_custom_call" | custom-call | tf_op jit(solution)/shard_map/finish/pallas_call | solution.py:824
  (1 shorter events, 0.0 us)

commit v5 on v4

--- a/solution.py
+++ b/solution.py
@@ -90,7 +90,7 @@
     return by if way == 0 else -by
 
 
-def mix_gather(ref, at, half, sems, hook=lambda step: None, ready=None):
+def mix_gather(ref, at, half, sems, hook=lambda step: None, ready=None, tail=None):
     ring_send, ring_recv, x_send, x_recv = sems
     dp, tensor, x_hi, z = places()
     partner = (dp, (1 - x_hi) * NZ + z)
@@ -150,10 +150,12 @@
                 ready((2,))
     ring(1, 4, 1, 4).wait_recv()
     sent.start(cross(turn(z, 4, NZ), 1, slot(1, 4)))
+    crossed(3)
+    if tail:
+        tail()
     for sub in (0, 2):
         ring(0, 4, sub, 4).wait_recv()
     crossed(4)
-    crossed(3)
     sent.finish()
 
 
@@ -216,42 +218,76 @@
             source = sbuf.at[way, far - 1, sub]
         sent.start(ring(way, far, sub, source))
 
-    far4 = turn(z, 4, NZ)
-    make([far4])
-    sent.start(cross(far4, 7))
-    for sub in (0, 2):
-        send(0, 4, sub)
-    for far in (3, 2, 1):
-        places_now = [turn(z, by, NZ) for by in (far, -far)]
-        make(places_now)
+    def make_pair(far):
+        pair = [turn(z, by, NZ) for by in (far, -far)]
+        make(pair)
         for way in range(2):
-            sent.start(cross(places_now[way], slot(way, far)))
-        if far == 3:
-            for sub in (0, 2):
-                send(1, 3, sub)
-            send(1, 4, 1)
+            sent.start(cross(pair[way], slot(way, far)))
+
+    def begin():
+        make_pair(3)
+        for sub in (0, 2):
+            send(1, 3, sub)
+
+    def rest():
+        far4 = turn(z, 4, NZ)
+        make([far4])
+        sent.start(cross(far4, 7))
+        for sub in (0, 2):
+            send(0, 4, sub)
+        make_pair(2)
+        send(1, 4, 1)
+        for sub in (1, 2, 0):
+            send(0, 3, sub)
+        send(1, 3, 1)
+        make_pair(1)
         for sub in (2, 0, 1):
             for way in range(2):
-                if not (far == 3 and way == 1 and sub != 1):
-                    send(way, far, sub)
-    make([z])
-    sent.start(cross(z, 0))
+                send(way, 2, sub)
+        make([z])
+        sent.start(cross(z, 0))
+        for sub in (2, 0, 1):
+            for way in range(2):
+                send(way, 1, sub)
+        return last_sums()
 
     def total(sub):
         return view(z, sub)[...].astype(F32) + arrived(0, 1, sub) + arrived(1, 1, sub)
 
-    xlast[...] = total(2).astype(BF16)
-    last = remote(xlast, xgot, x_send.at[8], x_recv.at[8], partner)
-    sent.start(last)
-    second = total(1) + crossed(0)
-    first = total(0)
-    last.wait_recv()
-    first = first + xgot[...].astype(F32)
-    return first, second, sent
+    def last_sums():
+        xlast[...] = total(2).astype(BF16)
+        last = remote(xlast, xgot, x_send.at[8], x_recv.at[8], partner)
+        sent.start(last)
+        second = total(1) + crossed(0)
+        first = total(0)
+        last.wait_recv()
+        first = first + xgot[...].astype(F32)
+        return first, second, sent
+
+    return begin, rest
 
 
 def rms(values):
     return values * lax.rsqrt(jnp.mean(values * values, axis=-1, keepdims=True) + 1e-05)
+
+
+def student(r, step):
+    own = r.tokens.shape[0] // (2 * NZ)
+    at = pl.ds(step * 128, 128)
+    values = rms(r.student[at, :].astype(F32))
+    r.normed_t[:, at] = values.T.astype(BF16)
+    values = values.astype(BF16)
+    gate = jnp.dot(values, r.s_gate[...], preferred_element_type=F32)
+    up = jnp.dot(values, r.s_up[...], preferred_element_type=F32)
+    sigmoid = jax.nn.sigmoid(gate)
+    r.by_gate[at, :] = up * sigmoid * (1.0 + gate * (1.0 - sigmoid))
+    r.by_up[at, :] = gate * sigmoid
+    hidden = gate * sigmoid * up
+    r.hidden_t[:, at] = hidden.T.astype(BF16)
+    out = jnp.dot(hidden.astype(BF16), r.s_down[...], preferred_element_type=F32)
+    for index in range(128 // own):
+        block = out[index * own : (index + 1) * own].astype(BF16)
+        r.part[index % 2, step * (64 // own) + index // 2] = block
 
 
 def project(r, after):
@@ -259,29 +295,9 @@
     rows = r.tokens.shape[0]
     own = rows // (2 * NZ)
 
-    def student(step):
-        at = pl.ds(step * 128, 128)
-        values = rms(r.student[at, :].astype(F32))
-        r.normed_t[:, at] = values.T.astype(BF16)
-        values = values.astype(BF16)
-        gate = jnp.dot(values, r.s_gate[...], preferred_element_type=F32)
-        up = jnp.dot(values, r.s_up[...], preferred_element_type=F32)
-        sigmoid = jax.nn.sigmoid(gate)
-        r.by_gate[at, :] = up * sigmoid * (1.0 + gate * (1.0 - sigmoid))
-        r.by_up[at, :] = gate * sigmoid
-        hidden = gate * sigmoid * up
-        r.hidden_t[:, at] = hidden.T.astype(BF16)
-        out = jnp.dot(hidden.astype(BF16), r.s_down[...], preferred_element_type=F32)
-        for index in range(128 // own):
-            block = out[index * own : (index + 1) * own].astype(BF16)
-            r.part[index % 2, step * (64 // own) + index // 2] = block
-
     def hook(step):
-        if step == 0:
-            r.weights[:, :HD] = r.w_query[...]
-            r.weights[:, HD : 2 * HD] = r.w_key[...]
-            r.weights[:, 2 * HD :] = r.w_value[...]
-        student(step)
+        if step == 3:
+            student(r, 3)
 
     mix_gather(r.tok, lambda zz, plane: plane * NZ + zz, rows // 2, (r.q_send, r.q_recv, r.qx_send, r.qx_recv), hook)
     after()
@@ -330,6 +346,23 @@
         begin = jnp.sum(jnp.sum(before, axis=0, keepdims=True), axis=1, keepdims=True)
         found = jnp.where(begin <= position, jnp.maximum(found, begin), found)
     r.start[...] = found.astype(jnp.int32)
+
+
+def prepare(r):
+    find_starts(r)
+    r.weights[:, :HD] = r.w_query[...]
+    r.weights[:, HD : 2 * HD] = r.w_key[...]
+    r.weights[:, 2 * HD :] = r.w_value[...]
+    for step in range(r.offsets.shape[0]):
+        at = pl.ds(step * HD, HD)
+        offset = jnp.broadcast_to(r.offsets[step : step + 1, :].astype(F32), (HD, HD)).T
+        angle = offset * r.frequency[...]
+        lane = lax.broadcasted_iota(jnp.int32, (HD, HD), 1)
+        r.cosine[at, :] = jnp.cos(angle)
+        sine = jnp.sin(angle)
+        r.sine[at, :] = jnp.where(lane < HD // 2, -sine, sine)
+    for step in range(3):
+        student(r, step)
 
 
 R1, R2, R3, X0, X1, H1, H2, H3, OWN = range(9)
@@ -589,7 +622,7 @@
     r.tok[tensor] = r.tokens[...]
     greet(
         [(dp, peer) for peer in t_peers] + [(peer, tensor) for peer in d_peers],
-        lambda: find_starts(r),
+        lambda: prepare(r),
     )
     sent = Sent()
     begin_wide, arrive, wide_whole, finish_exchange = exchange(r, sent)
@@ -609,42 +642,48 @@
                 z_peers[by - 1],
             )
         )
-    for by in range(1, NZ):
-        sent.start(
-            remote(
-                r.s_out.at[turn(z, by, NZ)],
-                r.s_in.at[by - 1],
-                r.sz_send.at[by - 1],
-                r.sz_recv.at[by - 1],
-                z_peers[by - 1],
+    def send_student():
+        for by in range(1, NZ):
+            sent.start(
+                remote(
+                    r.s_out.at[turn(z, by, NZ)],
+                    r.s_in.at[by - 1],
+                    r.sz_send.at[by - 1],
+                    r.sz_recv.at[by - 1],
+                    z_peers[by - 1],
+                )
             )
-        )
+
     r.heads[z] = r.attended[rows_of(z), :]
     wide_whole()
     for by in range(1, NZ):
         block = r.heads.at[turn(z, -by, NZ)]
         remote(block, block, r.a_send.at[by - 1], r.a_recv.at[by - 1], z_peers[by - 1]).wait_recv()
-    chunk = 512
+    chunk = width // 4
     joined = jnp.concatenate([r.heads[index] for index in range(NZ)], axis=1)
     depth = joined.shape[1]
 
-    @pl.loop(0, width // chunk)
-    def _(step):
-        at = pl.ds(pl.multiple_of(step * chunk, chunk), chunk)
-        r.partial[:, at] = jnp.dot(
+    def half_rows(plane):
+        return pl.ds(pl.multiple_of(plane * own, own), own)
+
+    def swap(step):
+        sems = r.o_send.at[step], r.o_recv.at[step]
+        return remote(r.out_send.at[step], r.out_recv.at[step], *sems, partner)
+
+    for step in range(width // chunk):
+        at = slice(step * chunk, (step + 1) * chunk)
+        r.partial[step] = jnp.dot(
             joined, r.wide[:, :, at].reshape(depth, chunk), preferred_element_type=F32
         )
-
-    def half_rows(plane):
-        return pl.ds(pl.multiple_of(plane * own, own), own)
-
-    r.out_send[...] = r.partial[half_rows(1 - x_hi), :].astype(BF16)
-    swap = remote(r.out_send, r.out_recv, r.o_send, r.o_recv, partner)
-    sent.start(swap)
-    mine = r.partial[half_rows(x_hi), :] + r.my_tokens[...].astype(F32)
-    swap.wait_recv()
-    mixed = (mine + r.out_recv[...].astype(F32)).astype(BF16)
-    r.mixed[...] = mixed
+        r.out_send[step] = r.partial[step, half_rows(1 - x_hi), :].astype(BF16)
+        sent.start(swap(step))
+    send_student()
+    for step in range(width // chunk):
+        at = slice(step * chunk, (step + 1) * chunk)
+        mine = r.partial[step, half_rows(x_hi), :] + r.my_tokens[:, at].astype(F32)
+        swap(step).wait_recv()
+        r.mixed[:, at] = (mine + r.out_recv[step].astype(F32)).astype(BF16)
+    mixed = r.mixed[...]
     r.blocks[row] = (rms(mixed.astype(F32)) * r.mlp_gain[...]).astype(BF16)
 
     waited = []
@@ -669,25 +708,11 @@
             zs += [z] if by == 0 else [turn(z, by, NZ), turn(z, -by, NZ)]
         units(zs)
 
-    mix_gather(
-        r.blocks,
-        lambda zz, plane: zz * 2 + plane,
-        own // 2,
-        (r.g_send, r.g_recv, r.gx_send, r.gx_recv),
-        ready=ready,
-    )
-    student_sum = r.s_out[z].astype(F32)
-    for by in range(1, NZ):
-        got = r.s_in.at[by - 1]
-        remote(got, got, r.sz_send.at[by - 1], r.sz_recv.at[by - 1], z_peers[by - 1]).wait_recv()
-        student_sum = student_sum + r.s_in[by - 1].astype(F32)
-    r.predicted[...] = r.student[my_rows, :].astype(F32) + student_sum
-    loads[2].wait()
-    fresh = [2]
+    fresh = [3, 4]
 
     def make(zs):
         if fresh:
-            fresh.pop() if len(zs) == 2 else None
+            fresh.pop()
             units(zs)
         value = jnp.concatenate([r.hidden[zz] for zz in zs], axis=0)
 
@@ -701,13 +726,29 @@
                     r.parts[zz * 2 + plane, :, at] = out[top : top + own]
 
     scratch = (r.sbuf, r.rbuf, r.xbuf, r.xlast, r.xgot, r.r_send, r.r_recv, r.rx_send, r.rx_recv)
-    top, bottom, more = mix_scatter(r.parts, make, scratch)
+    begin_sum, rest_of_sum = mix_scatter(r.parts, make, scratch)
+    loads[2].wait()
+    mix_gather(
+        r.blocks,
+        lambda zz, plane: zz * 2 + plane,
+        own // 2,
+        (r.g_send, r.g_recv, r.gx_send, r.gx_recv),
+        ready=ready,
+        tail=begin_sum,
+    )
+    top, bottom, more = rest_of_sum()
+    student_sum = r.s_out[z].astype(F32)
+    for by in range(1, NZ):
+        got = r.s_in.at[by - 1]
+        remote(got, got, r.sz_send.at[by - 1], r.sz_recv.at[by - 1], z_peers[by - 1]).wait_recv()
+        student_sum = student_sum + r.s_in[by - 1].astype(F32)
+    predicted = r.student[my_rows, :].astype(F32) + student_sum
     teacher = r.mixed[...].astype(F32) + jnp.concatenate([top, bottom], axis=0)
     teacher = teacher.astype(BF16)
     r.teacher[...] = teacher
     loads[3].wait()
     target = jnp.dot(teacher, r.projector[...], preferred_element_type=F32)
-    scaled = ((r.predicted[...] - target) * total_rows ** (-0.5)).astype(BF16)
+    scaled = ((predicted - target) * total_rows ** (-0.5)).astype(BF16)
 
     def place(by, plane):
         return r.gathered.at[turn(z, by, NZ) * 2 + plane]
@@ -726,6 +767,9 @@
     for by in (4, 3, 5, 2, 6, 1, 7):
         sent.start(along(by, True))
     sent.start(across(0, x_hi))
+    for by in (1, 7, 2, 6, 3, 5, 4):
+        along(by, None).wait_recv()
+        sent.start(across(-by, x_hi))
     for by, peer in enumerate(t_peers):
         sent.start(
             remote(
@@ -737,9 +781,6 @@
             )
         )
     r.columns[row] = r.teacher[:, pl.ds(pl.multiple_of(tensor * HD, HD), HD)]
-    for by in (1, 7, 2, 6, 3, 5, 4):
-        along(by, None).wait_recv()
-        sent.start(across(-by, x_hi))
     for by in (0, 1, 7, 2, 6, 3, 5, 4):
         across(-by, 1 - x_hi).wait_recv()
 
@@ -862,16 +903,14 @@
     narrow = student_in.shape[1]
     units = s_gate.shape[1]
     ff = w_gate.shape[1]
-    angles = offsets.astype(F32)[:, None] * frequencies(HD)[None, :]
-    cosine, sine = jnp.cos(angles), jnp.sin(angles)
-    cosine = jnp.concatenate([cosine, cosine], axis=1)
-    sine = jnp.concatenate([-sine, sine], axis=1)
+    frequency = frequencies(HD)
+    frequency = jnp.concatenate([frequency, frequency])[None]
     inputs = {
         "tokens": tokens,
         "series": series_ids.reshape(-1, HD),
         "norm_gain": norm_gain[None],
-        "cosine": cosine,
-        "sine": sine,
+        "offsets": offsets.reshape(-1, HD),
+        "frequency": frequency,
         "w_query": w_query,
         "w_key": w_key,
         "w_value": w_value,
@@ -895,6 +934,8 @@
     half = own // 2
     scratch = {
         "tok": pltpu.VMEM((size, rows, HD), BF16),
+        "cosine": pltpu.VMEM((rows, HD), F32),
+        "sine": pltpu.VMEM((rows, HD), F32),
         "normed": pltpu.VMEM((rows, width), BF16),
         "weights": pltpu.VMEM((width, 3 * HD), BF16),
         "query": pltpu.VMEM((rows, HD), BF16),
@@ -938,16 +979,15 @@
         "heads": pltpu.VMEM((NZ, 2 * own, HD), BF16),
         "a_send": dma(7),
         "a_recv": dma(7),
-        "out_send": pltpu.VMEM((own, width), BF16),
-        "out_recv": pltpu.VMEM((own, width), BF16),
-        "o_send": one,
-        "o_recv": one,
-        "partial": pltpu.VMEM((2 * own, width), F32),
+        "out_send": pltpu.VMEM((4, own, width // 4), BF16),
+        "out_recv": pltpu.VMEM((4, own, width // 4), BF16),
+        "o_send": dma(4),
+        "o_recv": dma(4),
+        "partial": pltpu.VMEM((4, 2 * own, width // 4), F32),
         "mixed": pltpu.VMEM((own, width), BF16),
         "blocks": pltpu.VMEM((size, own, width), BF16),
         "hidden": pltpu.VMEM((NZ, 2 * own, ff), BF16),
         "parts": pltpu.VMEM((size, own, width), BF16),
-        "predicted": pltpu.VMEM((own, narrow), F32),
         "g_send": dma(2, 4, 3),
         "g_recv": dma(2, 4, 3),
         "gx_send": dma(9),

time: 164 us -> 157 us (0.957)
  Pallas kernels: 160 us -> 156 us
  other arithmetic: 2.68 us -> 0.59 us
    pallas_call x1, Pallas kernels: 158 us -> 154 us  [call(): pl.pallas_call(body, out_shape=tuple((jax.ShapeDtypeStruct(shape, kind) f...]
where the time goes in v5:
time: 157 us
  Pallas kernels  156 us (99%)
    pallas_call x1, Pallas kernels, call(): pl.pallas_call(body, out_shape=tuple((jax.ShapeDtypeStruct(shape, kind) f...  154 us

profile of v5, /device:TPU:1, one launch (start us, length us, event | category | flops | bytes accessed | tf_op | source)
XLA Modules:
  0.0 157.4 jit_solution(1774443949517564871)
XLA Ops:
  0.6 0.6 maximum_bitcast_fusion.refs_4_
  1.2 154.1 %layer.1 = (bf16[16,32,128]{2,1,0:T(8,128)(2,1)}, bf16[16,96,128]{2,1,0:T(8,128)(2,1)}, f32[8,128]{1,0:T(8,128)}) custom-call(bf16[512,128]{1,0:T(8,128)(2,1)} %refs_0_.1, s32[64,128]{1,0:T(8,128)} %bitcast.7, f32[1,2048]{1,0:T(1,128)} %bitcast.8, s32[4,128]{1,0:T(4,128)} %bitcast.10, f32[1,128]{1,0:T(1,128)} %maximum_bitcast_fusion.refs_4_, ...), custom_call_target="tpu_custom_call" | custom-call | tf_op jit(solution)/shard_map/layer/pallas_call | solution.py:61
  155.4 2.0 %finish.1 = (bf16[512,128]{1,0:T(8,128)(2,1)}, f32[512,128]{1,0:T(8,128)}, f32[512,128]{1,0:T(8,128)}, f32[128,512]{1,0:T(8,128)}, f32[1,1]{1,0:T(1,128)}) custom-call(bf16[16,32,128]{2,1,0:T(8,128)(2,1)} %get-tuple-element.13.columns_ref, bf16[16,96,128]{2,1,0:T(8,128)(2,1)} %get-tuple-element.14.sums_ref, f32[8,128]{1,0:T(8,128)} %get-tuple-element.15.squares_ref), custom_call_target="tpu_custom_call" | custom-call | tf_op jit(solution)/shard_map/finish/pallas_call | solution.py:865
  (1 shorter events, 0.0 us)

commit v6 on v5

--- a/solution.py
+++ b/solution.py
@@ -2,6 +2,7 @@
 
 import jax
 import jax.numpy as jnp
+import numpy as np
 from jax import lax
 from jax.experimental import pallas as pl
 from jax.experimental.pallas import tpu as pltpu
@@ -260,9 +261,12 @@
         sent.start(last)
         second = total(1) + crossed(0)
         first = total(0)
-        last.wait_recv()
-        first = first + xgot[...].astype(F32)
-        return first, second, sent
+
+        def other():
+            last.wait_recv()
+            return first + xgot[...].astype(F32)
+
+        return other, second, sent
 
     return begin, rest
 
@@ -272,7 +276,7 @@
 
 
 def student(r, step):
-    own = r.tokens.shape[0] // (2 * NZ)
+    own = r.student.shape[0] // (2 * NZ)
     at = pl.ds(step * 128, 128)
     values = rms(r.student[at, :].astype(F32))
     r.normed_t[:, at] = values.T.astype(BF16)
@@ -290,50 +294,72 @@
         r.part[index % 2, step * (64 // own) + index // 2] = block
 
 
-def project(r, after):
+def project(r, after, weights_there):
     dp, tensor, x_hi, z = places()
-    rows = r.tokens.shape[0]
+    rows = r.tok.shape[1]
     own = rows // (2 * NZ)
 
     def hook(step):
+        if step == 0:
+            weights_there()
         if step == 3:
             student(r, 3)
 
-    mix_gather(r.tok, lambda zz, plane: plane * NZ + zz, rows // 2, (r.q_send, r.q_recv, r.qx_send, r.qx_recv), hook)
+    tile = 256
+    started = []
+
+    def add(distances):
+        places_now = []
+        for by in distances:
+            for zz in [z] if by == 0 else [turn(z, 4, NZ)] if by == 4 else [turn(z, by, NZ), turn(z, -by, NZ)]:
+                places_now += [zz, NZ + zz]
+        weights = jnp.concatenate(
+            [r.weights[pl.ds(pl.multiple_of(at * HD, HD), HD), :] for at in places_now], axis=0
+        )
+        for step in range(rows // tile):
+            at = pl.ds(step * tile, tile)
+            square = None if not started else r.square[at, :]
+            values = []
+            for index in places_now:
+                value = r.tok[index, at, :].astype(F32)
+                square = value * value if square is None else square + value * value
+                values.append((value * r.norm_gain[pl.ds(index, 1), :]).astype(BF16))
+            r.square[at, :] = square
+            out = jnp.dot(jnp.concatenate(values, axis=1), weights, preferred_element_type=F32)
+            r.product[at, :] = out if not started else r.product[at, :] + out
+        started.append(True)
+
+    mix_gather(
+        r.tok,
+        lambda zz, plane: plane * NZ + zz,
+        rows // 2,
+        (r.q_send, r.q_recv, r.qx_send, r.qx_recv),
+        hook,
+        ready=add,
+        tail=lambda: add((3,)),
+    )
     after()
+    add((4,))
+    for step in range(rows // tile):
+        at = pl.ds(step * tile, tile)
+        mean = jnp.sum(r.square[at, :], axis=1, keepdims=True) / (2 * NZ * HD)
+        out = r.product[at, :] * lax.rsqrt(mean + 1e-05)
+        cosine, sine = r.cosine[at, :], r.sine[at, :]
+
+        def rotary(values):
+            return (values * cosine + pltpu.roll(values, HD // 2, 1) * sine).astype(BF16)
+
+        r.pairs[dp, 0, at, :] = rotary(out[:, HD : 2 * HD])
+        r.pairs[dp, 1, at, :] = out[:, 2 * HD :].astype(BF16)
+        r.query[at, :] = rotary(out[:, :HD])
+
+
+def keep_tokens(r):
+    _, _, x_hi, z = places()
+    own = r.my_tokens.shape[0]
     my_rows = pl.multiple_of((z * 2 + x_hi) * own, own)
     for index in range(2 * NZ):
         r.my_tokens[:, index * HD : (index + 1) * HD] = r.tok[index, pl.ds(my_rows, own)]
-    tile = 128
-
-    @pl.loop(0, rows // tile)
-    def _(step):
-        at = pl.ds(pl.multiple_of(step * tile, tile), tile)
-        square = jnp.zeros((tile, HD), F32)
-        for index in range(2 * NZ):
-            value = r.tok[index, at].astype(F32)
-            square = square + value * value
-        mean = jnp.sum(square, axis=1, keepdims=True) / (2 * NZ * HD)
-        scale = lax.rsqrt(mean + 1e-05)
-        for index in range(2 * NZ):
-            lanes = slice(index * HD, (index + 1) * HD)
-            value = r.tok[index, at].astype(F32) * scale * r.norm_gain[:, lanes]
-            r.normed[at, lanes] = value.astype(BF16)
-
-    tile = 256
-
-    @pl.loop(0, rows // tile)
-    def _(step):
-        at = pl.ds(pl.multiple_of(step * tile, tile), tile)
-        out = jnp.dot(r.normed[at, :], r.weights[...], preferred_element_type=F32)
-        cosine, sine = r.cosine[at, :], r.sine[at, :]
-
-        def rotary(values):
-            return (values * cosine + pltpu.roll(values, HD // 2, 1) * sine).astype(BF16)
-
-        r.query[at, :] = rotary(out[:, :HD])
-        r.pairs[dp, 0, at, :] = rotary(out[:, HD : 2 * HD])
-        r.pairs[dp, 1, at, :] = out[:, 2 * HD :].astype(BF16)
 
 
 def find_starts(r):
@@ -348,11 +374,10 @@
     r.start[...] = found.astype(jnp.int32)
 
 
-def prepare(r):
+def prepare(r, loaded):
+    loaded("series")
     find_starts(r)
-    r.weights[:, :HD] = r.w_query[...]
-    r.weights[:, HD : 2 * HD] = r.w_key[...]
-    r.weights[:, 2 * HD :] = r.w_value[...]
+    loaded("offsets", "frequency")
     for step in range(r.offsets.shape[0]):
         at = pl.ds(step * HD, HD)
         offset = jnp.broadcast_to(r.offsets[step : step + 1, :].astype(F32), (HD, HD)).T
@@ -361,6 +386,7 @@
         r.cosine[at, :] = jnp.cos(angle)
         sine = jnp.sin(angle)
         r.sine[at, :] = jnp.where(lane < HD // 2, -sine, sine)
+    loaded("student", "s_gate", "s_up", "s_down")
     for step in range(3):
         student(r, step)
 
@@ -418,7 +444,7 @@
     z_peers = [(dp, x_hi * NZ + turn(z, by, NZ)) for by in range(1, NZ)]
     z_nexts = (z_peers[0], z_peers[-1])
     s_partner = (dp, (1 - x_hi) * NZ + z)
-    deep = r.w_out.shape[0] // 4
+    deep = r.wide.shape[1] // 4
     first, second = x_lo == 0, x_lo == 1
 
     def chip(by):
@@ -600,11 +626,33 @@
     return begin_wide, arrive, wide_whole, finish
 
 
+ORDER = (
+    "tokens",
+    "series",
+    "offsets",
+    "frequency",
+    "student",
+    "s_gate",
+    "s_up",
+    "s_down",
+    "w_query",
+    "w_key",
+    "w_value",
+    "norm_gain",
+    "w_out",
+    "mlp_gain",
+    "w_gate",
+    "w_up",
+    "w_down",
+    "projector",
+)
+
+
 def layer_body(names, total_rows, *refs):
     r = Refs(names, refs)
     dp, tensor, x_hi, z = places()
     size = 2 * NZ
-    rows, width = r.tokens.shape[0], r.w_query.shape[0]
+    rows, width = r.tok.shape[1], r.w_gate.shape[0]
     own = rows // size
     pair = 2 * own
     row = z * 2 + x_hi
@@ -613,20 +661,38 @@
     z_peers = [(dp, x_hi * NZ + turn(z, by, NZ)) for by in range(1, NZ)]
     t_peers = [turn(tensor, by, size) for by in range(1, size)]
     d_peers = [turn(dp, by, size) for by in range(1, size)]
-    loads = []
-    for index, name in enumerate(("w_gate", "w_up", "w_down", "projector")):
-        far, near = getattr(r, name + "_hbm"), getattr(r, name)
-        loads.append(pltpu.make_async_copy(far, near, r.load_sem.at[index]))
-        loads[-1].start()
-    r.wide[z] = r.w_out[...]
-    r.tok[tensor] = r.tokens[...]
+    loads = {}
+    near = {
+        "tokens": r.tok.at[tensor],
+        "w_query": r.weights.at[:, pl.ds(0, HD)],
+        "w_key": r.weights.at[:, pl.ds(HD, HD)],
+        "w_value": r.weights.at[:, pl.ds(2 * HD, HD)],
+        "w_out": r.wide.at[z],
+    }
+    for index, name in enumerate(ORDER):
+        target = near[name] if name in near else getattr(r, name)
+        loads[name] = pltpu.make_async_copy(
+            getattr(r, name + "_hbm"), target, r.load_sem.at[index]
+        )
+        loads[name].start()
+
+    def loaded(*names):
+        for name in names:
+            loads.pop(name).wait()
+
     greet(
         [(dp, peer) for peer in t_peers] + [(peer, tensor) for peer in d_peers],
-        lambda: prepare(r),
+        lambda: prepare(r, loaded),
     )
     sent = Sent()
     begin_wide, arrive, wide_whole, finish_exchange = exchange(r, sent)
-    project(r, begin_wide)
+    loaded("tokens")
+
+    def after():
+        loaded("w_out")
+        begin_wide()
+
+    project(r, after, lambda: loaded("w_query", "w_key", "w_value", "norm_gain"))
     arrive()
 
     def rows_of(zz):
@@ -678,20 +744,21 @@
         r.out_send[step] = r.partial[step, half_rows(1 - x_hi), :].astype(BF16)
         sent.start(swap(step))
     send_student()
+    keep_tokens(r)
     for step in range(width // chunk):
         at = slice(step * chunk, (step + 1) * chunk)
         mine = r.partial[step, half_rows(x_hi), :] + r.my_tokens[:, at].astype(F32)
         swap(step).wait_recv()
         r.mixed[:, at] = (mine + r.out_recv[step].astype(F32)).astype(BF16)
     mixed = r.mixed[...]
+    loaded("mlp_gain")
     r.blocks[row] = (rms(mixed.astype(F32)) * r.mlp_gain[...]).astype(BF16)
 
     waited = []
 
     def units(zs):
         if not waited:
-            loads[0].wait()
-            loads[1].wait()
+            loaded("w_gate", "w_up")
             waited.append(True)
         value = jnp.concatenate(
             [r.blocks[pl.ds(zz * 2, 2)].reshape(pair, width) for zz in zs], axis=0
@@ -702,11 +769,22 @@
         for at, zz in enumerate(zs):
             r.hidden[zz] = found[at * pair : (at + 1) * pair]
 
+    def predict():
+        student_sum = r.s_out[z].astype(F32)
+        for by in range(1, NZ):
+            got = r.s_in.at[by - 1]
+            sems = r.sz_send.at[by - 1], r.sz_recv.at[by - 1]
+            remote(got, got, *sems, z_peers[by - 1]).wait_recv()
+            student_sum = student_sum + r.s_in[by - 1].astype(F32)
+        r.predicted[...] = r.student[my_rows, :].astype(F32) + student_sum
+
     def ready(distances):
         zs = []
         for by in distances:
             zs += [z] if by == 0 else [turn(z, by, NZ), turn(z, -by, NZ)]
         units(zs)
+        if 2 in distances:
+            predict()
 
     fresh = [3, 4]
 
@@ -727,7 +805,7 @@
 
     scratch = (r.sbuf, r.rbuf, r.xbuf, r.xlast, r.xgot, r.r_send, r.r_recv, r.rx_send, r.rx_recv)
     begin_sum, rest_of_sum = mix_scatter(r.parts, make, scratch)
-    loads[2].wait()
+    loaded("w_down")
     mix_gather(
         r.blocks,
         lambda zz, plane: zz * 2 + plane,
@@ -737,18 +815,18 @@
         tail=begin_sum,
     )
     top, bottom, more = rest_of_sum()
-    student_sum = r.s_out[z].astype(F32)
-    for by in range(1, NZ):
-        got = r.s_in.at[by - 1]
-        remote(got, got, r.sz_send.at[by - 1], r.sz_recv.at[by - 1], z_peers[by - 1]).wait_recv()
-        student_sum = student_sum + r.s_in[by - 1].astype(F32)
-    predicted = r.student[my_rows, :].astype(F32) + student_sum
-    teacher = r.mixed[...].astype(F32) + jnp.concatenate([top, bottom], axis=0)
-    teacher = teacher.astype(BF16)
-    r.teacher[...] = teacher
-    loads[3].wait()
-    target = jnp.dot(teacher, r.projector[...], preferred_element_type=F32)
-    scaled = ((predicted - target) * total_rows ** (-0.5)).astype(BF16)
+    loaded("projector")
+
+    def last_rows(first, summed):
+        at = slice(first, first + own // 2)
+        teacher = (r.mixed[at, :].astype(F32) + summed).astype(BF16)
+        r.teacher[at, :] = teacher
+        target = jnp.dot(teacher, r.projector[...], preferred_element_type=F32)
+        scaled = (r.predicted[at, :] - target) * total_rows ** (-0.5)
+        r.gathered[row, at, :] = scaled.astype(BF16)
+
+    last_rows(own // 2, bottom)
+    last_rows(0, top())
 
     def place(by, plane):
         return r.gathered.at[turn(z, by, NZ) * 2 + plane]
@@ -763,7 +841,6 @@
         sems = r.p_send.at[by - 1], r.p_recv.at[by - 1]
         return remote(block, block, *sems, z_peers[by - 1])
 
-    r.gathered[row] = scaled
     for by in (4, 3, 5, 2, 6, 1, 7):
         sent.start(along(by, True))
     sent.start(across(0, x_hi))
@@ -873,8 +950,9 @@
 
 
 def frequencies(head_dim):
-    indices = jnp.arange(head_dim // 2).astype(F32)
-    return jnp.exp(-jnp.log(500000.0) * 2.0 * indices / head_dim)
+    indices = np.arange(head_dim // 2)
+    found = np.exp(-np.log(500000.0) * 2.0 * indices / head_dim).astype(np.float32)
+    return np.concatenate([found, found])[None]
 
 
 def local(
@@ -903,12 +981,11 @@
     narrow = student_in.shape[1]
     units = s_gate.shape[1]
     ff = w_gate.shape[1]
-    frequency = frequencies(HD)
-    frequency = jnp.concatenate([frequency, frequency])[None]
+    frequency = jnp.asarray(frequencies(HD))
     inputs = {
         "tokens": tokens,
         "series": series_ids.reshape(-1, HD),
-        "norm_gain": norm_gain[None],
+        "norm_gain": norm_gain.reshape(-1, HD),
         "offsets": offsets.reshape(-1, HD),
         "frequency": frequency,
         "w_query": w_query,
@@ -916,10 +993,10 @@
         "w_value": w_value,
         "w_out": w_out,
         "mlp_gain": mlp_gain[None],
-        "w_gate_hbm": w_gate,
-        "w_up_hbm": w_up,
-        "w_down_hbm": w_down,
-        "projector_hbm": projector,
+        "w_gate": w_gate,
+        "w_up": w_up,
+        "w_down": w_down,
+        "projector": projector,
         "student": student_in,
         "s_gate": s_gate,
         "s_up": s_up,
@@ -936,7 +1013,9 @@
         "tok": pltpu.VMEM((size, rows, HD), BF16),
         "cosine": pltpu.VMEM((rows, HD), F32),
         "sine": pltpu.VMEM((rows, HD), F32),
-        "normed": pltpu.VMEM((rows, width), BF16),
+        "square": pltpu.VMEM((rows, HD), F32),
+        "product": pltpu.VMEM((rows, 3 * HD), F32),
+        "predicted": pltpu.VMEM((own, narrow), F32),
         "weights": pltpu.VMEM((width, 3 * HD), BF16),
         "query": pltpu.VMEM((rows, HD), BF16),
         "my_tokens": pltpu.VMEM((own, width), BF16),
@@ -971,11 +1050,7 @@
         "sx_recv": one,
         "sz_send": dma(7),
         "sz_recv": dma(7),
-        "w_gate": pltpu.VMEM(w_gate.shape, BF16),
-        "w_up": pltpu.VMEM(w_up.shape, BF16),
-        "w_down": pltpu.VMEM(w_down.shape, BF16),
-        "projector": pltpu.VMEM(projector.shape, BF16),
-        "load_sem": dma(4),
+        "load_sem": dma(len(ORDER)),
         "heads": pltpu.VMEM((NZ, 2 * own, HD), BF16),
         "a_send": dma(7),
         "a_recv": dma(7),
@@ -1013,17 +1088,21 @@
             "recv2": dma(size - 1),
         }
     )
-    far = pl.BlockSpec(memory_space=pl.ANY)
+    elsewhere = ("tokens", "w_query", "w_key", "w_value", "w_out")
+    for name in ORDER:
+        if name not in elsewhere:
+            scratch[name] = pltpu.VMEM(inputs[name].shape, inputs[name].dtype)
+    names = [name + "_hbm" for name in inputs]
     columns, sums, squares = call(
         functools.partial(
-            layer_body, (*inputs, *outputs, *scratch), rows * lax.axis_size("dp")
+            layer_body, (*names, *outputs, *scratch), rows * lax.axis_size("dp")
         ),
         "layer",
         1,
         tuple(inputs.values()),
         tuple(outputs.values()),
         list(scratch.values()),
-        [far if name.endswith("_hbm") else VM for name in inputs],
+        [pl.BlockSpec(memory_space=pl.ANY)] * len(inputs),
     )
     teacher_out, grad_gate, grad_up, grad_down, error = finish(columns, sums, squares)
     return (teacher_out, grad_gate, grad_up, grad_down, error.reshape(()))

time: 157 us -> 156 us (level)
  no operation moved by 1% of the time
where the time goes in v6:
time: 156 us
  Pallas kernels  155 us (99%)
    pallas_call x1, Pallas kernels, call(): pl.pallas_call(body, out_shape=tuple((jax.ShapeDtypeStruct(shape, kind) f...  153 us

profile of v6, /device:TPU:1, one launch (start us, length us, event | category | flops | bytes accessed | tf_op | source)
XLA Modules:
  0.0 155.7 jit_solution(9858315202987667916)
XLA Ops:
  0.6 153.1 %layer.1 = (bf16[16,32,128]{2,1,0:T(8,128)(2,1)}, bf16[16,96,128]{2,1,0:T(8,128)(2,1)}, f32[8,128]{1,0:T(8,128)}) custom-call(bf16[512,128]{1,0:T(8,128)(2,1)} %refs_0_.1, s32[64,128]{1,0:T(8,128)} %bitcast.5, f32[16,128]{1,0:T(8,128)} %bitcast.6, s32[4,128]{1,0:T(4,128)} %bitcast.8, f32[1,128]{1,0:T(1,128)} %constant.2.clone.refs_4_, ...), custom_call_target="tpu_custom_call" | custom-call | tf_op jit(solution)/shard_map/layer/pallas_call | solution.py:62
  153.7 2.0 %finish.1 = (bf16[512,128]{1,0:T(8,128)(2,1)}, f32[512,128]{1,0:T(8,128)}, f32[512,128]{1,0:T(8,128)}, f32[128,512]{1,0:T(8,128)}, f32[1,1]{1,0:T(1,128)}) custom-call(bf16[16,32,128]{2,1,0:T(8,128)(2,1)} %get-tuple-element.13.columns_ref, bf16[16,96,128]{2,1,0:T(8,128)(2,1)} %get-tuple-element.14.sums_ref, f32[8,128]{1,0:T(8,128)} %get-tuple-element.15.squares_ref), custom_call_target="tpu_custom_call" | custom-call | tf_op jit(solution)/shard_map/finish/pallas_call | solution.py:942

commit v7 on v6

--- a/solution.py
+++ b/solution.py
@@ -294,7 +294,7 @@
         r.part[index % 2, step * (64 // own) + index // 2] = block
 
 
-def project(r, after, weights_there):
+def project(r, before, after, weights_there):
     dp, tensor, x_hi, z = places()
     rows = r.tok.shape[1]
     own = rows // (2 * NZ)
@@ -302,7 +302,6 @@
     def hook(step):
         if step == 0:
             weights_there()
-        if step == 3:
             student(r, 3)
 
     tile = 256
@@ -329,6 +328,10 @@
             r.product[at, :] = out if not started else r.product[at, :] + out
         started.append(True)
 
+    def tail():
+        before()
+        add((3,))
+
     mix_gather(
         r.tok,
         lambda zz, plane: plane * NZ + zz,
@@ -336,7 +339,7 @@
         (r.q_send, r.q_recv, r.qx_send, r.qx_recv),
         hook,
         ready=add,
-        tail=lambda: add((3,)),
+        tail=tail,
     )
     after()
     add((4,))
@@ -550,6 +553,11 @@
         for way in range(2):
             sent.start(w_share(towards(way, -far), 2 * (far - 1) + way, core))
 
+    s_cross = remote(r.part.at[1 - x_hi], r.s_got, r.sx_send, r.sx_recv, s_partner)
+
+    def begin_student():
+        sent.start(s_cross)
+
     def begin_wide():
         for sub in range(2):
             for way in range(2):
@@ -561,8 +569,6 @@
             when(y == 0, k_copy(R3, part, x_lo, y, down))
             when(first, k_copy(X0, part, 0, y, k_partner))
         share(OWN)
-        s_cross = remote(r.part.at[1 - x_hi], r.s_got, r.sx_send, r.sx_recv, s_partner)
-        sent.start(s_cross)
         w_forward(1, 0)
         w_forward(1, 1)
         w_spread(1)
@@ -623,7 +629,7 @@
         for slot, by in enumerate([-1, 1, -2, 2, -3, 3, 4]):
             w_share(by, slot, 1 - core).wait_recv()
 
-    return begin_wide, arrive, wide_whole, finish
+    return begin_student, begin_wide, arrive, wide_whole, finish
 
 
 ORDER = (
@@ -685,14 +691,14 @@
         lambda: prepare(r, loaded),
     )
     sent = Sent()
-    begin_wide, arrive, wide_whole, finish_exchange = exchange(r, sent)
+    begin_student, begin_wide, arrive, wide_whole, finish_exchange = exchange(r, sent)
     loaded("tokens")
 
     def after():
         loaded("w_out")
         begin_wide()
 
-    project(r, after, lambda: loaded("w_query", "w_key", "w_value", "norm_gain"))
+    project(r, begin_student, after, lambda: loaded("w_query", "w_key", "w_value", "norm_gain"))
     arrive()
 
     def rows_of(zz):
@@ -743,7 +749,8 @@
         )
         r.out_send[step] = r.partial[step, half_rows(1 - x_hi), :].astype(BF16)
         sent.start(swap(step))
-    send_student()
+        if step == 0:
+            send_student()
     keep_tokens(r)
     for step in range(width // chunk):
         at = slice(step * chunk, (step + 1) * chunk)

time: 156 us -> 155 us (level)
  no operation moved by 1% of the time
where the time goes in v7:
time: 155 us
  Pallas kernels  154 us (99%)
    pallas_call x1, Pallas kernels, call(): pl.pallas_call(body, out_shape=tuple((jax.ShapeDtypeStruct(shape, kind) f...  152 us

profile of v7, /device:TPU:1, one launch (start us, length us, event | category | flops | bytes accessed | tf_op | source)
XLA Modules:
  0.0 155.0 jit_solution(3713965075441430374)
XLA Ops:
  0.6 152.4 %layer.1 = (bf16[16,32,128]{2,1,0:T(8,128)(2,1)}, bf16[16,96,128]{2,1,0:T(8,128)(2,1)}, f32[8,128]{1,0:T(8,128)}) custom-call(bf16[512,128]{1,0:T(8,128)(2,1)} %refs_0_.1, s32[64,128]{1,0:T(8,128)} %bitcast.5, f32[16,128]{1,0:T(8,128)} %bitcast.6, s32[4,128]{1,0:T(4,128)} %bitcast.8, f32[1,128]{1,0:T(1,128)} %constant.2.clone.refs_4_, ...), custom_call_target="tpu_custom_call" | custom-call | tf_op jit(solution)/shard_map/layer/pallas_call | solution.py:62
  153.0 2.0 %finish.1 = (bf16[512,128]{1,0:T(8,128)(2,1)}, f32[512,128]{1,0:T(8,128)}, f32[512,128]{1,0:T(8,128)}, f32[128,512]{1,0:T(8,128)}, f32[1,1]{1,0:T(1,128)}) custom-call(bf16[16,32,128]{2,1,0:T(8,128)(2,1)} %get-tuple-element.13.columns_ref, bf16[16,96,128]{2,1,0:T(8,128)(2,1)} %get-tuple-element.14.sums_ref, f32[8,128]{1,0:T(8,128)} %get-tuple-element.15.squares_ref), custom_call_target="tpu_custom_call" | custom-call | tf_op jit(solution)/shard_map/finish/pallas_call | solution.py:949

commit v8 on v7

--- a/solution.py
+++ b/solution.py
@@ -449,6 +449,7 @@
     s_partner = (dp, (1 - x_hi) * NZ + z)
     deep = r.wide.shape[1] // 4
     first, second = x_lo == 0, x_lo == 1
+    half = r.pairs.shape[2] // 2
 
     def chip(by):
         return turn(y, by, NY)
@@ -466,7 +467,8 @@
     }
 
     def k_copy(event, part, xx, yy, device):
-        block = r.pairs.at[index(xx, yy, core), part]
+        top = (part % 2) * half
+        block = r.pairs.at[index(xx, yy, core), part // 2, pl.ds(top, half)]
         return remote(block, block, r.k_send.at[event, part], r.k_recv.at[event, part], device)
 
     later = []
@@ -564,7 +566,7 @@
                 sent.start(w_copy(way, 1, sub, 0))
 
     def arrive():
-        for part in range(2):
+        for part in range(4):
             when(y <= 2, k_copy(R1, part, x_lo, y, up))
             when(y == 0, k_copy(R3, part, x_lo, y, down))
             when(first, k_copy(X0, part, 0, y, k_partner))
@@ -573,25 +575,26 @@
         w_forward(1, 1)
         w_spread(1)
         attend(r, dp, dp, True)
-        for part in range(2):
+        for part in range(4):
             k_wait(R1, part)
             when((y >= 1) & (y <= 2), k_copy(R2, part, x_lo, chip(-1), up))
             when(first & (y >= 1), k_copy(X1, part, 0, chip(-1), k_partner))
             k_wait(X0, part)
             when(second & (y >= 1), k_copy(H1, part, 0, y, down))
             when(second & (y == 3), k_copy(H3, part, 0, y, up))
-            w_forward(2, part)
+            if part % 2:
+                w_forward(2, part // 2)
         share(R1)
         share(X0)
         w_spread(2)
-        k_wait(R3, 0)
-        k_wait(R3, 1)
+        for part in range(4):
+            k_wait(R3, part)
         share(R3)
         s_cross.wait_recv()
         r.s_out[...] = (r.part[x_hi].astype(F32) + r.s_got[...].astype(F32)).astype(BF16)
         shared(OWN, R1)
         work(OWN, R1)
-        for part in range(2):
+        for part in range(4):
             k_wait(H1, part)
             when(second & (y >= 1) & (y <= 2), k_copy(H2, part, 0, chip(1), down))
         share(H1)
@@ -601,16 +604,16 @@
         w_forward(3, 1)
         w_spread(3)
         for event in (X1, R2, H3):
-            k_wait(event, 0)
-            k_wait(event, 1)
+            for part in range(4):
+                k_wait(event, part)
             share(event)
         shared(R3, H1)
         work(R3, H1)
         w_forward(4, 0)
         w_forward(4, 1)
         sent.start(w_share(4, 6, core))
-        k_wait(H2, 0)
-        k_wait(H2, 1)
+        for part in range(4):
+            k_wait(H2, part)
         share(H2)
         shared(X1, R2, H3)
         work(X1, R2, H3)
@@ -1042,8 +1045,8 @@
         "denom": pltpu.VMEM((rows, HD), F32),
         "accum": pltpu.VMEM((rows, HD), F32),
         "attended": pltpu.VMEM((rows, HD), BF16),
-        "k_send": dma(9, 2),
-        "k_recv": dma(9, 2),
+        "k_send": dma(9, 4),
+        "k_recv": dma(9, 4),
         "c_send": dma(9),
         "c_recv": dma(9),
         "w_send": dma(2, 4, 2),

time: 155 us -> 155 us (level)
  no operation moved by 1% of the time
where the time goes in v8:
time: 155 us
  Pallas kernels  154 us (99%)
    pallas_call x1, Pallas kernels, call(): pl.pallas_call(body, out_shape=tuple((jax.ShapeDtypeStruct(shape, kind) f...  152 us

profile of v8, /device:TPU:1, one launch (start us, length us, event | category | flops | bytes accessed | tf_op | source)
XLA Modules:
  0.0 155.0 jit_solution(17083988247531315927)
XLA Ops:
  0.6 152.4 %layer.1 = (bf16[16,32,128]{2,1,0:T(8,128)(2,1)}, bf16[16,96,128]{2,1,0:T(8,128)(2,1)}, f32[8,128]{1,0:T(8,128)}) custom-call(bf16[512,128]{1,0:T(8,128)(2,1)} %refs_0_.1, s32[64,128]{1,0:T(8,128)} %bitcast.5, f32[16,128]{1,0:T(8,128)} %bitcast.6, s32[4,128]{1,0:T(4,128)} %bitcast.8, f32[1,128]{1,0:T(1,128)} %constant.2.clone.refs_4_, ...), custom_call_target="tpu_custom_call" | custom-call | tf_op jit(solution)/shard_map/layer/pallas_call | solution.py:62
  153.0 2.0 %finish.1 = (bf16[512,128]{1,0:T(8,128)(2,1)}, f32[512,128]{1,0:T(8,128)}, f32[512,128]{1,0:T(8,128)}, f32[128,512]{1,0:T(8,128)}, f32[1,1]{1,0:T(1,128)}) custom-call(bf16[16,32,128]{2,1,0:T(8,128)(2,1)} %get-tuple-element.13.columns_ref, bf16[16,96,128]{2,1,0:T(8,128)(2,1)} %get-tuple-element.14.sums_ref, f32[8,128]{1,0:T(8,128)} %get-tuple-element.15.squares_ref), custom_call_target="tpu_custom_call" | custom-call | tf_op jit(solution)/shard_map/finish/pallas_call | solution.py:952
